TPU v7x, 256 devices: a whole 4x4x8 slice. The times are simulated.
256 devices in a mesh: ccd: 64 (over z, x, core), tile: 4 (over y).
Axes of the slice: x: 4, y: 4, z: 8, core: 2. Of those that a mesh axis runs over, the one named last changes fastest.
Arguments:
- visit_image: bfloat16 [32768, 1024], P(('ccd', 'tile')), may hold values from -6 to 6
- mask_bits: int32 [32768, 1024], P(('ccd', 'tile')), may hold values from 0 to 15
- visit_weight: float32 [64], P('ccd'), may hold values from 1 to 4
- basis_cols: bfloat16 [31, 21], replicated, may hold values from -1.25 to 1.25
- basis_rows: bfloat16 [31, 21], replicated, may hold values from -1.25 to 1.25
- kernel_coef: float32 [64, 31, 6], P('ccd'), may hold values from -1 to 1
- row_warp: bfloat16 [32768, 512], P(('ccd', 'tile')), may hold values from -1 to 1, as said below
- col_warp: bfloat16 [64, 1024, 1024], P('ccd'), may hold values from -1 to 1, as said below
- dest_owner: int32 [16384, 1], P(('ccd', 'tile')), may hold values from 0 to 63; in each aligned block of 64 rows (0 to 63, 64 to 127, ...) at most 2 rows name the same one
- dest_block: int32 [16384], P(('ccd', 'tile')), may hold values from 0 to 63
- new_science: float32 [32768, 1024], P(('ccd', 'tile')), may hold values from -6 to 6
- tmpl_owner: int32 [16384, 1], P(('ccd', 'tile')), may hold values from 0 to 63; in each aligned block of 64 rows (0 to 63, 64 to 127, ...) at most 2 rows name the same one
- tmpl_block: int32 [16384], P(('ccd', 'tile')), may hold values from 0 to 63
Outputs:
- coadd: float32 [32768, 1024], P(('ccd', 'tile'))
- difference: float32 [32768, 1024], P(('ccd', 'tile'))
Inputs may be any that keep to these rules, and one draw needn't show every extreme that they name: `dest_owner`: within the 64 rows of one device no patch is named more than 2 times, a bound that some block reaches. `tmpl_owner`: within the 64 rows of one device no patch is named more than 2 times, a bound that some block reaches. `row_warp`: Lanczos-3 interpolation weights for a dither of 0 or plus or minus 512 / 2 rows plus a shift within 8 pixels, and a scale change within 3 / 512; rows that fall off the cutout are zero. `col_warp`: Lanczos-3 interpolation weights for a shift within 8 pixels and a scale change within 3 / 1024; every nonzero lies within 14 of the diagonal.
All inputs are finite; a program needn't handle non-finite values.
Results may differ from a plain program's by a relative error of at most 0.015.
Values may be sent and summed in bfloat16 or wider, within the bound.
No kernel may reach another device: no remote copies, remote signals or barrier semaphores. Data moves between devices by JAX's collectives and lax.ppermute only.
A program may use at most 192 MiB of HBM per device.

v0:
```python
import functools

import jax
import jax.numpy as jnp
from jax import lax
from jax.experimental import pallas as pl
from jax.experimental.pallas import tpu as pltpu
from jax.sharding import PartitionSpec as P

BLOCK_ROWS = 16
BLOCK_COLUMNS = 128
FLOOR = 1.0

ROWS = 128
WIDTH = 1024
CUTOUT = 512
NTILE = 4
NB = 31
TAPS = 21
HALF = 10
EDGE = 16
BAND = 64
WINDOW = 96
DEPTH = 2048
USED = TAPS * WINDOW
NBLK = 64
SLOTS = 128

VMEM = pl.BlockSpec(memory_space=pltpu.VMEM)
SMEM = pl.BlockSpec(memory_space=pltpu.SMEM)


def call(body, out_shape, in_specs, out_specs, scratch, name, flops, nbytes):
    return pl.pallas_call(
        body,
        out_shape=out_shape,
        in_specs=in_specs,
        out_specs=out_specs,
        scratch_shapes=scratch,
        name=name,
        compiler_params=pltpu.CompilerParams(vmem_limit_bytes=40 * 1024 * 1024),
        cost_estimate=pl.CostEstimate(flops=flops, bytes_accessed=nbytes, transcendentals=0),
    )


def index_kernel(dest_owner, dest_block, tmpl_owner, tmpl_block, dest_slot, tmpl_slot, table, count):
    def clear(i, _):
        count[i] = 0
        count[64 + i] = 0
        table[4 * i] = NBLK
        table[4 * i + 1] = NBLK
        table[4 * i + 2] = 0
        table[4 * i + 3] = 0
        return 0

    lax.fori_loop(0, 64, clear, 0, unroll=8)

    def place(k, _):
        owner = dest_owner[k]
        rank = count[owner]
        count[owner] = rank + 1
        dest_slot[k] = 2 * owner + rank
        table[4 * owner + rank] = dest_block[k]
        asked = tmpl_owner[k]
        rank = count[64 + asked]
        count[64 + asked] = rank + 1
        tmpl_slot[k] = 2 * asked + rank
        table[4 * asked + 2 + rank] = tmpl_block[k]
        return 0

    lax.fori_loop(0, 64, place, 0, unroll=8)


def table_kernel(tile, coef, cols, rows_t, table):
    taps = []
    for p in range(6):
        taps.append(
            jnp.dot(
                rows_t[...],
                coef[:, p : p + 1] * cols[...],
                preferred_element_type=jnp.float32,
                precision=lax.Precision.HIGHEST,
            )
        )
    lane = lax.broadcasted_iota(jnp.int32, (BAND, 128), 1)
    row = lax.broadcasted_iota(jnp.int32, (BAND, 128), 0)
    for band in range(2):
        first = tile[0] * ROWS + band * BAND
        yn = (2.0 * (first + row).astype(jnp.float32) + 1.0) / CUTOUT - 1.0
        yy = yn * yn

        def turned(i):
            v = [jnp.broadcast_to(taps[p][i : i + 1, :], (BAND, 128)) for p in range(6)]
            mixed = (v[0] + yn * v[1] + yy * v[3], v[2] + yn * v[4], v[5])
            return [
                pltpu.roll(m, (i * WINDOW) % 128, 1, stride=1, stride_axis=0) for m in mixed
            ]

        held = {}
        for column in range(DEPTH // 128):
            left = (128 * column) // WINDOW
            bound = (left + 1) * WINDOW - 128 * column
            for i in (left, left + 1):
                if i < TAPS and i not in held:
                    held[i] = turned(i)
            for q in range(3):
                other = held[left + 1][q] if left + 1 < TAPS else jnp.zeros((BAND, 128), jnp.float32)
                table[band, q * BAND : (q + 1) * BAND, column * 128 : (column + 1) * 128] = jnp.where(
                    lane < bound, held[left][q], other
                ).astype(jnp.bfloat16)
            held = {i: held[i] for i in held if i > left}


def conv_kernel(visit_weight, top, image, bottom, table, mask, planes, edges, stack):
    for group in range(10):
        if group == 0:
            strip = top[...]
        elif group == 9:
            strip = bottom[...]
        else:
            strip = image[(group - 1) * 16 : group * 16, :]
        strip = jnp.concatenate(
            [strip.astype(jnp.float32), jnp.zeros((16, 128), jnp.float32)], axis=1
        )
        for i in range(TAPS):
            moved = strip if i == HALF else pltpu.roll(strip, (HALF - i) % (WIDTH + 128), 1)
            moved = moved[:, :WIDTH].astype(jnp.bfloat16)
            if group < 6:
                at = i * WINDOW + group * 16
                stack[0, at : at + 16, :] = moved
            if group >= 4:
                at = i * WINDOW + group * 16 - BAND
                stack[1, at : at + 16, :] = moved
    stack[:, USED:, :] = jnp.zeros((2, DEPTH - USED, WIDTH), jnp.bfloat16)
    scale = visit_weight[0].astype(jnp.bfloat16).astype(jnp.float32)
    for band in range(2):
        rows = slice(band * BAND, (band + 1) * BAND)
        for n in range(4):
            columns = slice(n * 256, (n + 1) * 256)
            parts = jnp.dot(
                table[band], stack[band, :, columns], preferred_element_type=jnp.float32
            )
            x = lax.broadcasted_iota(jnp.int32, (BAND, 256), 1) + n * 256
            xn = (2.0 * x.astype(jnp.float32) + 1.0) / WIDTH - 1.0
            conv = parts[:BAND] + xn * (parts[BAND : 2 * BAND] + xn * parts[2 * BAND :])
            bad = jnp.bitwise_and(mask[rows, columns], 3) == 3
            weight = jnp.where(bad, 0.0, scale)
            planes[0, rows, columns] = (weight * conv).astype(jnp.bfloat16)
            planes[1, rows, columns] = weight.astype(jnp.bfloat16)
    edges[:, :EDGE, :] = planes[:, :EDGE, :]
    edges[:, EDGE:, :] = planes[:, ROWS - EDGE :, :]


def warp_kernel(
    tile, dest_slot, planes, far, after, before, row_warp, col_warp, outgoing, cutout, rowed
):
    t = tile[0]
    for block, edges in ((lax.rem(t + 1, NTILE), after), (lax.rem(t + 3, NTILE), before)):
        start = pl.multiple_of(block * ROWS, ROWS)
        cutout[:, pl.ds(start + EDGE, ROWS - 2 * EDGE), :] = jnp.zeros(
            (2, ROWS - 2 * EDGE, WIDTH), jnp.bfloat16
        )
        cutout[:, pl.ds(start, EDGE), :] = edges[:, :EDGE, :]
        cutout[:, pl.ds(start + ROWS - EDGE, EDGE), :] = edges[:, EDGE:, :]
    cutout[:, pl.ds(pl.multiple_of(t * ROWS, ROWS), ROWS), :] = planes[...]
    cutout[:, pl.ds(pl.multiple_of(lax.rem(t + 2, NTILE) * ROWS, ROWS), ROWS), :] = far[...]
    for plane in range(2):
        rowed[plane * ROWS : (plane + 1) * ROWS, :] = jnp.dot(
            row_warp[...], cutout[plane], preferred_element_type=jnp.float32
        ).astype(jnp.bfloat16)
    for n in range(4):
        low, high = max(0, 256 * n - 128), min(WIDTH, 256 * n + 384)
        warped = jnp.dot(
            rowed[:, low:high],
            col_warp[low:high, 256 * n : 256 * n + 256],
            preferred_element_type=jnp.float32,
        ).astype(jnp.bfloat16)
        for down in range(8):
            for c in range(2):
                slot = dest_slot[down * 8 + 2 * n + c]
                rows = slice(down * 16, down * 16 + 16)
                columns = slice(c * 128, c * 128 + 128)
                outgoing[slot, :16, :] = warped[:ROWS][rows, columns]
                outgoing[slot, 16:, :] = warped[ROWS:][rows, columns]


def patch_kernel(table, arriving, coadd, reply, sums, served):
    sums[...] = jnp.zeros_like(sums)

    def add(patch, _):
        for rank in range(2):
            at = table[4 * patch + rank]
            sums[at] = sums[at] + arriving[2 * patch + rank].astype(jnp.float32)
        return 0

    lax.fori_loop(0, 64, add, 0, unroll=4)
    for block in range(NBLK):
        down, c = block // 8, block % 8
        value = sums[block, :16, :] / jnp.maximum(sums[block, 16:, :], FLOOR)
        coadd[down * 16 : down * 16 + 16, c * 128 : c * 128 + 128] = value
        served[block] = value.astype(jnp.bfloat16)

    def serve(patch, _):
        for rank in range(2):
            reply[2 * patch + rank] = served[table[4 * patch + 2 + rank]]
        return 0

    lax.fori_loop(0, 64, serve, 0, unroll=4)


def difference_kernel(tmpl_slot, returned, new_science, difference):
    for block in range(NBLK):
        down, c = block // 8, block % 8
        at = (slice(down * 16, down * 16 + 16), slice(c * 128, c * 128 + 128))
        difference[at] = new_science[at] - returned[tmpl_slot[block]].astype(jnp.float32)


def per_device(
    visit_image,
    mask_bits,
    visit_weight,
    basis_cols,
    basis_rows,
    kernel_coef,
    row_warp,
    col_warp,
    dest_owner,
    dest_block,
    new_science,
    tmpl_owner,
    tmpl_block,
):
    f32, bf16, i32 = jnp.float32, jnp.bfloat16, jnp.int32
    struct = jax.ShapeDtypeStruct
    tile = lax.axis_index("tile").astype(i32).reshape(1)
    up = [(i, (i + 1) % NTILE) for i in range(NTILE)]
    down = [(i, (i + 3) % NTILE) for i in range(NTILE)]
    across = [(i, (i + 2) % NTILE) for i in range(NTILE)]

    top = lax.ppermute(visit_image[ROWS - EDGE :], "tile", up[:-1])
    bottom = lax.ppermute(visit_image[:EDGE], "tile", down[1:])

    dest_slot, tmpl_slot, table = call(
        index_kernel,
        (struct((64,), i32), struct((64,), i32), struct((256,), i32)),
        [SMEM] * 4,
        (SMEM,) * 3,
        [pltpu.SMEM((128,), i32)],
        "slots",
        1000,
        4096,
    )(dest_owner[:, 0], dest_block, tmpl_owner[:, 0], tmpl_block)
    received = lax.all_to_all(
        table.reshape(64, 4), "ccd", split_axis=0, concat_axis=0, tiled=True
    ).reshape(256)

    cols = jnp.pad(basis_cols.astype(f32), ((0, 1), (6, 128 - 6 - TAPS)))
    rows_t = jnp.pad(basis_rows.astype(f32).T, ((0, 3), (0, 1)))
    coef = jnp.pad(kernel_coef[0], ((0, 1), (0, 0)))
    taps = call(
        table_kernel,
        struct((2, 3 * BAND, DEPTH), bf16),
        [SMEM, VMEM, VMEM, VMEM],
        VMEM,
        [],
        "taps",
        10_000_000,
        2_000_000,
    )(tile, coef, cols, rows_t)
    planes, edges = call(
        conv_kernel,
        (struct((2, ROWS, WIDTH), bf16), struct((2, 2 * EDGE, WIDTH), bf16)),
        [SMEM] + [VMEM] * 5,
        (VMEM, VMEM),
        [pltpu.VMEM((2, DEPTH, WIDTH), bf16)],
        "matching",
        2 * 2 * 192 * DEPTH * WIDTH,
        3_000_000,
    )(visit_weight, top, visit_image, bottom, taps, mask_bits)
    far = lax.ppermute(planes, "tile", across)
    after = lax.ppermute(edges, "tile", down)
    before = lax.ppermute(edges, "tile", up)
    outgoing = call(
        warp_kernel,
        struct((SLOTS, 32, 128), bf16),
        [SMEM, SMEM] + [VMEM] * 6,
        VMEM,
        [pltpu.VMEM((2, CUTOUT, WIDTH), bf16), pltpu.VMEM((2 * ROWS, WIDTH), bf16)],
        "warp",
        2 * 256 * WIDTH * WIDTH,
        5_000_000,
    )(tile, dest_slot, planes, far, after, before, row_warp, col_warp[0])
    arriving = lax.all_to_all(outgoing, "ccd", split_axis=0, concat_axis=0, tiled=True)
    coadd, reply = call(
        patch_kernel,
        (struct((ROWS, WIDTH), f32), struct((SLOTS, 16, 128), bf16)),
        [SMEM, VMEM],
        (VMEM, VMEM),
        [pltpu.VMEM((NBLK + 8, 32, 128), f32), pltpu.VMEM((NBLK, 16, 128), bf16)],
        "patch",
        1_000_000,
        2_000_000,
    )(received, arriving)
    returned = lax.all_to_all(reply, "ccd", split_axis=0, concat_axis=0, tiled=True)
    difference = call(
        difference_kernel,
        struct((ROWS, WIDTH), f32),
        [SMEM, VMEM, VMEM],
        VMEM,
        [],
        "difference",
        1_000_000,
        2_000_000,
    )(tmpl_slot, returned, new_science)
    return coadd, difference


def solution(mesh):
    both = P(("ccd", "tile"), None)
    return jax.shard_map(
        per_device,
        mesh=mesh,
        in_specs=(
            both,
            both,
            P("ccd"),
            P(),
            P(),
            P("ccd", None, None),
            both,
            P("ccd", None, None),
            both,
            P(("ccd", "tile")),
            both,
            both,
            P(("ccd", "tile")),
        ),
        out_specs=(both, both),
        check_vma=False,
    )
```

profile of v0, /device:TPU:1, one launch (start us, length us, event | category | flops | bytes accessed | tf_op | source)
XLA Modules:
  0.0 109.3 jit_solution(10961205684047989442)
XLA Ops:
  0.6 0.8 fusion
  1.4 1.3 %collective-permute-start.1 = (bf16[16,1024]{1,0:T(8,128)(2,1)S(1)}, bf16[16,1024]{1,0:T(8,128)(2,1)S(1)}, u32[]{:S(2)}, u32[]{:S(2)}) collective-permute-start(bf16[16,1024]{1,0:T(8,128)(2,1)S(1)} %get-tuple-element.16), channel_id=1, source_target_pairs={{1,0},{2,1},{3,2},{5,4},{6,5},{7,6},{9,8},{10,9},{11,10},{13,12},{... | collective-permute-start | bytes 98312 | tf_op jit(solution)/shard_map/ppermute | solution.py:241
  2.7 4.7 %collective-permute-start = (bf16[16,1024]{1,0:T(8,128)(2,1)S(1)}, bf16[16,1024]{1,0:T(8,128)(2,1)S(1)}, u32[]{:S(2)}, u32[]{:S(2)}) collective-permute-start(bf16[16,1024]{1,0:T(8,128)(2,1)S(1)} %get-tuple-element.17), channel_id=1, source_target_pairs={{0,1},{1,2},{2,3},{4,5},{5,6},{6,7},{8,9},{9,10},{10,11},{12,13},{... | collective-permute-start | bytes 98312 | tf_op jit(solution)/shard_map/ppermute | solution.py:240
  7.4 0.8 copy.21
  8.2 0.1 pad_convert_fusion.cols
  8.2 0.7 pad_convert_fusion.1.rows_t
  9.6 0.8 copy.20
  10.4 0.0 copy-start.5
  10.4 0.0 copy-start.6
  10.4 0.0 copy-start.7
  10.4 1.1 %taps.1.table = bf16[2,192,2048]{2,1,0:T(8,128)(2,1)S(1)} custom-call(s32[1]{0:T(128)} %bitcast.3.tile, f32[32,6]{1,0:T(8,128)S(1)} %pad.16.coef, f32[32,128]{1,0:T(8,128)S(1)} %pad_convert_fusion.cols, f32[24,32]{1,0:T(8,128)S(1)} %pad_convert_fusion.1.rows_t), custom_call_target="tpu_custom_call" | custom-call | flops 10000000 | bytes 2000000 | tf_op jit(solution)/shard_map/taps/pallas_call | solution.py:260
  11.5 0.0 copy-start
  11.5 0.0 copy-start.2
  11.6 0.0 copy-start.3
  11.6 1.1 copy-done.3
  12.7 1.0 copy-done.8
  13.7 3.5 %matching.1 = (bf16[2,128,1024]{2,1,0:T(8,128)(2,1)S(1)}, bf16[2,32,1024]{2,1,0:T(8,128)(2,1)}) custom-call(f32[1]{0:T(128)S(6)} %copy.22.visit_weight, bf16[16,1024]{1,0:T(8,128)(2,1)S(1)} %collective-permute-done.top, bf16[128,1024]{1,0:T(8,128)(2,1)S(1)} %copy-done.3, bf16[16,1024]{1,0:T(8,128)(2,1)S(1)} %collective-permute-done.1.bottom, ...), custom_call_target="tpu_custom_call" | custom-call | flops 1610612736 | bytes 3000000 | tf_op jit(solution)/shard_map/matching/pallas_call | solution.py:270
  17.2 3.1 %collective-permute-start.2 = (bf16[2,128,1024]{2,1,0:T(8,128)(2,1)S(1)}, bf16[2,128,1024]{2,1,0:T(8,128)(2,1)S(1)}, u32[]{:S(2)}, u32[]{:S(2)}) collective-permute-start(bf16[2,128,1024]{2,1,0:T(8,128)(2,1)S(1)} %get-tuple-element.11.planes), channel_id=1, source_target_pairs={{0,2},{1,3},{2,0},{3,1},{4,6},{5,7},{6,4},{7,5},{8,10},{9,11},{10,... | collective-permute-start | bytes 1572872 | tf_op jit(solution)/shard_map/ppermute | solution.py:280
  20.3 2.7 %collective-permute-start.3 = (bf16[2,32,1024]{2,1,0:T(8,128)(2,1)}, bf16[2,32,1024]{2,1,0:T(8,128)(2,1)S(1)}, u32[]{:S(2)}, u32[]{:S(2)}) collective-permute-start(bf16[2,32,1024]{2,1,0:T(8,128)(2,1)} %get-tuple-element.12), channel_id=1, source_target_pairs={{0,3},{1,0},{2,1},{3,2},{4,7},{5,4},{6,5},{7,6},{8,11},{9,8},{10,9... | collective-permute-start | bytes 393224 | tf_op jit(solution)/shard_map/ppermute | solution.py:281
  22.9 2.1 %slots.1 = (s32[64]{0:T(128)S(1)}, s32[64]{0:T(128)S(1)}, s32[256]{0:T(256)S(1)}) custom-call(s32[64]{0:T(128)S(1)} %bitcast.8, s32[64]{0:T(128)S(1)} %copy-done.5, s32[64]{0:T(128)S(1)} %bitcast.9, s32[64]{0:T(128)S(1)} %copy-done.7), custom_call_target="tpu_custom_call" | custom-call | flops 1000 | bytes 4096 | tf_op jit(solution)/shard_map/slots/pallas_call | solution.py:243
  25.1 0.7 all_to_all.12
  25.8 13.7 %all-to-all-start = ((s32[64,1,4]{2,1,0:T(1,128)}), s32[64,1,4]{2,1,0:T(1,128)}, u32[]{:S(2)}, u32[]{:S(2)}) async-start(s32[64,1,4]{2,1,0:T(1,128)} %bitcast.10), calls=%async_computation | async-start | bytes 65536 | tf_op jit(solution)/shard_map/all_to_all | solution.py:253
  39.6 2.5 %warp.1 = bf16[128,32,128]{2,1,0:T(8,128)(2,1)} custom-call(s32[1]{0:T(128)} %bitcast.3.tile, s32[64]{0:T(128)S(1)} %get-tuple-element.10.dest_slot, bf16[2,128,1024]{2,1,0:T(8,128)(2,1)S(1)} %get-tuple-element.11.planes, bf16[2,128,1024]{2,1,0:T(8,128)(2,1)S(1)} %collective-permute-done.2.far, bf16[2,32,1024]{2,1,0:T(8,128)(2,1)S(1)} %collective-permute-done.3.after, ...), custom_call_target="tpu_custom_call" | custom-call | flops 536870912 | bytes 5000000 | tf_op jit(solution)/shard_map/warp/pallas_call | solution.py:283
  42.1 6.7 %all-to-all-done = s32[64,1,4]{2,1,0:T(1,128)} async-done(((s32[64,1,4]{2,1,0:T(1,128)}), s32[64,1,4]{2,1,0:T(1,128)}, u32[]{:S(2)}, u32[]{:S(2)}) %all-to-all-start) | async-done | bytes 1056 | tf_op jit(solution)/shard_map/all_to_all | solution.py:253
  48.7 4.9 %all-to-all-start.1 = ((bf16[128,32,128]{2,1,0:T(8,128)(2,1)}), bf16[128,32,128]{2,1,0:T(8,128)(2,1)S(1)}, u32[]{:S(2)}, u32[]{:S(2)}) async-start(bf16[128,32,128]{2,1,0:T(8,128)(2,1)} %warp.1), calls=%async_computation.1 | async-start | bytes 2097152 | tf_op jit(solution)/shard_map/all_to_all | solution.py:293
  53.6 0.5 broadcast.9
  54.1 1.5 %reduce.3 = s32[64,4]{1,0:T(8,128)S(1)} reduce(s32[64,1,4]{2,1,0:T(1,128)} %all-to-all-done, s32[]{:T(128)} %broadcast.9), dimensions={1}, to_apply=%all_to_all.13.reduce_sub_computation.3 | reduce | bytes 2052 | tf_op jit(solution)/shard_map/all_to_all | solution.py:253
  55.6 0.1 reshape.15.table
  55.7 26.0 %all-to-all-done.1.arriving = bf16[128,32,128]{2,1,0:T(8,128)(2,1)S(1)} async-done(((bf16[128,32,128]{2,1,0:T(8,128)(2,1)}), bf16[128,32,128]{2,1,0:T(8,128)(2,1)S(1)}, u32[]{:S(2)}, u32[]{:S(2)}) %all-to-all-start.1) | async-done | bytes 1048608 | tf_op jit(solution)/shard_map/all_to_all | solution.py:293
  81.7 2.3 %patch.1 = (f32[128,1024]{1,0:T(8,128)}, bf16[128,16,128]{2,1,0:T(8,128)(2,1)S(1)}) custom-call(s32[256]{0:T(256)S(1)} %reshape.15.table, bf16[128,32,128]{2,1,0:T(8,128)(2,1)S(1)} %all-to-all-done.1.arriving), custom_call_target="tpu_custom_call" | custom-call | flops 1000000 | bytes 2000000 | tf_op jit(solution)/shard_map/patch/pallas_call | solution.py:294
  84.0 23.8 %all_to_all.19.returned = bf16[128,16,128]{2,1,0:T(8,128)(2,1)S(1)} all-to-all(bf16[128,16,128]{2,1,0:T(8,128)(2,1)S(1)} %get-tuple-element.15), channel_id=1, replica_groups=mesh['ccd'=64,'tile'=4] {'ccd'}, dimensions={0} | all-to-all | bytes 1048576 | tf_op jit(solution)/shard_map/all_to_all | solution.py:304
  107.9 1.4 %difference.1 = f32[128,1024]{1,0:T(8,128)} custom-call(s32[64]{0:T(128)S(1)} %get-tuple-element.14.tmpl_slot, bf16[128,16,128]{2,1,0:T(8,128)(2,1)S(1)} %all_to_all.19.returned, f32[128,1024]{1,0:T(8,128)S(1)} %copy-done.1), custom_call_target="tpu_custom_call" | custom-call | flops 1000000 | bytes 2000000 | tf_op jit(solution)/shard_map/difference/pallas_call | solution.py:305
  (17 shorter events, 0.0 us)
Async XLA Ops:
  1.4 10.1 %collective-permute-start.1 = (bf16[16,1024]{1,0:T(8,128)(2,1)S(1)}, bf16[16,1024]{1,0:T(8,128)(2,1)S(1)}, u32[]{:S(2)}, u32[]{:S(2)}) collective-permute-start(bf16[16,1024]{1,0:T(8,128)(2,1)S(1)} %get-tuple-element.16), channel_id=1, source_target_pairs={{1,0},{2,1},{3,2},{5,4},{6,5},{7,6},{9,8},{10,9},{11,10},{13,12},{... | collective-permute-start | bytes 98312 | tf_op jit(solution)/shard_map/ppermute | solution.py:241
  2.7 8.9 %collective-permute-start = (bf16[16,1024]{1,0:T(8,128)(2,1)S(1)}, bf16[16,1024]{1,0:T(8,128)(2,1)S(1)}, u32[]{:S(2)}, u32[]{:S(2)}) collective-permute-start(bf16[16,1024]{1,0:T(8,128)(2,1)S(1)} %get-tuple-element.17), channel_id=1, source_target_pairs={{0,1},{1,2},{2,3},{4,5},{5,6},{6,7},{8,9},{9,10},{10,11},{12,13},{... | collective-permute-start | bytes 98312 | tf_op jit(solution)/shard_map/ppermute | solution.py:240
  10.4 12.5 %copy-start.4 = (s32[64,1]{0,1:T(1,128)S(1)}, s32[64,1]{0,1:T(1,128)}, u32[]{:S(2)}) copy-start(s32[64,1]{0,1:T(1,128)} %param.21) | copy-start | bytes 772
  10.4 12.5 %copy-start.5 = (s32[64]{0:T(128)S(1)}, s32[64]{0:T(128)}, u32[]{:S(2)}) copy-start(s32[64]{0:T(128)} %dest_block.1) | copy-start | bytes 772
  10.4 12.5 %copy-start.6 = (s32[64,1]{0,1:T(1,128)S(1)}, s32[64,1]{0,1:T(1,128)}, u32[]{:S(2)}) copy-start(s32[64,1]{0,1:T(1,128)} %param.24) | copy-start | bytes 772
  10.4 12.5 %copy-start.7 = (s32[64]{0:T(128)S(1)}, s32[64]{0:T(128)}, u32[]{:S(2)}) copy-start(s32[64]{0:T(128)} %tmpl_block.1) | copy-start | bytes 772
  11.5 28.0 %copy-start = (bf16[1,1024,1024]{2,1,0:T(8,128)(2,1)S(1)}, bf16[1,1024,1024]{2,1,0:T(8,128)(2,1)}, u32[]{:S(2)}) copy-start(bf16[1,1024,1024]{2,1,0:T(8,128)(2,1)} %param.20) | copy-start | bytes 6291460
  11.5 28.0 %copy-start.2 = (bf16[128,512]{1,0:T(8,128)(2,1)S(1)}, bf16[128,512]{1,0:T(8,128)(2,1)}, u32[]{:S(2)}) copy-start(bf16[128,512]{1,0:T(8,128)(2,1)} %row_warp.1) | copy-start | bytes 393220
  11.6 1.1 %copy-start.3 = (bf16[128,1024]{1,0:T(8,128)(2,1)S(1)}, bf16[128,1024]{1,0:T(8,128)(2,1)}, u32[]{:S(2)}) copy-start(bf16[128,1024]{1,0:T(8,128)(2,1)} %image.1) | copy-start | bytes 786436
  12.7 1.0 copy-start.8
  17.2 22.4 %collective-permute-start.2 = (bf16[2,128,1024]{2,1,0:T(8,128)(2,1)S(1)}, bf16[2,128,1024]{2,1,0:T(8,128)(2,1)S(1)}, u32[]{:S(2)}, u32[]{:S(2)}) collective-permute-start(bf16[2,128,1024]{2,1,0:T(8,128)(2,1)S(1)} %get-tuple-element.11.planes), channel_id=1, source_target_pairs={{0,2},{1,3},{2,0},{3,1},{4,6},{5,7},{6,4},{7,5},{8,10},{9,11},{10,... | collective-permute-start | bytes 1572872 | tf_op jit(solution)/shard_map/ppermute | solution.py:280
  20.2 19.3 %collective-permute-start.4 = (bf16[2,32,1024]{2,1,0:T(8,128)(2,1)}, bf16[2,32,1024]{2,1,0:T(8,128)(2,1)S(1)}, u32[]{:S(2)}, u32[]{:S(2)}) collective-permute-start(bf16[2,32,1024]{2,1,0:T(8,128)(2,1)} %get-tuple-element.12), channel_id=1, source_target_pairs={{0,1},{1,2},{2,3},{3,0},{4,5},{5,6},{6,7},{7,4},{8,9},{9,10},{10,1... | collective-permute-start | bytes 393224 | tf_op jit(solution)/shard_map/ppermute | solution.py:282
  20.3 19.3 %collective-permute-start.3 = (bf16[2,32,1024]{2,1,0:T(8,128)(2,1)}, bf16[2,32,1024]{2,1,0:T(8,128)(2,1)S(1)}, u32[]{:S(2)}, u32[]{:S(2)}) collective-permute-start(bf16[2,32,1024]{2,1,0:T(8,128)(2,1)} %get-tuple-element.12), channel_id=1, source_target_pairs={{0,3},{1,0},{2,1},{3,2},{4,7},{5,4},{6,5},{7,6},{8,11},{9,8},{10,9... | collective-permute-start | bytes 393224 | tf_op jit(solution)/shard_map/ppermute | solution.py:281
  25.8 22.9 %all-to-all-start = ((s32[64,1,4]{2,1,0:T(1,128)}), s32[64,1,4]{2,1,0:T(1,128)}, u32[]{:S(2)}, u32[]{:S(2)}) async-start(s32[64,1,4]{2,1,0:T(1,128)} %bitcast.10), calls=%async_computation | async-start | bytes 65536 | tf_op jit(solution)/shard_map/all_to_all | solution.py:253
  42.0 65.8 %copy-start.1 = (f32[128,1024]{1,0:T(8,128)S(1)}, f32[128,1024]{1,0:T(8,128)}, u32[]{:S(2)}) copy-start(f32[128,1024]{1,0:T(8,128)} %new_science.1) | copy-start | bytes 1572868
  48.7 33.0 %all-to-all-start.1 = ((bf16[128,32,128]{2,1,0:T(8,128)(2,1)}), bf16[128,32,128]{2,1,0:T(8,128)(2,1)S(1)}, u32[]{:S(2)}, u32[]{:S(2)}) async-start(bf16[128,32,128]{2,1,0:T(8,128)(2,1)} %warp.1), calls=%async_computation.1 | async-start | bytes 2097152 | tf_op jit(solution)/shard_map/all_to_all | solution.py:293
where the time goes:
time: 110 us; the launch traced here: 109 us
  waiting for transfers between devices  32.7 us (30%)
  starting transfers between devices  30.3 us (28%)
  blocking collectives  23.8 us (22%)
  Pallas kernels  12.8 us (12%)
  local copies, waits for them, and re-layouts  5.87 us (5%)
  other arithmetic  2.26 us (2%)
  between operations  1.45 us (1%)
    all_to_all x1, waiting for transfers between devices, per_device(): lax.all_to_all(outgoing, 'ccd', split_axis=0, concat_axis=0, tiled=True)  26 us
    all_to_all x1, blocking collectives, per_device(): lax.all_to_all(reply, 'ccd', split_axis=0, concat_axis=0, tiled=True)  23.8 us
    all_to_all x1, starting transfers between devices, per_device(): lax.all_to_all(table.reshape(64, 4), 'ccd', split_axis=0, concat_axis=0,...  13.7 us
    all_to_all x1, waiting for transfers between devices, per_device(): lax.all_to_all(table.reshape(64, 4), 'ccd', split_axis=0, concat_axis=0,...  6.66 us
    all_to_all x1, starting transfers between devices, per_device(): lax.all_to_all(outgoing, 'ccd', split_axis=0, concat_axis=0, tiled=True)  4.87 us
    ppermute x1, starting transfers between devices, per_device(): top = lax.ppermute(visit_image[ROWS - EDGE:], 'tile', up[:-1])  4.66 us
    unnamed x20, local copies, waits for them, and re-layouts  3.75 us
    pallas_call x1, Pallas kernels, per_device(): call(conv_kernel, (struct((2, ROWS, WIDTH), bf16), struct((2, 2 * EDGE, W...  3.46 us
  transfers between devices with their start and end apart: 7, of which 2 were waited for; matrix products, arithmetic and copies ran while one was open for 4% of the time, Pallas kernels for 5%

commit v1 on v0

v1 whole, which is shorter than its diff:
```python
import functools

import jax
import jax.numpy as jnp
from jax import lax
from jax.experimental import pallas as pl
from jax.experimental.pallas import tpu as pltpu
from jax.sharding import PartitionSpec as P

BLOCK_ROWS = 16
BLOCK_COLUMNS = 128
FLOOR = 1.0

ROWS = 128
WIDTH = 1024
CUTOUT = 512
NTILE = 4
NB = 31
TAPS = 21
HALF = 10
EDGE = 16
BAND = 64
WINDOW = 96
DEPTH = 2048
USED = TAPS * WINDOW
NBLK = 64
SLOTS = 128
NOTE = 8
MESSAGE = 64 + NOTE

VMEM = pl.BlockSpec(memory_space=pltpu.VMEM)
HBM = pl.BlockSpec(memory_space=pltpu.HBM)
SMEM = pl.BlockSpec(memory_space=pltpu.SMEM)


def in_hbm(array):
    return pltpu.with_memory_space_constraint(array, pltpu.HBM)


def call(body, out_shape, in_specs, out_specs, scratch, name, flops, nbytes):
    return pl.pallas_call(
        body,
        out_shape=out_shape,
        in_specs=in_specs,
        out_specs=out_specs,
        scratch_shapes=scratch,
        name=name,
        compiler_params=pltpu.CompilerParams(vmem_limit_bytes=40 * 1024 * 1024),
        cost_estimate=pl.CostEstimate(flops=flops, bytes_accessed=nbytes, transcendentals=0),
    )


def index_kernel(
    home,
    dest_owner,
    dest_block,
    tmpl_owner,
    tmpl_block,
    dest_slot,
    tmpl_slot,
    notes,
    count,
    table,
):
    def clear(i, _):
        count[i] = 0
        count[64 + i] = 0
        table[4 * i] = NBLK
        table[4 * i + 1] = NBLK
        table[4 * i + 2] = 0
        table[4 * i + 3] = 0
        return 0

    lax.fori_loop(0, 64, clear, 0, unroll=8)

    def place(k, _):
        owner = dest_owner[k]
        rank = count[owner]
        count[owner] = rank + 1
        dest_slot[k] = 2 * owner + rank
        table[4 * owner + rank] = dest_block[k]
        asked = tmpl_owner[k]
        rank = count[64 + asked]
        count[64 + asked] = rank + 1
        tmpl_slot[k] = 2 * asked + rank
        table[4 * asked + 2 + rank] = tmpl_block[k]
        return 0

    lax.fori_loop(0, 64, place, 0, unroll=8)

    row = lax.broadcasted_iota(jnp.int32, (NOTE, 128), 0)
    lane = lax.broadcasted_iota(jnp.int32, (NOTE, 128), 1) - 2 * home[0]
    for patch in range(64):
        note = jnp.zeros((NOTE, 128), jnp.int32)
        for kind in range(2):
            for rank in range(2):
                here = (row == kind) & (lane == rank)
                note = jnp.where(here, table[4 * patch + 2 * kind + rank], note)
        notes[patch] = note.astype(jnp.float32).astype(jnp.bfloat16)


def table_kernel(tile, coef, cols_t, rows_t, table, wide):
    wide[...] = jnp.zeros_like(wide)
    wide[6 : 6 + TAPS, :] = cols_t[...].astype(jnp.float32)
    taps = []
    for p in range(6):
        taps.append(
            lax.dot_general(
                rows_t[...].astype(jnp.float32) * coef[p],
                wide[...],
                (((1,), (1,)), ((), ())),
                preferred_element_type=jnp.float32,
                precision=lax.Precision.HIGHEST,
            )
        )
    lane = lax.broadcasted_iota(jnp.int32, (BAND, 128), 1)
    row = lax.broadcasted_iota(jnp.int32, (BAND, 128), 0)
    for band in range(2):
        first = tile[0] * ROWS + band * BAND
        yn = (2.0 * (first + row).astype(jnp.float32) + 1.0) / CUTOUT - 1.0
        yy = yn * yn

        def turned(i):
            v = [jnp.broadcast_to(taps[p][i : i + 1, :], (BAND, 128)) for p in range(6)]
            mixed = (v[0] + yn * v[1] + yy * v[3], v[2] + yn * v[4], v[5])
            return [
                pltpu.roll(m, (i * WINDOW) % 128, 1, stride=1, stride_axis=0) for m in mixed
            ]

        held = {}
        for column in range(DEPTH // 128):
            left = (128 * column) // WINDOW
            bound = (left + 1) * WINDOW - 128 * column
            for i in (left, left + 1):
                if i < TAPS and i not in held:
                    held[i] = turned(i)
            for q in range(3):
                other = held[left + 1][q] if left + 1 < TAPS else jnp.zeros((BAND, 128), jnp.float32)
                table[band, q * BAND : (q + 1) * BAND, column * 128 : (column + 1) * 128] = jnp.where(
                    lane < bound, held[left][q], other
                ).astype(jnp.bfloat16)
            held = {i: held[i] for i in held if i > left}


def good_weight(mask, scale):
    return jnp.where(jnp.bitwise_and(mask, 3) == 3, 0.0, scale)


def edge_kernel(visit_weight, image, mask, to_next, to_previous, ends, sems):
    last = ROWS - EDGE
    copies = [
        pltpu.make_async_copy(mask.at[pl.ds(0, EDGE)], ends.at[0], sems.at[0]),
        pltpu.make_async_copy(mask.at[pl.ds(last, EDGE)], ends.at[1], sems.at[1]),
        pltpu.make_async_copy(image.at[pl.ds(last, EDGE)], to_next.at[pl.ds(0, EDGE)], sems.at[2]),
        pltpu.make_async_copy(image.at[pl.ds(0, EDGE)], to_previous.at[pl.ds(0, EDGE)], sems.at[3]),
    ]
    for copy in copies:
        copy.start()
    scale = visit_weight[0].astype(jnp.bfloat16).astype(jnp.float32)
    for end in range(2):
        copies[end].wait()
        weight = good_weight(ends[end], scale).astype(jnp.bfloat16)
        rows = slice((end + 1) * EDGE, (end + 2) * EDGE)
        to_next[rows, :] = weight
        to_previous[rows, :] = weight
    copies[2].wait()
    copies[3].wait()


def weight_kernel(visit_weight, mask, weights, held, sems):
    copies = []
    for part in range(4):
        rows = pl.ds(part * 32, 32)
        copies.append(pltpu.make_async_copy(mask.at[rows], held.at[rows], sems.at[part]))
        copies[part].start()
    scale = visit_weight[0].astype(jnp.bfloat16).astype(jnp.float32)
    for part in range(4):
        copies[part].wait()
        rows = slice(part * 32, part * 32 + 32)
        weights[rows, :] = good_weight(held[rows, :], scale).astype(jnp.bfloat16)


def conv_kernel(tile, before, image, after, table, weights, flux, edges, stack):
    t = tile[0]
    for group in range(10):
        if group == 0:
            strip = jnp.where(t > 0, before[:EDGE, :].astype(jnp.float32), 0.0)
        elif group == 9:
            strip = jnp.where(t < NTILE - 1, after[:EDGE, :].astype(jnp.float32), 0.0)
        else:
            strip = image[(group - 1) * 16 : group * 16, :].astype(jnp.float32)
        strip = jnp.concatenate([strip, jnp.zeros((16, 128), jnp.float32)], axis=1)
        for i in range(TAPS):
            moved = strip if i == HALF else pltpu.roll(strip, (HALF - i) % (WIDTH + 128), 1)
            moved = moved[:, :WIDTH].astype(jnp.bfloat16)
            if group < 6:
                at = i * WINDOW + group * 16
                stack[0, at : at + 16, :] = moved
            if group >= 4:
                at = i * WINDOW + group * 16 - BAND
                stack[1, at : at + 16, :] = moved
    stack[:, USED:, :] = jnp.zeros((2, DEPTH - USED, WIDTH), jnp.bfloat16)
    for band in range(2):
        rows = slice(band * BAND, (band + 1) * BAND)
        for n in range(4):
            columns = slice(n * 256, (n + 1) * 256)
            parts = jnp.dot(
                table[band], stack[band, :, columns], preferred_element_type=jnp.float32
            )
            x = lax.broadcasted_iota(jnp.int32, (BAND, 256), 1) + n * 256
            xn = (2.0 * x.astype(jnp.float32) + 1.0) / WIDTH - 1.0
            conv = parts[:BAND] + xn * (parts[BAND : 2 * BAND] + xn * parts[2 * BAND :])
            flux[rows, columns] = (weights[rows, columns].astype(jnp.float32) * conv).astype(
                jnp.bfloat16
            )
    edges[:EDGE, :] = flux[:EDGE, :]
    edges[EDGE:, :] = flux[ROWS - EDGE :, :]


def warp_plane(t, own, far, after, before, row_warp, col_warp, cutout, rowed):
    for block, edges in ((lax.rem(t + 1, NTILE), after), (lax.rem(t + 3, NTILE), before)):
        start = pl.multiple_of(block * ROWS, ROWS)
        cutout[pl.ds(start + EDGE, ROWS - 2 * EDGE), :] = jnp.zeros(
            (ROWS - 2 * EDGE, WIDTH), jnp.bfloat16
        )
        cutout[pl.ds(start, EDGE), :] = edges[:EDGE, :]
        cutout[pl.ds(start + ROWS - EDGE, EDGE), :] = edges[EDGE:, :]
    cutout[pl.ds(pl.multiple_of(t * ROWS, ROWS), ROWS), :] = own[...]
    cutout[pl.ds(pl.multiple_of(lax.rem(t + 2, NTILE) * ROWS, ROWS), ROWS), :] = far[...]
    rowed[...] = jnp.dot(row_warp[...], cutout[...], preferred_element_type=jnp.float32).astype(
        jnp.bfloat16
    )
    for n in range(4):
        low, high = max(0, 256 * n - 128), min(WIDTH, 256 * n + 384)
        yield (
            n,
            jnp.dot(
                rowed[:, low:high],
                col_warp[low:high, 256 * n : 256 * n + 256],
                preferred_element_type=jnp.float32,
            ).astype(jnp.bfloat16),
        )


def warp_weight_kernel(
    tile, own, far, after, before, row_warp, col_warp, warped, cutout, rowed
):
    after, before = after.at[pl.ds(EDGE, 2 * EDGE)], before.at[pl.ds(EDGE, 2 * EDGE)]
    for n, part in warp_plane(
        tile[0], own, far, after, before, row_warp, col_warp, cutout, rowed
    ):
        warped[:, 256 * n : 256 * n + 256] = part


def warp_flux_kernel(
    tile,
    dest_slot,
    own,
    far,
    after,
    before,
    row_warp,
    col_warp,
    warped_weight,
    notes,
    outgoing,
    cutout,
    rowed,
):
    outgoing[:, 64:, :] = notes[...]
    for n, part in warp_plane(
        tile[0], own, far, after, before, row_warp, col_warp, cutout, rowed
    ):
        for down in range(8):
            for c in range(2):
                column = 2 * n + c
                slot = dest_slot[down * 8 + column]
                owner, at = slot // 2, pl.multiple_of(lax.rem(slot, 2) * 32, 32)
                rows = slice(down * 16, down * 16 + 16)
                outgoing[owner, pl.ds(at, 16), :] = part[rows, c * 128 : c * 128 + 128]
                outgoing[owner, pl.ds(at + 16, 16), :] = warped_weight[
                    rows, column * 128 : column * 128 + 128
                ]


def patch_kernel(arriving, coadd, reply, sums, served, note, table, sem):
    notes = arriving[0, 64:, :].astype(jnp.float32)
    for sender in range(1, 64):
        notes = notes + arriving[sender, 64:, :].astype(jnp.float32)
    note[...] = notes.astype(jnp.int32)
    copy = pltpu.make_async_copy(note, table, sem)
    copy.start()
    sums[...] = jnp.zeros_like(sums)
    copy.wait()

    def add(sender, _):
        for rank in range(2):
            at = table[0, 2 * sender + rank]
            sums[at] = sums[at] + arriving[sender, rank * 32 : rank * 32 + 32, :].astype(jnp.float32)
        return 0

    lax.fori_loop(0, 64, add, 0, unroll=4)
    for block in range(NBLK):
        down, c = block // 8, block % 8
        value = sums[block, :16, :] / jnp.maximum(sums[block, 16:, :], FLOOR)
        coadd[down * 16 : down * 16 + 16, c * 128 : c * 128 + 128] = value
        served[block] = value.astype(jnp.bfloat16)

    def serve(sender, _):
        for rank in range(2):
            reply[2 * sender + rank] = served[table[1, 2 * sender + rank]]
        return 0

    lax.fori_loop(0, 64, serve, 0, unroll=4)


def difference_kernel(tmpl_slot, returned, new_science, difference):
    for block in range(NBLK):
        down, c = block // 8, block % 8
        at = (slice(down * 16, down * 16 + 16), slice(c * 128, c * 128 + 128))
        difference[at] = new_science[at] - returned[tmpl_slot[block]].astype(jnp.float32)


def per_device(
    visit_image,
    mask_bits,
    visit_weight,
    basis_cols,
    basis_rows,
    kernel_coef,
    row_warp,
    col_warp,
    dest_owner,
    dest_block,
    new_science,
    tmpl_owner,
    tmpl_block,
):
    f32, bf16, i32 = jnp.float32, jnp.bfloat16, jnp.int32
    struct = jax.ShapeDtypeStruct
    tile = lax.axis_index("tile").astype(i32).reshape(1)
    home = lax.axis_index("ccd").astype(i32).reshape(1)
    up = [(i, (i + 1) % NTILE) for i in range(NTILE)]
    down = [(i, (i + 3) % NTILE) for i in range(NTILE)]
    across = [(i, (i + 2) % NTILE) for i in range(NTILE)]

    to_next, to_previous = call(
        edge_kernel,
        (struct((3 * EDGE, WIDTH), bf16),) * 2,
        [SMEM, HBM, HBM],
        (VMEM, VMEM),
        [pltpu.VMEM((2, EDGE, WIDTH), i32), pltpu.SemaphoreType.DMA((4,))],
        "edges",
        100_000,
        400_000,
    )(visit_weight, in_hbm(visit_image), in_hbm(mask_bits))
    before = lax.ppermute(to_next, "tile", up)
    after = lax.ppermute(to_previous, "tile", down)
    weights = call(
        weight_kernel,
        struct((ROWS, WIDTH), bf16),
        [SMEM, HBM],
        VMEM,
        [pltpu.VMEM((ROWS, WIDTH), i32), pltpu.SemaphoreType.DMA((4,))],
        "weights",
        400_000,
        800_000,
    )(visit_weight, in_hbm(mask_bits))
    far_weights = lax.ppermute(weights, "tile", across)

    dest_slot, tmpl_slot, notes = call(
        index_kernel,
        (struct((64,), i32), struct((64,), i32), struct((64, NOTE, 128), bf16)),
        [SMEM] * 5,
        (SMEM, SMEM, VMEM),
        [pltpu.SMEM((128,), i32), pltpu.SMEM((256,), i32)],
        "slots",
        2_000_000,
        1_000_000,
    )(home, dest_owner[:, 0], dest_block, tmpl_owner[:, 0], tmpl_block)

    taps = call(
        table_kernel,
        struct((2, 3 * BAND, DEPTH), bf16),
        [SMEM, VMEM, VMEM, VMEM],
        VMEM,
        [pltpu.VMEM((128, NB), f32)],
        "taps",
        10_000_000,
        2_000_000,
    )(tile, kernel_coef.transpose(2, 0, 1), basis_cols.T, basis_rows.T)
    flux, edges = call(
        conv_kernel,
        (struct((ROWS, WIDTH), bf16), struct((2 * EDGE, WIDTH), bf16)),
        [SMEM] + [VMEM] * 5,
        (VMEM, VMEM),
        [pltpu.VMEM((2, DEPTH, WIDTH), bf16)],
        "matching",
        2 * 2 * 192 * DEPTH * WIDTH,
        3_000_000,
    )(tile, before, visit_image, after, taps, weights)
    far_flux = lax.ppermute(flux, "tile", across)
    after_flux = lax.ppermute(edges, "tile", down)
    before_flux = lax.ppermute(edges, "tile", up)
    scratch = [pltpu.VMEM((CUTOUT, WIDTH), bf16), pltpu.VMEM((ROWS, WIDTH), bf16)]
    warped_weight = call(
        warp_weight_kernel,
        struct((ROWS, WIDTH), bf16),
        [SMEM] + [VMEM] * 6,
        VMEM,
        scratch,
        "warp_weight",
        2 * 128 * WIDTH * WIDTH,
        4_000_000,
    )(tile, weights, far_weights, after, before, row_warp, col_warp[0])
    outgoing = call(
        warp_flux_kernel,
        struct((64, MESSAGE, 128), bf16),
        [SMEM, SMEM] + [VMEM] * 8,
        VMEM,
        scratch,
        "warp_flux",
        2 * 128 * WIDTH * WIDTH,
        5_000_000,
    )(
        tile,
        dest_slot,
        flux,
        far_flux,
        after_flux,
        before_flux,
        row_warp,
        col_warp[0],
        warped_weight,
        notes,
    )
    arriving = lax.all_to_all(outgoing, "ccd", split_axis=0, concat_axis=0, tiled=True)
    coadd, reply = call(
        patch_kernel,
        (struct((ROWS, WIDTH), f32), struct((SLOTS, 16, 128), bf16)),
        [VMEM],
        (VMEM, VMEM),
        [
            pltpu.VMEM((NBLK + 8, 32, 128), f32),
            pltpu.VMEM((NBLK, 16, 128), bf16),
            pltpu.VMEM((NOTE, 128), i32),
            pltpu.SMEM((NOTE, 128), i32),
            pltpu.SemaphoreType.DMA,
        ],
        "patch",
        1_000_000,
        2_000_000,
    )(arriving)
    returned = lax.all_to_all(reply, "ccd", split_axis=0, concat_axis=0, tiled=True)
    difference = call(
        difference_kernel,
        struct((ROWS, WIDTH), f32),
        [SMEM, VMEM, VMEM],
        VMEM,
        [],
        "difference",
        1_000_000,
        2_000_000,
    )(tmpl_slot, returned, new_science)
    return coadd, difference


def solution(mesh):
    both = P(("ccd", "tile"), None)
    return jax.shard_map(
        per_device,
        mesh=mesh,
        in_specs=(
            both,
            both,
            P("ccd"),
            P(),
            P(),
            P("ccd", None, None),
            both,
            P("ccd", None, None),
            both,
            P(("ccd", "tile")),
            both,
            both,
            P(("ccd", "tile")),
        ),
        out_specs=(both, both),
        check_vma=False,
    )
```

time: 110 us -> 97.5 us (0.89)
  blocking collectives: 23.8 us -> 70.2 us
  waiting for transfers between devices: 32.7 us -> 1.83 us
  starting transfers between devices: 30.3 us -> 8.25 us
  local copies, waits for them, and re-layouts: 5.87 us -> 0.06 us
  Pallas kernels: 12.8 us -> 15.4 us
  other arithmetic: 2.26 us -> 0 us
    all_to_all x0 -> x1, blocking collectives: none -> 46.1 us  [per_device(): lax.all_to_all(outgoing, 'ccd', split_axis=0, concat_axis=0, tiled=True)]
    all_to_all x2 -> x0, waiting for transfers between devices: 32.7 us -> none  [the longest x1 26 us: per_device(): lax.all_to_all(outgoing, 'ccd', split_axis=0, concat_axis=0, tiled=True)]
    all_to_all x2 -> x0, starting transfers between devices: 18.6 us -> none  [the longest x1 13.7 us: per_device(): lax.all_to_all(table.reshape(64, 4), 'ccd', split_axis=0, concat_axis=0,...]
    unnamed x20 -> x22, local copies, waits for them, and re-layouts: 3.75 us -> 0.06 us
    ppermute x5 -> x6, starting transfers between devices: 11.7 us -> 8.25 us  [the longest x1 2.2 us: per_device(): before = lax.ppermute(to_next, 'tile', up)]
    pallas_call x3 -> x6, Pallas kernels: 8.03 us -> 10 us  [the longest x1 3.53 us: per_device(): call(conv_kernel, (struct((ROWS, WIDTH), bf16), struct((2 * EDGE, WIDTH),...]
    ppermute x5 -> x6, waiting for transfers between devices: 0.01 us -> 1.83 us  [the longest x1 1.67 us: per_device(): before_flux = lax.ppermute(edges, 'tile', up)]
    all_to_all x1 -> x0, other arithmetic: 1.49 us -> none  [per_device(): lax.all_to_all(table.reshape(64, 4), 'ccd', split_axis=0, concat_axis=0,...]
  transfers between devices with their start and end apart: 7 -> 6, of which waited for: 2 -> 2; matrix products, arithmetic and copies ran while one was open for 4% -> 0% of each run, Pallas kernels for 5% -> 9%
where the time goes in v1:
time: 97.5 us; the launch traced here: 97.2 us
  blocking collectives  70.2 us (72%)
  Pallas kernels  15.4 us (16%)
  starting transfers between devices  8.25 us (8%)
  waiting for transfers between devices  1.83 us (2%)
  between operations  1.5 us (2%)
    all_to_all x1, blocking collectives, per_device(): lax.all_to_all(outgoing, 'ccd', split_axis=0, concat_axis=0, tiled=True)  46.1 us
    all_to_all x1, blocking collectives, per_device(): lax.all_to_all(reply, 'ccd', split_axis=0, concat_axis=0, tiled=True)  24.1 us
    pallas_call x1, Pallas kernels, per_device(): call(conv_kernel, (struct((ROWS, WIDTH), bf16), struct((2 * EDGE, WIDTH),...  3.53 us
    pallas_call x1, Pallas kernels, per_device(): call(patch_kernel, (struct((ROWS, WIDTH), f32), struct((SLOTS, 16, 128),...  2.59 us
    ppermute x1, starting transfers between devices, per_device(): before = lax.ppermute(to_next, 'tile', up)  2.2 us
    pallas_call x1, Pallas kernels, per_device(): call(index_kernel, (struct((64,), i32), struct((64,), i32), struct((64, N...  2.16 us
  transfers between devices with their start and end apart: 6, of which 2 were waited for; matrix products, arithmetic and copies ran while one was open for 0% of the time, Pallas kernels for 9%

profile of v1, /device:TPU:1, one launch (start us, length us, event | category | flops | bytes accessed | tf_op | source)
XLA Modules:
  0.0 97.2 jit_solution(9777608612489358931)
XLA Ops:
  0.6 0.0 copy-start.6
  0.6 0.0 copy-start.4
  0.7 0.0 copy-start.5
  1.3 1.0 edges.1
  2.3 2.2 %collective-permute-start = (bf16[48,1024]{1,0:T(8,128)(2,1)S(1)}, bf16[48,1024]{1,0:T(8,128)(2,1)S(1)}, u32[]{:S(2)}, u32[]{:S(2)}) collective-permute-start(bf16[48,1024]{1,0:T(8,128)(2,1)S(1)} %get-tuple-element.12), channel_id=1, source_target_pairs={{0,1},{1,2},{2,3},{3,0},{4,5},{5,6},{6,7},{7,4},{8,9},{9,10},{10,1... | collective-permute-start | bytes 294920 | tf_op jit(solution)/shard_map/ppermute | solution.py:357
  4.5 1.5 %collective-permute-start.1 = (bf16[48,1024]{1,0:T(8,128)(2,1)S(1)}, bf16[48,1024]{1,0:T(8,128)(2,1)S(1)}, u32[]{:S(2)}, u32[]{:S(2)}) collective-permute-start(bf16[48,1024]{1,0:T(8,128)(2,1)S(1)} %get-tuple-element.13), channel_id=1, source_target_pairs={{0,3},{1,0},{2,1},{3,2},{4,7},{5,4},{6,5},{7,6},{8,11},{9,8},{10,9... | collective-permute-start | bytes 294920 | tf_op jit(solution)/shard_map/ppermute | solution.py:358
  6.0 1.1 %weights.1.own = bf16[128,1024]{1,0:T(8,128)(2,1)S(1)} custom-call(f32[1]{0:T(128)S(6)} %copy.15.visit_weight, s32[128,1024]{1,0:T(8,128)} %mask.3), custom_call_target="tpu_custom_call" | custom-call | flops 400000 | bytes 800000 | tf_op jit(solution)/shard_map/weights/pallas_call | solution.py:359
  7.2 1.6 %collective-permute-start.5 = (bf16[128,1024]{1,0:T(8,128)(2,1)S(1)}, bf16[128,1024]{1,0:T(8,128)(2,1)S(1)}, u32[]{:S(2)}, u32[]{:S(2)}) collective-permute-start(bf16[128,1024]{1,0:T(8,128)(2,1)S(1)} %weights.1.own), channel_id=1, source_target_pairs={{0,2},{1,3},{2,0},{3,1},{4,6},{5,7},{6,4},{7,5},{8,10},{9,11},{10,... | collective-permute-start | bytes 786440 | tf_op jit(solution)/shard_map/ppermute | solution.py:369
  8.8 1.4 %taps.1.table = bf16[2,192,2048]{2,1,0:T(8,128)(2,1)S(1)} custom-call(s32[1]{0:T(128)} %bitcast.tile, f32[6,1,31]{2,1,0:T(1,128)S(1)} %bitcast.12, bf16[21,31]{1,0:T(8,128)(2,1)S(1)} %bitcast.10, bf16[21,31]{1,0:T(8,128)(2,1)S(1)} %bitcast.11), custom_call_target="tpu_custom_call" | custom-call | flops 10000000 | bytes 2000000 | tf_op jit(solution)/shard_map/taps/pallas_call | solution.py:382
  10.3 0.0 copy-start.7
  10.3 0.0 copy-start.8
  10.3 0.0 copy-start.9
  10.3 0.0 copy-start.10
  10.3 0.0 copy-start
  10.3 0.0 copy-start.2
  10.3 0.0 collective-permute-done.before
  10.3 0.0 collective-permute-done.1.after
  10.4 3.5 %matching.1 = (bf16[128,1024]{1,0:T(8,128)(2,1)S(1)}, bf16[32,1024]{1,0:T(8,128)(2,1)}) custom-call(s32[1]{0:T(128)} %bitcast.tile, bf16[48,1024]{1,0:T(8,128)(2,1)S(1)} %collective-permute-done.before, bf16[128,1024]{1,0:T(8,128)(2,1)S(1)} %copy-done.3, bf16[48,1024]{1,0:T(8,128)(2,1)S(1)} %collective-permute-done.1.after, ...), custom_call_target="tpu_custom_call" | custom-call | flops 1610612736 | bytes 3000000 | tf_op jit(solution)/shard_map/matching/pallas_call | solution.py:392
  13.9 1.4 %collective-permute-start.2 = (bf16[128,1024]{1,0:T(8,128)(2,1)S(1)}, bf16[128,1024]{1,0:T(8,128)(2,1)S(1)}, u32[]{:S(2)}, u32[]{:S(2)}) collective-permute-start(bf16[128,1024]{1,0:T(8,128)(2,1)S(1)} %get-tuple-element.14.own), channel_id=1, source_target_pairs={{0,2},{1,3},{2,0},{3,1},{4,6},{5,7},{6,4},{7,5},{8,10},{9,11},{10,... | collective-permute-start | bytes 786440 | tf_op jit(solution)/shard_map/ppermute | solution.py:402
  15.3 1.4 %collective-permute-start.3 = (bf16[32,1024]{1,0:T(8,128)(2,1)}, bf16[32,1024]{1,0:T(8,128)(2,1)S(1)}, u32[]{:S(2)}, u32[]{:S(2)}) collective-permute-start(bf16[32,1024]{1,0:T(8,128)(2,1)} %get-tuple-element.15), channel_id=1, source_target_pairs={{0,3},{1,0},{2,1},{3,2},{4,7},{5,4},{6,5},{7,6},{8,11},{9,8},{10,9... | collective-permute-start | bytes 196616 | tf_op jit(solution)/shard_map/ppermute | solution.py:403
  16.7 0.1 collective-permute-start.4
  16.8 2.2 %slots.1 = (s32[64]{0:T(128)S(1)}, s32[64]{0:T(128)S(1)}, bf16[64,8,128]{2,1,0:T(8,128)(2,1)S(1)}) custom-call(s32[1]{0:T(128)} %bitcast.1.home, s32[64]{0:T(128)S(1)} %bitcast.13, s32[64]{0:T(128)S(1)} %copy-done.8, s32[64]{0:T(128)S(1)} %bitcast.14, s32[64]{0:T(128)S(1)} %copy-done.10), custom_call_target="tpu_custom_call" | custom-call | flops 2000000 | bytes 1000000 | tf_op jit(solution)/shard_map/slots/pallas_call | solution.py:371
  18.9 0.0 collective-permute-done.5.far
  19.0 0.6 warp_weight.1.warped_weight
  19.6 0.1 collective-permute-done.3.after
  19.8 1.7 %collective-permute-done.4.before = bf16[32,1024]{1,0:T(8,128)(2,1)} collective-permute-done((bf16[32,1024]{1,0:T(8,128)(2,1)}, bf16[32,1024]{1,0:T(8,128)(2,1)}, u32[]{:S(2)}, u32[]{:S(2)}) %collective-permute-start.4) | collective-permute-done | bytes 65568 | tf_op jit(solution)/shard_map/ppermute | solution.py:404
  21.4 0.0 collective-permute-done.2.far
  21.4 1.6 %warp_flux.1 = bf16[64,72,128]{2,1,0:T(8,128)(2,1)S(1)} custom-call(s32[1]{0:T(128)} %bitcast.tile, s32[64]{0:T(128)S(1)} %get-tuple-element.11.dest_slot, bf16[128,1024]{1,0:T(8,128)(2,1)S(1)} %get-tuple-element.14.own, bf16[128,1024]{1,0:T(8,128)(2,1)S(1)} %collective-permute-done.2.far, bf16[32,1024]{1,0:T(8,128)(2,1)S(1)} %collective-permute-done.3.after, ...), custom_call_target="tpu_custom_call" | custom-call | flops 268435456 | bytes 5000000 | tf_op jit(solution)/shard_map/warp_flux/pallas_call | solution.py:416
  23.0 46.1 %all_to_all.10.arriving = bf16[64,72,128]{2,1,0:T(8,128)(2,1)S(1)} all-to-all(bf16[64,72,128]{2,1,0:T(8,128)(2,1)S(1)} %warp_flux.1), channel_id=1, replica_groups=mesh['ccd'=64,'tile'=4] {'ccd'}, dimensions={0} | all-to-all | bytes 2359296 | tf_op jit(solution)/shard_map/all_to_all | solution.py:437
  69.1 2.6 %patch.1 = (f32[128,1024]{1,0:T(8,128)}, bf16[128,16,128]{2,1,0:T(8,128)(2,1)S(1)}) custom-call(bf16[64,72,128]{2,1,0:T(8,128)(2,1)S(1)} %all_to_all.10.arriving), custom_call_target="tpu_custom_call" | custom-call | flops 1000000 | bytes 2000000 | tf_op jit(solution)/shard_map/patch/pallas_call | solution.py:438
  71.7 24.1 %all_to_all.11.returned = bf16[128,16,128]{2,1,0:T(8,128)(2,1)S(1)} all-to-all(bf16[128,16,128]{2,1,0:T(8,128)(2,1)S(1)} %get-tuple-element.19), channel_id=1, replica_groups=mesh['ccd'=64,'tile'=4] {'ccd'}, dimensions={0} | all-to-all | bytes 1048576 | tf_op jit(solution)/shard_map/all_to_all | solution.py:454
  95.8 1.4 %difference.1 = f32[128,1024]{1,0:T(8,128)} custom-call(s32[64]{0:T(128)S(1)} %get-tuple-element.18.tmpl_slot, bf16[128,16,128]{2,1,0:T(8,128)(2,1)S(1)} %all_to_all.11.returned, f32[128,1024]{1,0:T(8,128)S(1)} %copy-done.1), custom_call_target="tpu_custom_call" | custom-call | flops 1000000 | bytes 2000000 | tf_op jit(solution)/shard_map/difference/pallas_call | solution.py:455
  (13 shorter events, 0.0 us)
Async XLA Ops:
  0.6 8.2 %copy-start.6 = (f32[1,31,6]{1,0,2:T(1,128)S(1)}, f32[1,31,6]{1,0,2:T(1,128)}, u32[]{:S(2)}) copy-start(f32[1,31,6]{1,0,2:T(1,128)} %param.18) | copy-start | bytes 2236
  0.6 8.2 %copy-start.4 = (bf16[31,21]{0,1:T(8,128)(2,1)S(1)}, bf16[31,21]{0,1:T(8,128)(2,1)}, u32[]{:S(2)}) copy-start(bf16[31,21]{0,1:T(8,128)(2,1)} %param.16) | copy-start | bytes 3910
  0.7 8.2 %copy-start.5 = (bf16[31,21]{0,1:T(8,128)(2,1)S(1)}, bf16[31,21]{0,1:T(8,128)(2,1)}, u32[]{:S(2)}) copy-start(bf16[31,21]{0,1:T(8,128)(2,1)} %param.17) | copy-start | bytes 3910
  1.3 9.0 %copy-start.3 = (bf16[128,1024]{1,0:T(8,128)(2,1)S(1)}, bf16[128,1024]{1,0:T(8,128)(2,1)}, u32[]{:S(2)}) copy-start(bf16[128,1024]{1,0:T(8,128)(2,1)} %image.3) | copy-start | bytes 786436
  2.3 8.0 %collective-permute-start = (bf16[48,1024]{1,0:T(8,128)(2,1)S(1)}, bf16[48,1024]{1,0:T(8,128)(2,1)S(1)}, u32[]{:S(2)}, u32[]{:S(2)}) collective-permute-start(bf16[48,1024]{1,0:T(8,128)(2,1)S(1)} %get-tuple-element.12), channel_id=1, source_target_pairs={{0,1},{1,2},{2,3},{3,0},{4,5},{5,6},{6,7},{7,4},{8,9},{9,10},{10,1... | collective-permute-start | bytes 294920 | tf_op jit(solution)/shard_map/ppermute | solution.py:357
  4.5 5.8 %collective-permute-start.1 = (bf16[48,1024]{1,0:T(8,128)(2,1)S(1)}, bf16[48,1024]{1,0:T(8,128)(2,1)S(1)}, u32[]{:S(2)}, u32[]{:S(2)}) collective-permute-start(bf16[48,1024]{1,0:T(8,128)(2,1)S(1)} %get-tuple-element.13), channel_id=1, source_target_pairs={{0,3},{1,0},{2,1},{3,2},{4,7},{5,4},{6,5},{7,6},{8,11},{9,8},{10,9... | collective-permute-start | bytes 294920 | tf_op jit(solution)/shard_map/ppermute | solution.py:358
  7.2 11.8 %collective-permute-start.5 = (bf16[128,1024]{1,0:T(8,128)(2,1)S(1)}, bf16[128,1024]{1,0:T(8,128)(2,1)S(1)}, u32[]{:S(2)}, u32[]{:S(2)}) collective-permute-start(bf16[128,1024]{1,0:T(8,128)(2,1)S(1)} %weights.1.own), channel_id=1, source_target_pairs={{0,2},{1,3},{2,0},{3,1},{4,6},{5,7},{6,4},{7,5},{8,10},{9,11},{10,... | collective-permute-start | bytes 786440 | tf_op jit(solution)/shard_map/ppermute | solution.py:369
  10.3 6.5 %copy-start.7 = (s32[64,1]{0,1:T(1,128)S(1)}, s32[64,1]{0,1:T(1,128)}, u32[]{:S(2)}) copy-start(s32[64,1]{0,1:T(1,128)} %param.21) | copy-start | bytes 772
  10.3 6.5 %copy-start.8 = (s32[64]{0:T(128)S(1)}, s32[64]{0:T(128)}, u32[]{:S(2)}) copy-start(s32[64]{0:T(128)} %dest_block.1) | copy-start | bytes 772
  10.3 6.5 %copy-start.9 = (s32[64,1]{0,1:T(1,128)S(1)}, s32[64,1]{0,1:T(1,128)}, u32[]{:S(2)}) copy-start(s32[64,1]{0,1:T(1,128)} %param.24) | copy-start | bytes 772
  10.3 6.5 %copy-start.10 = (s32[64]{0:T(128)S(1)}, s32[64]{0:T(128)}, u32[]{:S(2)}) copy-start(s32[64]{0:T(128)} %tmpl_block.1) | copy-start | bytes 772
  10.3 8.7 %copy-start = (bf16[1,1024,1024]{2,1,0:T(8,128)(2,1)S(1)}, bf16[1,1024,1024]{2,1,0:T(8,128)(2,1)}, u32[]{:S(2)}) copy-start(bf16[1,1024,1024]{2,1,0:T(8,128)(2,1)} %param.20) | copy-start | bytes 6291460
  10.3 8.7 %copy-start.2 = (bf16[128,512]{1,0:T(8,128)(2,1)S(1)}, bf16[128,512]{1,0:T(8,128)(2,1)}, u32[]{:S(2)}) copy-start(bf16[128,512]{1,0:T(8,128)(2,1)} %row_warp.3) | copy-start | bytes 393220
  13.9 7.5 %collective-permute-start.2 = (bf16[128,1024]{1,0:T(8,128)(2,1)S(1)}, bf16[128,1024]{1,0:T(8,128)(2,1)S(1)}, u32[]{:S(2)}, u32[]{:S(2)}) collective-permute-start(bf16[128,1024]{1,0:T(8,128)(2,1)S(1)} %get-tuple-element.14.own), channel_id=1, source_target_pairs={{0,2},{1,3},{2,0},{3,1},{4,6},{5,7},{6,4},{7,5},{8,10},{9,11},{10,... | collective-permute-start | bytes 786440 | tf_op jit(solution)/shard_map/ppermute | solution.py:402
  15.3 4.4 %collective-permute-start.3 = (bf16[32,1024]{1,0:T(8,128)(2,1)}, bf16[32,1024]{1,0:T(8,128)(2,1)S(1)}, u32[]{:S(2)}, u32[]{:S(2)}) collective-permute-start(bf16[32,1024]{1,0:T(8,128)(2,1)} %get-tuple-element.15), channel_id=1, source_target_pairs={{0,3},{1,0},{2,1},{3,2},{4,7},{5,4},{6,5},{7,6},{8,11},{9,8},{10,9... | collective-permute-start | bytes 196616 | tf_op jit(solution)/shard_map/ppermute | solution.py:403
  16.7 4.7 %collective-permute-start.4 = (bf16[32,1024]{1,0:T(8,128)(2,1)}, bf16[32,1024]{1,0:T(8,128)(2,1)}, u32[]{:S(2)}, u32[]{:S(2)}) collective-permute-start(bf16[32,1024]{1,0:T(8,128)(2,1)} %get-tuple-element.15), channel_id=1, source_target_pairs={{0,1},{1,2},{2,3},{3,0},{4,5},{5,6},{6,7},{7,4},{8,9},{9,10},{10,1... | collective-permute-start | bytes 196616 | tf_op jit(solution)/shard_map/ppermute | solution.py:404
  69.1 26.7 %copy-start.1 = (f32[128,1024]{1,0:T(8,128)S(1)}, f32[128,1024]{1,0:T(8,128)}, u32[]{:S(2)}) copy-start(f32[128,1024]{1,0:T(8,128)} %new_science.1) | copy-start | bytes 1572868

commit v2 on v1

--- a/solution.py
+++ b/solution.py
@@ -29,6 +29,7 @@
 MESSAGE = 64 + NOTE
 
 VMEM = pl.BlockSpec(memory_space=pltpu.VMEM)
+ANY = pl.BlockSpec(memory_space=pl.ANY)
 HBM = pl.BlockSpec(memory_space=pltpu.HBM)
 SMEM = pl.BlockSpec(memory_space=pltpu.SMEM)
 
@@ -45,7 +46,7 @@
         out_specs=out_specs,
         scratch_shapes=scratch,
         name=name,
-        compiler_params=pltpu.CompilerParams(vmem_limit_bytes=40 * 1024 * 1024),
+        compiler_params=pltpu.CompilerParams(vmem_limit_bytes=20 * 1024 * 1024),
         cost_estimate=pl.CostEstimate(flops=flops, bytes_accessed=nbytes, transcendentals=0),
     )
 
@@ -99,8 +100,14 @@
         notes[patch] = note.astype(jnp.float32).astype(jnp.bfloat16)
 
 
-def table_kernel(tile, coef, cols_t, rows_t, table, wide):
+def table_kernel(tile, coef_in, cols_in, rows_in, table, wide, coef, cols_t, rows_t, sems):
+    copies = []
+    for source, held in ((coef_in, coef), (cols_in, cols_t), (rows_in, rows_t)):
+        copies.append(pltpu.make_async_copy(source, held, sems.at[len(copies)]))
+        copies[-1].start()
     wide[...] = jnp.zeros_like(wide)
+    for copy in copies:
+        copy.wait()
     wide[6 : 6 + TAPS, :] = cols_t[...].astype(jnp.float32)
     taps = []
     for p in range(6):
@@ -146,28 +153,18 @@
     return jnp.where(jnp.bitwise_and(mask, 3) == 3, 0.0, scale)
 
 
-def edge_kernel(visit_weight, image, mask, to_next, to_previous, ends, sems):
-    last = ROWS - EDGE
+def halo_kernel(image, to_next, to_previous, sems):
     copies = [
-        pltpu.make_async_copy(mask.at[pl.ds(0, EDGE)], ends.at[0], sems.at[0]),
-        pltpu.make_async_copy(mask.at[pl.ds(last, EDGE)], ends.at[1], sems.at[1]),
-        pltpu.make_async_copy(image.at[pl.ds(last, EDGE)], to_next.at[pl.ds(0, EDGE)], sems.at[2]),
-        pltpu.make_async_copy(image.at[pl.ds(0, EDGE)], to_previous.at[pl.ds(0, EDGE)], sems.at[3]),
+        pltpu.make_async_copy(image.at[pl.ds(ROWS - EDGE, EDGE)], to_next, sems.at[0]),
+        pltpu.make_async_copy(image.at[pl.ds(0, EDGE)], to_previous, sems.at[1]),
     ]
     for copy in copies:
         copy.start()
-    scale = visit_weight[0].astype(jnp.bfloat16).astype(jnp.float32)
-    for end in range(2):
-        copies[end].wait()
-        weight = good_weight(ends[end], scale).astype(jnp.bfloat16)
-        rows = slice((end + 1) * EDGE, (end + 2) * EDGE)
-        to_next[rows, :] = weight
-        to_previous[rows, :] = weight
-    copies[2].wait()
-    copies[3].wait()
-
-
-def weight_kernel(visit_weight, mask, weights, held, sems):
+    for copy in copies:
+        copy.wait()
+
+
+def weight_kernel(visit_weight, mask, weights, edges, held, sems):
     copies = []
     for part in range(4):
         rows = pl.ds(part * 32, 32)
@@ -178,15 +175,25 @@
         copies[part].wait()
         rows = slice(part * 32, part * 32 + 32)
         weights[rows, :] = good_weight(held[rows, :], scale).astype(jnp.bfloat16)
-
-
-def conv_kernel(tile, before, image, after, table, weights, flux, edges, stack):
+    edges[:EDGE, :] = weights[:EDGE, :]
+    edges[EDGE:, :] = weights[ROWS - EDGE :, :]
+
+
+def conv_kernel(tile, before, image, after, table, weights, flux, edges, stack, halo, sems):
     t = tile[0]
-    for group in range(10):
+    copies = [
+        pltpu.make_async_copy(before, halo.at[0], sems.at[0]),
+        pltpu.make_async_copy(after, halo.at[1], sems.at[1]),
+    ]
+    for copy in copies:
+        copy.start()
+    for group in (1, 2, 3, 4, 5, 6, 7, 8, 0, 9):
         if group == 0:
-            strip = jnp.where(t > 0, before[:EDGE, :].astype(jnp.float32), 0.0)
+            copies[0].wait()
+            strip = jnp.where(t > 0, halo[0].astype(jnp.float32), 0.0)
         elif group == 9:
-            strip = jnp.where(t < NTILE - 1, after[:EDGE, :].astype(jnp.float32), 0.0)
+            copies[1].wait()
+            strip = jnp.where(t < NTILE - 1, halo[1].astype(jnp.float32), 0.0)
         else:
             strip = image[(group - 1) * 16 : group * 16, :].astype(jnp.float32)
         strip = jnp.concatenate([strip, jnp.zeros((16, 128), jnp.float32)], axis=1)
@@ -217,19 +224,23 @@
     edges[EDGE:, :] = flux[ROWS - EDGE :, :]
 
 
-def warp_plane(t, own, far, after, before, row_warp, col_warp, cutout, rowed):
-    for block, edges in ((lax.rem(t + 1, NTILE), after), (lax.rem(t + 3, NTILE), before)):
-        start = pl.multiple_of(block * ROWS, ROWS)
-        cutout[pl.ds(start + EDGE, ROWS - 2 * EDGE), :] = jnp.zeros(
-            (ROWS - 2 * EDGE, WIDTH), jnp.bfloat16
-        )
-        cutout[pl.ds(start, EDGE), :] = edges[:EDGE, :]
-        cutout[pl.ds(start + ROWS - EDGE, EDGE), :] = edges[EDGE:, :]
-    cutout[pl.ds(pl.multiple_of(t * ROWS, ROWS), ROWS), :] = own[...]
-    cutout[pl.ds(pl.multiple_of(lax.rem(t + 2, NTILE) * ROWS, ROWS), ROWS), :] = far[...]
-    rowed[...] = jnp.dot(row_warp[...], cutout[...], preferred_element_type=jnp.float32).astype(
-        jnp.bfloat16
-    )
+def near_columns(t, row_warp):
+    def columns(block):
+        return row_warp[:, pl.ds(pl.multiple_of(lax.rem(block, NTILE) * ROWS, ROWS), ROWS)]
+
+    after, before = columns(t + 1), columns(t + 3)
+    last = ROWS - EDGE
+    parts = [columns(t + 2), after[:, :EDGE], after[:, last:], before[:, :EDGE], before[:, last:]]
+    return columns(t), jnp.concatenate(parts, axis=1)
+
+
+def gather_rest(rest, far, after, before):
+    rest[:ROWS, :] = far[...]
+    rest[ROWS : ROWS + 2 * EDGE, :] = after[...]
+    rest[ROWS + 2 * EDGE :, :] = before[...]
+
+
+def warp_columns(rowed, col_warp):
     for n in range(4):
         low, high = max(0, 256 * n - 128), min(WIDTH, 256 * n + 384)
         yield (
@@ -243,34 +254,40 @@
 
 
 def warp_weight_kernel(
-    tile, own, far, after, before, row_warp, col_warp, warped, cutout, rowed
+    tile, flux, own, far, after, before, row_warp, col_warp, warped, share, turn, rest, rowed
 ):
-    after, before = after.at[pl.ds(EDGE, 2 * EDGE)], before.at[pl.ds(EDGE, 2 * EDGE)]
-    for n, part in warp_plane(
-        tile[0], own, far, after, before, row_warp, col_warp, cutout, rowed
-    ):
+    near, turned = near_columns(tile[0], row_warp)
+    share[...] = jnp.dot(near, flux[...], preferred_element_type=jnp.float32)
+    turn[...] = turned
+    gather_rest(rest, far, after, before)
+    both = jnp.dot(near, own[...], preferred_element_type=jnp.float32) + jnp.dot(
+        turned, rest[...], preferred_element_type=jnp.float32
+    )
+    rowed[...] = both.astype(jnp.bfloat16)
+    for n, part in warp_columns(rowed, col_warp):
         warped[:, 256 * n : 256 * n + 256] = part
 
 
 def warp_flux_kernel(
-    tile,
     dest_slot,
-    own,
+    share,
+    turn,
     far,
     after,
     before,
-    row_warp,
     col_warp,
     warped_weight,
     notes,
     outgoing,
-    cutout,
+    rest,
     rowed,
 ):
+    gather_rest(rest, far, after, before)
+    rowed[...] = (
+        share[...] + jnp.dot(turn[...], rest[...], preferred_element_type=jnp.float32)
+    ).astype(jnp.bfloat16)
     outgoing[:, 64:, :] = notes[...]
-    for n, part in warp_plane(
-        tile[0], own, far, after, before, row_warp, col_warp, cutout, rowed
-    ):
+    for n, part in warp_columns(rowed, col_warp):
         for down in range(8):
             for c in range(2):
                 column = 2 * n + c
@@ -283,7 +300,7 @@
                 ]
 
 
-def patch_kernel(arriving, coadd, reply, sums, served, note, table, sem):
+def patch_kernel(arriving, coadd, reply, sums, values, served, note, table, sem, out_sem):
     notes = arriving[0, 64:, :].astype(jnp.float32)
     for sender in range(1, 64):
         notes = notes + arriving[sender, 64:, :].astype(jnp.float32)
@@ -303,8 +320,10 @@
     for block in range(NBLK):
         down, c = block // 8, block % 8
         value = sums[block, :16, :] / jnp.maximum(sums[block, 16:, :], FLOOR)
-        coadd[down * 16 : down * 16 + 16, c * 128 : c * 128 + 128] = value
+        values[down * 16 : down * 16 + 16, c * 128 : c * 128 + 128] = value
         served[block] = value.astype(jnp.bfloat16)
+    out = pltpu.make_async_copy(values, coadd, out_sem)
+    out.start()
 
     def serve(sender, _):
         for rank in range(2):
@@ -312,13 +331,25 @@
         return 0
 
     lax.fori_loop(0, 64, serve, 0, unroll=4)
-
-
-def difference_kernel(tmpl_slot, returned, new_science, difference):
-    for block in range(NBLK):
-        down, c = block // 8, block % 8
-        at = (slice(down * 16, down * 16 + 16), slice(c * 128, c * 128 + 128))
-        difference[at] = new_science[at] - returned[tmpl_slot[block]].astype(jnp.float32)
+    out.wait()
+
+
+def difference_kernel(tmpl_slot, returned, new_science, difference, held, sems):
+    copies = []
+    for down in range(8):
+        rows = slice(down * 16, down * 16 + 16)
+        for c in range(8):
+            columns = slice(c * 128, c * 128 + 128)
+            template = returned[tmpl_slot[down * 8 + c]].astype(jnp.float32)
+            held[rows, columns] = new_science[rows, columns] - template
+        if down % 2 == 1:
+            part = pl.ds(down * 16 - 16, 32)
+            copies.append(
+                pltpu.make_async_copy(held.at[part], difference.at[part], sems.at[down // 2])
+            )
+            copies[-1].start()
+    for copy in copies:
+        copy.wait()
 
 
 def per_device(
@@ -345,27 +376,29 @@
     across = [(i, (i + 2) % NTILE) for i in range(NTILE)]
 
     to_next, to_previous = call(
-        edge_kernel,
-        (struct((3 * EDGE, WIDTH), bf16),) * 2,
-        [SMEM, HBM, HBM],
+        halo_kernel,
+        (struct((EDGE, WIDTH), bf16),) * 2,
+        [HBM],
         (VMEM, VMEM),
-        [pltpu.VMEM((2, EDGE, WIDTH), i32), pltpu.SemaphoreType.DMA((4,))],
-        "edges",
+        [pltpu.SemaphoreType.DMA((2,))],
+        "halo",
+        1000,
         100_000,
-        400_000,
-    )(visit_weight, in_hbm(visit_image), in_hbm(mask_bits))
+    )(in_hbm(visit_image))
     before = lax.ppermute(to_next, "tile", up)
     after = lax.ppermute(to_previous, "tile", down)
-    weights = call(
+    weights, weight_edges = call(
         weight_kernel,
-        struct((ROWS, WIDTH), bf16),
+        (struct((ROWS, WIDTH), bf16), struct((2 * EDGE, WIDTH), bf16)),
         [SMEM, HBM],
-        VMEM,
+        (VMEM, VMEM),
         [pltpu.VMEM((ROWS, WIDTH), i32), pltpu.SemaphoreType.DMA((4,))],
         "weights",
         400_000,
         800_000,
     )(visit_weight, in_hbm(mask_bits))
+    before_weights = lax.ppermute(weight_edges, "tile", up)
+    after_weights = lax.ppermute(weight_edges, "tile", down)
     far_weights = lax.ppermute(weights, "tile", across)
 
     dest_slot, tmpl_slot, notes = call(
@@ -382,54 +415,67 @@
     taps = call(
         table_kernel,
         struct((2, 3 * BAND, DEPTH), bf16),
-        [SMEM, VMEM, VMEM, VMEM],
+        [SMEM, HBM, HBM, HBM],
         VMEM,
-        [pltpu.VMEM((128, NB), f32)],
+        [
+            pltpu.VMEM((128, NB), f32),
+            pltpu.VMEM((6, 1, NB), f32),
+            pltpu.VMEM((TAPS, NB), bf16),
+            pltpu.VMEM((TAPS, NB), bf16),
+            pltpu.SemaphoreType.DMA((3,)),
+        ],
         "taps",
         10_000_000,
         2_000_000,
-    )(tile, kernel_coef.transpose(2, 0, 1), basis_cols.T, basis_rows.T)
+    )(tile, in_hbm(kernel_coef.transpose(2, 0, 1)), in_hbm(basis_cols.T), in_hbm(basis_rows.T))
     flux, edges = call(
         conv_kernel,
         (struct((ROWS, WIDTH), bf16), struct((2 * EDGE, WIDTH), bf16)),
-        [SMEM] + [VMEM] * 5,
+        [SMEM, ANY, VMEM, ANY, VMEM, VMEM],
         (VMEM, VMEM),
-        [pltpu.VMEM((2, DEPTH, WIDTH), bf16)],
+        [
+            pltpu.VMEM((2, DEPTH, WIDTH), bf16),
+            pltpu.VMEM((2, EDGE, WIDTH), bf16),
+            pltpu.SemaphoreType.DMA((2,)),
+        ],
         "matching",
         2 * 2 * 192 * DEPTH * WIDTH,
         3_000_000,
-    )(tile, before, visit_image, after, taps, weights)
+    )(tile, before, visit_image, in_hbm(after), taps, weights)
+    flux, edges, before_weights, after_weights = lax.optimization_barrier(
+        (flux, edges, before_weights, after_weights)
+    )
     far_flux = lax.ppermute(flux, "tile", across)
     after_flux = lax.ppermute(edges, "tile", down)
     before_flux = lax.ppermute(edges, "tile", up)
-    scratch = [pltpu.VMEM((CUTOUT, WIDTH), bf16), pltpu.VMEM((ROWS, WIDTH), bf16)]
-    warped_weight = call(
+    reach = ROWS + 4 * EDGE
+    scratch = [pltpu.VMEM((reach, WIDTH), bf16), pltpu.VMEM((ROWS, WIDTH), bf16)]
+    warped_weight, share, turn = call(
         warp_weight_kernel,
-        struct((ROWS, WIDTH), bf16),
-        [SMEM] + [VMEM] * 6,
-        VMEM,
+        (struct((ROWS, WIDTH), bf16), struct((ROWS, WIDTH), f32), struct((ROWS, reach), bf16)),
+        [SMEM] + [VMEM] * 7,
+        (VMEM,) * 3,
         scratch,
         "warp_weight",
         2 * 128 * WIDTH * WIDTH,
         4_000_000,
-    )(tile, weights, far_weights, after, before, row_warp, col_warp[0])
+    )(tile, flux, weights, far_weights, after_weights, before_weights, row_warp, col_warp[0])
     outgoing = call(
         warp_flux_kernel,
         struct((64, MESSAGE, 128), bf16),
-        [SMEM, SMEM] + [VMEM] * 8,
+        [SMEM] + [VMEM] * 8,
         VMEM,
         scratch,
         "warp_flux",
         2 * 128 * WIDTH * WIDTH,
         5_000_000,
     )(
-        tile,
         dest_slot,
-        flux,
+        share,
+        turn,
         far_flux,
         after_flux,
         before_flux,
-        row_warp,
         col_warp[0],
         warped_weight,
         notes,
@@ -439,12 +485,14 @@
         patch_kernel,
         (struct((ROWS, WIDTH), f32), struct((SLOTS, 16, 128), bf16)),
         [VMEM],
-        (VMEM, VMEM),
+        (HBM, VMEM),
         [
             pltpu.VMEM((NBLK + 8, 32, 128), f32),
+            pltpu.VMEM((ROWS, WIDTH), f32),
             pltpu.VMEM((NBLK, 16, 128), bf16),
             pltpu.VMEM((NOTE, 128), i32),
             pltpu.SMEM((NOTE, 128), i32),
+            pltpu.SemaphoreType.DMA,
             pltpu.SemaphoreType.DMA,
         ],
         "patch",
@@ -456,8 +504,8 @@
         difference_kernel,
         struct((ROWS, WIDTH), f32),
         [SMEM, VMEM, VMEM],
-        VMEM,
-        [],
+        HBM,
+        [pltpu.VMEM((ROWS, WIDTH), f32), pltpu.SemaphoreType.DMA((4,))],
         "difference",
         1_000_000,
         2_000_000,

time: 97.5 us -> 99.7 us (1.023)
  starting transfers between devices: 8.25 us -> 11 us
  waiting for transfers between devices: 1.83 us -> 0.53 us
    ppermute x0 -> x2, starting transfers between devices: none -> 2.75 us  [the longest x1 2.66 us: per_device(): after_weights = lax.ppermute(weight_edges, 'tile', down)]
    ppermute x1, starting transfers between devices: 1.41 us -> 2.72 us  [per_device(): far_flux = lax.ppermute(flux, 'tile', across)]
    ppermute x1, starting transfers between devices: 1.64 us -> 0.34 us  [per_device(): far_weights = lax.ppermute(weights, 'tile', across)]
    ppermute x1, starting transfers between devices: 1.37 us -> 0.13 us  [per_device(): after_flux = lax.ppermute(edges, 'tile', down)]
    ppermute x1, starting transfers between devices: 0.09 us -> 1.34 us  [per_device(): before_flux = lax.ppermute(edges, 'tile', up)]
    ppermute x1, waiting for transfers between devices: 1.67 us -> 0.51 us  [per_device(): before_flux = lax.ppermute(edges, 'tile', up)]
    pallas_call x1, Pallas kernels: 3.53 us -> 4.53 us  [per_device(): call(conv_kernel, (struct((ROWS, WIDTH), bf16), struct((2 * EDGE, WIDTH),...]
  transfers between devices with their start and end apart: 6 -> 8, of which waited for: 2 -> 1; matrix products, arithmetic and copies ran while one was open for 0% -> 0% of each run, Pallas kernels for 9% -> 11%
where the time goes in v2:
time: 99.7 us; the launch traced here: 99.5 us
  blocking collectives  70.3 us (71%)
  Pallas kernels  16.1 us (16%)
  starting transfers between devices  11 us (11%)
  between operations  1.49 us (1%)
    all_to_all x1, blocking collectives, per_device(): lax.all_to_all(outgoing, 'ccd', split_axis=0, concat_axis=0, tiled=True)  46.1 us
    all_to_all x1, blocking collectives, per_device(): lax.all_to_all(reply, 'ccd', split_axis=0, concat_axis=0, tiled=True)  24.2 us
    pallas_call x1, Pallas kernels, per_device(): call(conv_kernel, (struct((ROWS, WIDTH), bf16), struct((2 * EDGE, WIDTH),...  4.53 us
    ppermute x1, starting transfers between devices, per_device(): far_flux = lax.ppermute(flux, 'tile', across)  2.72 us
    ppermute x1, starting transfers between devices, per_device(): after_weights = lax.ppermute(weight_edges, 'tile', down)  2.66 us
    ppermute x1, starting transfers between devices, per_device(): before = lax.ppermute(to_next, 'tile', up)  2.2 us
    pallas_call x1, Pallas kernels, per_device(): call(index_kernel, (struct((64,), i32), struct((64,), i32), struct((64, N...  2.16 us
    pallas_call x1, Pallas kernels, per_device(): call(table_kernel, struct((2, 3 * BAND, DEPTH), bf16), [SMEM, HBM, HBM, H...  2.15 us
  transfers between devices with their start and end apart: 8, of which 1 were waited for; matrix products, arithmetic and copies ran while one was open for 0% of the time, Pallas kernels for 11%

profile of v2, /device:TPU:1, one launch (start us, length us, event | category | flops | bytes accessed | tf_op | source)
XLA Modules:
  0.0 99.5 jit_solution(7356543442504638216)
XLA Ops:
  0.6 0.8 halo.1
  1.5 2.2 %collective-permute-start = (bf16[16,1024]{1,0:T(8,128)(2,1)S(1)}, bf16[16,1024]{1,0:T(8,128)(2,1)S(1)}, u32[]{:S(2)}, u32[]{:S(2)}) collective-permute-start(bf16[16,1024]{1,0:T(8,128)(2,1)S(1)} %get-tuple-element.21), channel_id=1, source_target_pairs={{0,1},{1,2},{2,3},{3,0},{4,5},{5,6},{6,7},{7,4},{8,9},{9,10},{10,1... | collective-permute-start | bytes 98312 | tf_op jit(solution)/shard_map/ppermute | solution.py:388
  3.7 1.5 %collective-permute-start.1 = (bf16[16,1024]{1,0:T(8,128)(2,1)S(1)}, bf16[16,1024]{1,0:T(8,128)(2,1)}, u32[]{:S(2)}, u32[]{:S(2)}) collective-permute-start(bf16[16,1024]{1,0:T(8,128)(2,1)S(1)} %get-tuple-element.22), channel_id=1, source_target_pairs={{0,3},{1,0},{2,1},{3,2},{4,7},{5,4},{6,5},{7,6},{8,11},{9,8},{10,9... | collective-permute-start | bytes 98312 | tf_op jit(solution)/shard_map/ppermute | solution.py:389
  5.9 1.2 %weights.1 = (bf16[128,1024]{1,0:T(8,128)(2,1)S(1)}, bf16[32,1024]{1,0:T(8,128)(2,1)S(1)}) custom-call(f32[1]{0:T(128)S(6)} %copy.15.visit_weight, s32[128,1024]{1,0:T(8,128)} %mask.1), custom_call_target="tpu_custom_call" | custom-call | flops 400000 | bytes 800000 | tf_op jit(solution)/shard_map/weights/pallas_call | solution.py:390
  7.0 0.1 collective-permute-start.2
  7.1 2.7 %collective-permute-start.3 = (bf16[32,1024]{1,0:T(8,128)(2,1)S(1)}, bf16[32,1024]{1,0:T(8,128)(2,1)S(1)}, u32[]{:S(2)}, u32[]{:S(2)}) collective-permute-start(bf16[32,1024]{1,0:T(8,128)(2,1)S(1)} %get-tuple-element.26), channel_id=1, source_target_pairs={{0,3},{1,0},{2,1},{3,2},{4,7},{5,4},{6,5},{7,6},{8,11},{9,8},{10,9... | collective-permute-start | bytes 196616 | tf_op jit(solution)/shard_map/ppermute | solution.py:401
  9.8 0.3 collective-permute-start.4
  10.1 2.1 %taps.1.table = bf16[2,192,2048]{2,1,0:T(8,128)(2,1)S(1)} custom-call(s32[1]{0:T(128)} %bitcast.3.tile, f32[6,1,31]{2,1,0:T(1,128)} %bitcast.14, bf16[21,31]{1,0:T(8,128)(2,1)} %bitcast.12, bf16[21,31]{1,0:T(8,128)(2,1)} %bitcast.13), custom_call_target="tpu_custom_call" | custom-call | flops 10000000 | bytes 2000000 | tf_op jit(solution)/shard_map/taps/pallas_call | solution.py:415
  12.3 0.0 copy-start.4
  12.3 0.0 copy-start.5
  12.3 0.0 copy-start.6
  12.3 0.0 copy-start.7
  12.3 0.0 copy-start
  12.4 0.0 copy-start.3
  12.4 0.0 collective-permute-done.before
  12.4 0.0 collective-permute-done.1.after
  12.4 4.5 %matching.1 = (bf16[128,1024]{1,0:T(8,128)(2,1)S(1)}, bf16[32,1024]{1,0:T(8,128)(2,1)}) custom-call(s32[1]{0:T(128)} %bitcast.3.tile, bf16[16,1024]{1,0:T(8,128)(2,1)S(1)} %collective-permute-done.before, bf16[128,1024]{1,0:T(8,128)(2,1)S(1)} %copy-done.2, bf16[16,1024]{1,0:T(8,128)(2,1)} %collective-permute-done.1.after, ...), custom_call_target="tpu_custom_call" | custom-call | flops 1610612736 | bytes 3000000 | tf_op jit(solution)/shard_map/matching/pallas_call | solution.py:431
  16.9 0.0 collective-permute-done.2.before
  17.0 2.7 %collective-permute-start.5 = (bf16[128,1024]{1,0:T(8,128)(2,1)S(1)}, bf16[128,1024]{1,0:T(8,128)(2,1)S(1)}, u32[]{:S(2)}, u32[]{:S(2)}) collective-permute-start(bf16[128,1024]{1,0:T(8,128)(2,1)S(1)} %get-tuple-element.27.flux), channel_id=1, source_target_pairs={{0,2},{1,3},{2,0},{3,1},{4,6},{5,7},{6,4},{7,5},{8,10},{9,11},{10,... | collective-permute-start | bytes 786440 | tf_op jit(solution)/shard_map/ppermute | solution.py:448
  19.7 0.1 collective-permute-start.6
  19.8 1.3 %collective-permute-start.7 = (bf16[32,1024]{1,0:T(8,128)(2,1)}, bf16[32,1024]{1,0:T(8,128)(2,1)S(1)}, u32[]{:S(2)}, u32[]{:S(2)}) collective-permute-start(bf16[32,1024]{1,0:T(8,128)(2,1)} %get-tuple-element.32), channel_id=1, source_target_pairs={{0,1},{1,2},{2,3},{3,0},{4,5},{5,6},{6,7},{7,4},{8,9},{9,10},{10,1... | collective-permute-start | bytes 196616 | tf_op jit(solution)/shard_map/ppermute | solution.py:450
  21.2 2.2 %slots.1 = (s32[64]{0:T(128)S(1)}, s32[64]{0:T(128)S(1)}, bf16[64,8,128]{2,1,0:T(8,128)(2,1)S(1)}) custom-call(s32[1]{0:T(128)} %bitcast.home, s32[64]{0:T(128)S(1)} %bitcast.10, s32[64]{0:T(128)S(1)} %copy-done.5, s32[64]{0:T(128)S(1)} %bitcast.11, s32[64]{0:T(128)S(1)} %copy-done.7), custom_call_target="tpu_custom_call" | custom-call | flops 2000000 | bytes 1000000 | tf_op jit(solution)/shard_map/slots/pallas_call | solution.py:404
  23.3 0.0 collective-permute-done.4.far
  23.4 0.6 warp_weight.1
  23.9 0.0 collective-permute-done.6.after
  24.0 0.5 collective-permute-done.7.before
  24.5 0.0 collective-permute-done.5.far
  24.5 1.2 %warp_flux.1 = bf16[64,72,128]{2,1,0:T(8,128)(2,1)S(1)} custom-call(s32[64]{0:T(128)S(1)} %get-tuple-element.20.dest_slot, f32[128,1024]{1,0:T(8,128)S(1)} %get-tuple-element.30.share, bf16[128,192]{1,0:T(8,128)(2,1)S(1)} %get-tuple-element.31.turn, bf16[128,1024]{1,0:T(8,128)(2,1)S(1)} %collective-permute-done.5.far, ...), custom_call_target="tpu_custom_call" | custom-call | flops 268435456 | bytes 5000000 | tf_op jit(solution)/shard_map/warp_flux/pallas_call | solution.py:463
  25.7 46.1 %all_to_all.10.arriving = bf16[64,72,128]{2,1,0:T(8,128)(2,1)S(1)} all-to-all(bf16[64,72,128]{2,1,0:T(8,128)(2,1)S(1)} %warp_flux.1), channel_id=1, replica_groups=mesh['ccd'=64,'tile'=4] {'ccd'}, dimensions={0} | all-to-all | bytes 2359296 | tf_op jit(solution)/shard_map/all_to_all | solution.py:483
  71.7 2.1 %patch.1 = (f32[128,1024]{1,0:T(8,128)}, bf16[128,16,128]{2,1,0:T(8,128)(2,1)S(1)}) custom-call(bf16[64,72,128]{2,1,0:T(8,128)(2,1)S(1)} %all_to_all.10.arriving), custom_call_target="tpu_custom_call" | custom-call | flops 1000000 | bytes 2000000 | tf_op jit(solution)/shard_map/patch/pallas_call | solution.py:484
  73.9 24.2 %all_to_all.11.returned = bf16[128,16,128]{2,1,0:T(8,128)(2,1)S(1)} all-to-all(bf16[128,16,128]{2,1,0:T(8,128)(2,1)S(1)} %get-tuple-element.37), channel_id=1, replica_groups=mesh['ccd'=64,'tile'=4] {'ccd'}, dimensions={0} | all-to-all | bytes 1048576 | tf_op jit(solution)/shard_map/all_to_all | solution.py:502
  98.1 1.4 %difference.1 = f32[128,1024]{1,0:T(8,128)} custom-call(s32[64]{0:T(128)S(1)} %get-tuple-element.36.tmpl_slot, bf16[128,16,128]{2,1,0:T(8,128)(2,1)S(1)} %all_to_all.11.returned, f32[128,1024]{1,0:T(8,128)S(1)} %copy-done.1), custom_call_target="tpu_custom_call" | custom-call | flops 1000000 | bytes 2000000 | tf_op jit(solution)/shard_map/difference/pallas_call | solution.py:503
  (11 shorter events, 0.0 us)
Async XLA Ops:
  0.6 11.8 %copy-start.2 = (bf16[128,1024]{1,0:T(8,128)(2,1)S(1)}, bf16[128,1024]{1,0:T(8,128)(2,1)}, u32[]{:S(2)}) copy-start(bf16[128,1024]{1,0:T(8,128)(2,1)} %image.3) | copy-start | bytes 786436
  1.5 10.9 %collective-permute-start = (bf16[16,1024]{1,0:T(8,128)(2,1)S(1)}, bf16[16,1024]{1,0:T(8,128)(2,1)S(1)}, u32[]{:S(2)}, u32[]{:S(2)}) collective-permute-start(bf16[16,1024]{1,0:T(8,128)(2,1)S(1)} %get-tuple-element.21), channel_id=1, source_target_pairs={{0,1},{1,2},{2,3},{3,0},{4,5},{5,6},{6,7},{7,4},{8,9},{9,10},{10,1... | collective-permute-start | bytes 98312 | tf_op jit(solution)/shard_map/ppermute | solution.py:388
  3.7 8.7 %collective-permute-start.1 = (bf16[16,1024]{1,0:T(8,128)(2,1)S(1)}, bf16[16,1024]{1,0:T(8,128)(2,1)}, u32[]{:S(2)}, u32[]{:S(2)}) collective-permute-start(bf16[16,1024]{1,0:T(8,128)(2,1)S(1)} %get-tuple-element.22), channel_id=1, source_target_pairs={{0,3},{1,0},{2,1},{3,2},{4,7},{5,4},{6,5},{7,6},{8,11},{9,8},{10,9... | collective-permute-start | bytes 98312 | tf_op jit(solution)/shard_map/ppermute | solution.py:389
  7.0 9.9 %collective-permute-start.2 = (bf16[32,1024]{1,0:T(8,128)(2,1)S(1)}, bf16[32,1024]{1,0:T(8,128)(2,1)S(1)}, u32[]{:S(2)}, u32[]{:S(2)}) collective-permute-start(bf16[32,1024]{1,0:T(8,128)(2,1)S(1)} %get-tuple-element.26), channel_id=1, source_target_pairs={{0,1},{1,2},{2,3},{3,0},{4,5},{5,6},{6,7},{7,4},{8,9},{9,10},{10,1... | collective-permute-start | bytes 196616 | tf_op jit(solution)/shard_map/ppermute | solution.py:400
  7.1 9.8 %collective-permute-start.3 = (bf16[32,1024]{1,0:T(8,128)(2,1)S(1)}, bf16[32,1024]{1,0:T(8,128)(2,1)S(1)}, u32[]{:S(2)}, u32[]{:S(2)}) collective-permute-start(bf16[32,1024]{1,0:T(8,128)(2,1)S(1)} %get-tuple-element.26), channel_id=1, source_target_pairs={{0,3},{1,0},{2,1},{3,2},{4,7},{5,4},{6,5},{7,6},{8,11},{9,8},{10,9... | collective-permute-start | bytes 196616 | tf_op jit(solution)/shard_map/ppermute | solution.py:401
  9.8 13.5 %collective-permute-start.4 = (bf16[128,1024]{1,0:T(8,128)(2,1)S(1)}, bf16[128,1024]{1,0:T(8,128)(2,1)S(1)}, u32[]{:S(2)}, u32[]{:S(2)}) collective-permute-start(bf16[128,1024]{1,0:T(8,128)(2,1)S(1)} %get-tuple-element.23.weights.own), channel_id=1, source_target_pairs={{0,2},{1,3},{2,0},{3,1},{4,6},{5,7},{6,4},{7,5},{8,10},{9,11},{10,... | collective-permute-start | bytes 786440 | tf_op jit(solution)/shard_map/ppermute | solution.py:402
  12.3 8.9 %copy-start.4 = (s32[64,1]{0,1:T(1,128)S(1)}, s32[64,1]{0,1:T(1,128)}, u32[]{:S(2)}) copy-start(s32[64,1]{0,1:T(1,128)} %param.21) | copy-start | bytes 772
  12.3 8.8 %copy-start.5 = (s32[64]{0:T(128)S(1)}, s32[64]{0:T(128)}, u32[]{:S(2)}) copy-start(s32[64]{0:T(128)} %dest_block.1) | copy-start | bytes 772
  12.3 8.8 %copy-start.6 = (s32[64,1]{0,1:T(1,128)S(1)}, s32[64,1]{0,1:T(1,128)}, u32[]{:S(2)}) copy-start(s32[64,1]{0,1:T(1,128)} %param.24) | copy-start | bytes 772
  12.3 8.8 %copy-start.7 = (s32[64]{0:T(128)S(1)}, s32[64]{0:T(128)}, u32[]{:S(2)}) copy-start(s32[64]{0:T(128)} %tmpl_block.1) | copy-start | bytes 772
  12.3 11.0 %copy-start = (bf16[1,1024,1024]{2,1,0:T(8,128)(2,1)S(1)}, bf16[1,1024,1024]{2,1,0:T(8,128)(2,1)}, u32[]{:S(2)}) copy-start(bf16[1,1024,1024]{2,1,0:T(8,128)(2,1)} %param.20) | copy-start | bytes 6291460
  12.4 11.0 %copy-start.3 = (bf16[128,512]{1,0:T(8,128)(2,1)S(1)}, bf16[128,512]{1,0:T(8,128)(2,1)}, u32[]{:S(2)}) copy-start(bf16[128,512]{1,0:T(8,128)(2,1)} %row_warp.1) | copy-start | bytes 393220
  17.0 7.5 %collective-permute-start.5 = (bf16[128,1024]{1,0:T(8,128)(2,1)S(1)}, bf16[128,1024]{1,0:T(8,128)(2,1)S(1)}, u32[]{:S(2)}, u32[]{:S(2)}) collective-permute-start(bf16[128,1024]{1,0:T(8,128)(2,1)S(1)} %get-tuple-element.27.flux), channel_id=1, source_target_pairs={{0,2},{1,3},{2,0},{3,1},{4,6},{5,7},{6,4},{7,5},{8,10},{9,11},{10,... | collective-permute-start | bytes 786440 | tf_op jit(solution)/shard_map/ppermute | solution.py:448
  19.7 4.3 %collective-permute-start.6 = (bf16[32,1024]{1,0:T(8,128)(2,1)}, bf16[32,1024]{1,0:T(8,128)(2,1)S(1)}, u32[]{:S(2)}, u32[]{:S(2)}) collective-permute-start(bf16[32,1024]{1,0:T(8,128)(2,1)} %get-tuple-element.32), channel_id=1, source_target_pairs={{0,3},{1,0},{2,1},{3,2},{4,7},{5,4},{6,5},{7,6},{8,11},{9,8},{10,9... | collective-permute-start | bytes 196616 | tf_op jit(solution)/shard_map/ppermute | solution.py:449
  19.8 4.7 %collective-permute-start.7 = (bf16[32,1024]{1,0:T(8,128)(2,1)}, bf16[32,1024]{1,0:T(8,128)(2,1)S(1)}, u32[]{:S(2)}, u32[]{:S(2)}) collective-permute-start(bf16[32,1024]{1,0:T(8,128)(2,1)} %get-tuple-element.32), channel_id=1, source_target_pairs={{0,1},{1,2},{2,3},{3,0},{4,5},{5,6},{6,7},{7,4},{8,9},{9,10},{10,1... | collective-permute-start | bytes 196616 | tf_op jit(solution)/shard_map/ppermute | solution.py:450
  71.7 26.3 %copy-start.1 = (f32[128,1024]{1,0:T(8,128)S(1)}, f32[128,1024]{1,0:T(8,128)}, u32[]{:S(2)}) copy-start(f32[128,1024]{1,0:T(8,128)} %new_science.1) | copy-start | bytes 1572868

commit v3 on v2

--- a/solution.py
+++ b/solution.py
@@ -29,7 +29,6 @@
 MESSAGE = 64 + NOTE
 
 VMEM = pl.BlockSpec(memory_space=pltpu.VMEM)
-ANY = pl.BlockSpec(memory_space=pl.ANY)
 HBM = pl.BlockSpec(memory_space=pltpu.HBM)
 SMEM = pl.BlockSpec(memory_space=pltpu.SMEM)
 
@@ -100,14 +99,8 @@
         notes[patch] = note.astype(jnp.float32).astype(jnp.bfloat16)
 
 
-def table_kernel(tile, coef_in, cols_in, rows_in, table, wide, coef, cols_t, rows_t, sems):
-    copies = []
-    for source, held in ((coef_in, coef), (cols_in, cols_t), (rows_in, rows_t)):
-        copies.append(pltpu.make_async_copy(source, held, sems.at[len(copies)]))
-        copies[-1].start()
+def table_kernel(tile, coef, cols_t, rows_t, table, wide):
     wide[...] = jnp.zeros_like(wide)
-    for copy in copies:
-        copy.wait()
     wide[6 : 6 + TAPS, :] = cols_t[...].astype(jnp.float32)
     taps = []
     for p in range(6):
@@ -149,51 +142,48 @@
             held = {i: held[i] for i in held if i > left}
 
 
-def good_weight(mask, scale):
-    return jnp.where(jnp.bitwise_and(mask, 3) == 3, 0.0, scale)
-
-
-def halo_kernel(image, to_next, to_previous, sems):
-    copies = [
-        pltpu.make_async_copy(image.at[pl.ds(ROWS - EDGE, EDGE)], to_next, sems.at[0]),
-        pltpu.make_async_copy(image.at[pl.ds(0, EDGE)], to_previous, sems.at[1]),
-    ]
+def edge_kernel(
+    image, mask, coef, cols, rows, to_next, to_previous, good, coef_near, cols_near, rows_near, held, sems
+):
+    last = ROWS - EDGE
+    copies = []
+    parts = [(0, EDGE), (last, EDGE)] + [(EDGE + 32 * part, 32) for part in range(3)]
+    for first, count in parts[:2]:
+        span = pl.ds(first, count)
+        copies.append(pltpu.make_async_copy(mask.at[span], held.at[span], sems.at[len(copies)]))
+    copies.append(
+        pltpu.make_async_copy(image.at[pl.ds(last, EDGE)], to_next.at[pl.ds(0, EDGE)], sems.at[2])
+    )
+    copies.append(
+        pltpu.make_async_copy(image.at[pl.ds(0, EDGE)], to_previous.at[pl.ds(0, EDGE)], sems.at[3])
+    )
+    for first, count in parts[2:]:
+        span = pl.ds(first, count)
+        copies.append(pltpu.make_async_copy(mask.at[span], held.at[span], sems.at[len(copies)]))
+    for source, near in ((coef, coef_near), (cols, cols_near), (rows, rows_near)):
+        copies.append(pltpu.make_async_copy(source, near, sems.at[len(copies)]))
     for copy in copies:
         copy.start()
-    for copy in copies:
+    for (first, count), copy in zip(parts, copies[:2] + copies[4:7]):
         copy.wait()
-
-
-def weight_kernel(visit_weight, mask, weights, edges, held, sems):
-    copies = []
-    for part in range(4):
-        rows = pl.ds(part * 32, 32)
-        copies.append(pltpu.make_async_copy(mask.at[rows], held.at[rows], sems.at[part]))
-        copies[part].start()
-    scale = visit_weight[0].astype(jnp.bfloat16).astype(jnp.float32)
-    for part in range(4):
-        copies[part].wait()
-        rows = slice(part * 32, part * 32 + 32)
-        weights[rows, :] = good_weight(held[rows, :], scale).astype(jnp.bfloat16)
-    edges[:EDGE, :] = weights[:EDGE, :]
-    edges[EDGE:, :] = weights[ROWS - EDGE :, :]
-
-
-def conv_kernel(tile, before, image, after, table, weights, flux, edges, stack, halo, sems):
+        span = slice(first, first + count)
+        flags = jnp.where(jnp.bitwise_and(held[span, :], 3) == 3, 0.0, 1.0).astype(jnp.bfloat16)
+        good[span, :] = flags
+        if count == EDGE:
+            at = slice(EDGE, 2 * EDGE) if first == 0 else slice(2 * EDGE, 3 * EDGE)
+            to_next[at, :] = flags
+            to_previous[at, :] = flags
+    for copy in copies[2:4] + copies[7:]:
+        copy.wait()
+
+
+def conv_kernel(tile, visit_weight, before, image, after, table, good, flux, edges, stack):
     t = tile[0]
-    copies = [
-        pltpu.make_async_copy(before, halo.at[0], sems.at[0]),
-        pltpu.make_async_copy(after, halo.at[1], sems.at[1]),
-    ]
-    for copy in copies:
-        copy.start()
-    for group in (1, 2, 3, 4, 5, 6, 7, 8, 0, 9):
+    for group in range(10):
         if group == 0:
-            copies[0].wait()
-            strip = jnp.where(t > 0, halo[0].astype(jnp.float32), 0.0)
+            strip = jnp.where(t > 0, before[:EDGE, :].astype(jnp.float32), 0.0)
         elif group == 9:
-            copies[1].wait()
-            strip = jnp.where(t < NTILE - 1, halo[1].astype(jnp.float32), 0.0)
+            strip = jnp.where(t < NTILE - 1, after[:EDGE, :].astype(jnp.float32), 0.0)
         else:
             strip = image[(group - 1) * 16 : group * 16, :].astype(jnp.float32)
         strip = jnp.concatenate([strip, jnp.zeros((16, 128), jnp.float32)], axis=1)
@@ -207,6 +197,7 @@
                 at = i * WINDOW + group * 16 - BAND
                 stack[1, at : at + 16, :] = moved
     stack[:, USED:, :] = jnp.zeros((2, DEPTH - USED, WIDTH), jnp.bfloat16)
+    scale = visit_weight[0].astype(jnp.bfloat16).astype(jnp.float32)
     for band in range(2):
         rows = slice(band * BAND, (band + 1) * BAND)
         for n in range(4):
@@ -217,9 +208,8 @@
             x = lax.broadcasted_iota(jnp.int32, (BAND, 256), 1) + n * 256
             xn = (2.0 * x.astype(jnp.float32) + 1.0) / WIDTH - 1.0
             conv = parts[:BAND] + xn * (parts[BAND : 2 * BAND] + xn * parts[2 * BAND :])
-            flux[rows, columns] = (weights[rows, columns].astype(jnp.float32) * conv).astype(
-                jnp.bfloat16
-            )
+            weight = scale * good[rows, columns].astype(jnp.float32)
+            flux[rows, columns] = (weight * conv).astype(jnp.bfloat16)
     edges[:EDGE, :] = flux[:EDGE, :]
     edges[EDGE:, :] = flux[ROWS - EDGE :, :]
 
@@ -254,16 +244,30 @@
 
 
 def warp_weight_kernel(
-    tile, flux, own, far, after, before, row_warp, col_warp, warped, share, turn, rest, rowed
+    tile,
+    visit_weight,
+    flux,
+    own,
+    far,
+    after,
+    before,
+    row_warp,
+    col_warp,
+    warped,
+    share,
+    turn,
+    rest,
+    rowed,
 ):
     near, turned = near_columns(tile[0], row_warp)
     share[...] = jnp.dot(near, flux[...], preferred_element_type=jnp.float32)
     turn[...] = turned
-    gather_rest(rest, far, after, before)
+    gather_rest(rest, far, after.at[pl.ds(EDGE, 2 * EDGE)], before.at[pl.ds(EDGE, 2 * EDGE)])
     both = jnp.dot(near, own[...], preferred_element_type=jnp.float32) + jnp.dot(
         turned, rest[...], preferred_element_type=jnp.float32
     )
-    rowed[...] = both.astype(jnp.bfloat16)
+    scale = visit_weight[0].astype(jnp.bfloat16).astype(jnp.float32)
+    rowed[...] = (scale * both).astype(jnp.bfloat16)
     for n, part in warp_columns(rowed, col_warp):
         warped[:, 256 * n : 256 * n + 256] = part
 
@@ -375,31 +379,32 @@
     down = [(i, (i + 3) % NTILE) for i in range(NTILE)]
     across = [(i, (i + 2) % NTILE) for i in range(NTILE)]
 
-    to_next, to_previous = call(
-        halo_kernel,
-        (struct((EDGE, WIDTH), bf16),) * 2,
-        [HBM],
-        (VMEM, VMEM),
-        [pltpu.SemaphoreType.DMA((2,))],
-        "halo",
-        1000,
-        100_000,
-    )(in_hbm(visit_image))
+    to_next, to_previous, good, coef, cols_t, rows_t = call(
+        edge_kernel,
+        (
+            struct((3 * EDGE, WIDTH), bf16),
+            struct((3 * EDGE, WIDTH), bf16),
+            struct((ROWS, WIDTH), bf16),
+            struct((6, 1, NB), f32),
+            struct((TAPS, NB), bf16),
+            struct((TAPS, NB), bf16),
+        ),
+        [HBM] * 5,
+        (VMEM,) * 6,
+        [pltpu.VMEM((ROWS, WIDTH), i32), pltpu.SemaphoreType.DMA((10,))],
+        "edges",
+        400_000,
+        1_000_000,
+    )(
+        in_hbm(visit_image),
+        in_hbm(mask_bits),
+        in_hbm(kernel_coef.transpose(2, 0, 1)),
+        in_hbm(basis_cols.T),
+        in_hbm(basis_rows.T),
+    )
     before = lax.ppermute(to_next, "tile", up)
     after = lax.ppermute(to_previous, "tile", down)
-    weights, weight_edges = call(
-        weight_kernel,
-        (struct((ROWS, WIDTH), bf16), struct((2 * EDGE, WIDTH), bf16)),
-        [SMEM, HBM],
-        (VMEM, VMEM),
-        [pltpu.VMEM((ROWS, WIDTH), i32), pltpu.SemaphoreType.DMA((4,))],
-        "weights",
-        400_000,
-        800_000,
-    )(visit_weight, in_hbm(mask_bits))
-    before_weights = lax.ppermute(weight_edges, "tile", up)
-    after_weights = lax.ppermute(weight_edges, "tile", down)
-    far_weights = lax.ppermute(weights, "tile", across)
+    far_good = lax.ppermute(good, "tile", across)
 
     dest_slot, tmpl_slot, notes = call(
         index_kernel,
@@ -415,36 +420,23 @@
     taps = call(
         table_kernel,
         struct((2, 3 * BAND, DEPTH), bf16),
-        [SMEM, HBM, HBM, HBM],
+        [SMEM, VMEM, VMEM, VMEM],
         VMEM,
-        [
-            pltpu.VMEM((128, NB), f32),
-            pltpu.VMEM((6, 1, NB), f32),
-            pltpu.VMEM((TAPS, NB), bf16),
-            pltpu.VMEM((TAPS, NB), bf16),
-            pltpu.SemaphoreType.DMA((3,)),
-        ],
+        [pltpu.VMEM((128, NB), f32)],
         "taps",
         10_000_000,
         2_000_000,
-    )(tile, in_hbm(kernel_coef.transpose(2, 0, 1)), in_hbm(basis_cols.T), in_hbm(basis_rows.T))
+    )(tile, coef, cols_t, rows_t)
     flux, edges = call(
         conv_kernel,
         (struct((ROWS, WIDTH), bf16), struct((2 * EDGE, WIDTH), bf16)),
-        [SMEM, ANY, VMEM, ANY, VMEM, VMEM],
+        [SMEM, SMEM] + [VMEM] * 5,
         (VMEM, VMEM),
-        [
-            pltpu.VMEM((2, DEPTH, WIDTH), bf16),
-            pltpu.VMEM((2, EDGE, WIDTH), bf16),
-            pltpu.SemaphoreType.DMA((2,)),
-        ],
+        [pltpu.VMEM((2, DEPTH, WIDTH), bf16)],
         "matching",
         2 * 2 * 192 * DEPTH * WIDTH,
         3_000_000,
-    )(tile, before, visit_image, in_hbm(after), taps, weights)
-    flux, edges, before_weights, after_weights = lax.optimization_barrier(
-        (flux, edges, before_weights, after_weights)
-    )
+    )(tile, visit_weight, before, visit_image, after, taps, good)
     far_flux = lax.ppermute(flux, "tile", across)
     after_flux = lax.ppermute(edges, "tile", down)
     before_flux = lax.ppermute(edges, "tile", up)
@@ -453,13 +445,13 @@
     warped_weight, share, turn = call(
         warp_weight_kernel,
         (struct((ROWS, WIDTH), bf16), struct((ROWS, WIDTH), f32), struct((ROWS, reach), bf16)),
-        [SMEM] + [VMEM] * 7,
+        [SMEM, SMEM] + [VMEM] * 7,
         (VMEM,) * 3,
         scratch,
         "warp_weight",
         2 * 128 * WIDTH * WIDTH,
         4_000_000,
-    )(tile, flux, weights, far_weights, after_weights, before_weights, row_warp, col_warp[0])
+    )(tile, visit_weight, flux, good, far_good, after, before, row_warp, col_warp[0])
     outgoing = call(
         warp_flux_kernel,
         struct((64, MESSAGE, 128), bf16),

time: 99.7 us -> 99 us (level)
  blocking collectives: 70.3 us -> 73.2 us
  starting transfers between devices: 11 us -> 8.15 us
  Pallas kernels: 16.1 us -> 14 us
  waiting for transfers between devices: 0.53 us -> 1.88 us
    all_to_all x1, blocking collectives: 46.1 us -> 49.1 us  [per_device(): lax.all_to_all(outgoing, 'ccd', split_axis=0, concat_axis=0, tiled=True)]
    ppermute x3 -> x1, starting transfers between devices: 3.09 us -> 1.56 us  [per_device(): far_good = lax.ppermute(good, 'tile', across)]
    pallas_call x3 -> x2, Pallas kernels: 4.14 us -> 2.68 us  [the longest x1 1.4 us: per_device(): call(table_kernel, struct((2, 3 * BAND, DEPTH), bf16), [SMEM, VMEM, VMEM,...]
    ppermute x1, starting transfers between devices: 2.72 us -> 1.4 us  [per_device(): far_flux = lax.ppermute(flux, 'tile', across)]
    ppermute x1, starting transfers between devices: 0.13 us -> 1.39 us  [per_device(): after_flux = lax.ppermute(edges, 'tile', down)]
    ppermute x1, starting transfers between devices: 1.34 us -> 0.08 us  [per_device(): before_flux = lax.ppermute(edges, 'tile', up)]
    ppermute x1, waiting for transfers between devices: 0.51 us -> 1.55 us  [per_device(): before_flux = lax.ppermute(edges, 'tile', up)]
    pallas_call x1, Pallas kernels: 4.53 us -> 3.53 us  [per_device(): call(conv_kernel, (struct((ROWS, WIDTH), bf16), struct((2 * EDGE, WIDTH),...]
  transfers between devices with their start and end apart: 8 -> 6, of which waited for: 1 -> 2; matrix products, arithmetic and copies ran while one was open for 0% -> 0% of each run, Pallas kernels for 11% -> 8%
where the time goes in v3:
time: 99 us; the launch traced here: 98.7 us
  blocking collectives  73.2 us (74%)
  Pallas kernels  14 us (14%)
  starting transfers between devices  8.15 us (8%)
  waiting for transfers between devices  1.88 us (2%)
  between operations  1.44 us (1%)
    all_to_all x1, blocking collectives, per_device(): lax.all_to_all(outgoing, 'ccd', split_axis=0, concat_axis=0, tiled=True)  49.1 us
    all_to_all x1, blocking collectives, per_device(): lax.all_to_all(reply, 'ccd', split_axis=0, concat_axis=0, tiled=True)  24.1 us
    pallas_call x1, Pallas kernels, per_device(): call(conv_kernel, (struct((ROWS, WIDTH), bf16), struct((2 * EDGE, WIDTH),...  3.53 us
    ppermute x1, starting transfers between devices, per_device(): before = lax.ppermute(to_next, 'tile', up)  2.2 us
    pallas_call x1, Pallas kernels, per_device(): call(patch_kernel, (struct((ROWS, WIDTH), f32), struct((SLOTS, 16, 128),...  2.18 us
    pallas_call x1, Pallas kernels, per_device(): call(index_kernel, (struct((64,), i32), struct((64,), i32), struct((64, N...  2.16 us
  transfers between devices with their start and end apart: 6, of which 2 were waited for; matrix products, arithmetic and copies ran while one was open for 0% of the time, Pallas kernels for 8%

profile of v3, /device:TPU:1, one launch (start us, length us, event | category | flops | bytes accessed | tf_op | source)
XLA Modules:
  0.0 98.7 jit_solution(5674065444773541840)
XLA Ops:
  0.6 0.0 copy-start.2
  0.6 1.3 %edges.1 = (bf16[48,1024]{1,0:T(8,128)(2,1)S(1)}, bf16[48,1024]{1,0:T(8,128)(2,1)S(1)}, bf16[128,1024]{1,0:T(8,128)(2,1)S(1)}, f32[6,1,31]{2,1,0:T(1,128)S(1)}, ...) custom-call(bf16[128,1024]{1,0:T(8,128)(2,1)} %image.3, s32[128,1024]{1,0:T(8,128)} %mask.1, f32[6,1,31]{2,1,0:T(1,128)} %bitcast.14, ...), custom_call_target="tpu_custom_call" | custom-call | flops 400000 | bytes 1000000 | tf_op jit(solution)/shard_map/edges/pallas_call | solution.py:382
  1.9 2.2 %collective-permute-start = (bf16[48,1024]{1,0:T(8,128)(2,1)S(1)}, bf16[48,1024]{1,0:T(8,128)(2,1)S(1)}, u32[]{:S(2)}, u32[]{:S(2)}) collective-permute-start(bf16[48,1024]{1,0:T(8,128)(2,1)S(1)} %get-tuple-element.19), channel_id=1, source_target_pairs={{0,1},{1,2},{2,3},{3,0},{4,5},{5,6},{6,7},{7,4},{8,9},{9,10},{10,1... | collective-permute-start | bytes 294920 | tf_op jit(solution)/shard_map/ppermute | solution.py:405
  4.1 1.5 %collective-permute-start.1 = (bf16[48,1024]{1,0:T(8,128)(2,1)S(1)}, bf16[48,1024]{1,0:T(8,128)(2,1)S(1)}, u32[]{:S(2)}, u32[]{:S(2)}) collective-permute-start(bf16[48,1024]{1,0:T(8,128)(2,1)S(1)} %get-tuple-element.20), channel_id=1, source_target_pairs={{0,3},{1,0},{2,1},{3,2},{4,7},{5,4},{6,5},{7,6},{8,11},{9,8},{10,9... | collective-permute-start | bytes 294920 | tf_op jit(solution)/shard_map/ppermute | solution.py:406
  5.7 1.6 %collective-permute-start.2 = (bf16[128,1024]{1,0:T(8,128)(2,1)S(1)}, bf16[128,1024]{1,0:T(8,128)(2,1)S(1)}, u32[]{:S(2)}, u32[]{:S(2)}) collective-permute-start(bf16[128,1024]{1,0:T(8,128)(2,1)S(1)} %get-tuple-element.24.good.own), channel_id=1, source_target_pairs={{0,2},{1,3},{2,0},{3,1},{4,6},{5,7},{6,4},{7,5},{8,10},{9,11},{10,... | collective-permute-start | bytes 786440 | tf_op jit(solution)/shard_map/ppermute | solution.py:407
  7.9 1.4 %taps.1.table = bf16[2,192,2048]{2,1,0:T(8,128)(2,1)S(1)} custom-call(s32[1]{0:T(128)} %bitcast.3.tile, f32[6,1,31]{2,1,0:T(1,128)S(1)} %get-tuple-element.21.coef, bf16[21,31]{1,0:T(8,128)(2,1)S(1)} %get-tuple-element.22.cols_t, bf16[21,31]{1,0:T(8,128)(2,1)S(1)} %get-tuple-element.23.rows_t), custom_call_target="tpu_custom_call" | custom-call | flops 10000000 | bytes 2000000 | tf_op jit(solution)/shard_map/taps/pallas_call | solution.py:420
  9.3 0.0 copy-start.4
  9.3 0.0 copy-start.5
  9.3 0.0 copy-start.6
  9.3 0.0 copy-start.7
  9.3 0.0 copy-start
  9.3 0.0 copy-start.3
  9.3 0.0 collective-permute-done.before
  9.4 0.0 collective-permute-done.1.after
  9.4 3.5 %matching.1 = (bf16[128,1024]{1,0:T(8,128)(2,1)S(1)}, bf16[32,1024]{1,0:T(8,128)(2,1)}) custom-call(s32[1]{0:T(128)} %bitcast.3.tile, f32[1]{0:T(128)S(6)} %copy.15.visit_weight, bf16[48,1024]{1,0:T(8,128)(2,1)S(1)} %collective-permute-done.before, bf16[128,1024]{1,0:T(8,128)(2,1)S(1)} %copy-done.2, bf16[48,1024]{1,0:T(8,128)(2,1)S(1)} %collective-permute-done.1.after, ...), custom_call_target="tpu_custom_call" | custom-call | flops 1610612736 | bytes 3000000 | tf_op jit(solution)/shard_map/matching/pallas_call | solution.py:430
  12.9 1.4 %collective-permute-start.3 = (bf16[128,1024]{1,0:T(8,128)(2,1)S(1)}, bf16[128,1024]{1,0:T(8,128)(2,1)S(1)}, u32[]{:S(2)}, u32[]{:S(2)}) collective-permute-start(bf16[128,1024]{1,0:T(8,128)(2,1)S(1)} %get-tuple-element.25.flux), channel_id=1, source_target_pairs={{0,2},{1,3},{2,0},{3,1},{4,6},{5,7},{6,4},{7,5},{8,10},{9,11},{10,... | collective-permute-start | bytes 786440 | tf_op jit(solution)/shard_map/ppermute | solution.py:440
  14.3 1.4 %collective-permute-start.4 = (bf16[32,1024]{1,0:T(8,128)(2,1)}, bf16[32,1024]{1,0:T(8,128)(2,1)S(1)}, u32[]{:S(2)}, u32[]{:S(2)}) collective-permute-start(bf16[32,1024]{1,0:T(8,128)(2,1)} %get-tuple-element.28), channel_id=1, source_target_pairs={{0,3},{1,0},{2,1},{3,2},{4,7},{5,4},{6,5},{7,6},{8,11},{9,8},{10,9... | collective-permute-start | bytes 196616 | tf_op jit(solution)/shard_map/ppermute | solution.py:441
  15.7 0.1 collective-permute-start.5
  15.8 2.2 %slots.1 = (s32[64]{0:T(128)S(1)}, s32[64]{0:T(128)S(1)}, bf16[64,8,128]{2,1,0:T(8,128)(2,1)S(1)}) custom-call(s32[1]{0:T(128)} %bitcast.home, s32[64]{0:T(128)S(1)} %bitcast.10, s32[64]{0:T(128)S(1)} %copy-done.5, s32[64]{0:T(128)S(1)} %bitcast.11, s32[64]{0:T(128)S(1)} %copy-done.7), custom_call_target="tpu_custom_call" | custom-call | flops 2000000 | bytes 1000000 | tf_op jit(solution)/shard_map/slots/pallas_call | solution.py:409
  18.0 0.0 collective-permute-done.2.far
  18.0 0.0 copy-done
  18.0 0.0 copy-done.3
  18.0 0.6 warp_weight.1
  18.6 0.3 collective-permute-done.4.after
  18.9 1.6 %collective-permute-done.5.before = bf16[32,1024]{1,0:T(8,128)(2,1)} collective-permute-done((bf16[32,1024]{1,0:T(8,128)(2,1)}, bf16[32,1024]{1,0:T(8,128)(2,1)}, u32[]{:S(2)}, u32[]{:S(2)}) %collective-permute-start.5) | collective-permute-done | bytes 65568 | tf_op jit(solution)/shard_map/ppermute | solution.py:442
  20.4 0.0 collective-permute-done.3.far
  20.4 1.5 %warp_flux.1 = bf16[64,72,128]{2,1,0:T(8,128)(2,1)S(1)} custom-call(s32[64]{0:T(128)S(1)} %get-tuple-element.18.dest_slot, f32[128,1024]{1,0:T(8,128)S(1)} %get-tuple-element.26.share, bf16[128,192]{1,0:T(8,128)(2,1)S(1)} %get-tuple-element.27.turn, bf16[128,1024]{1,0:T(8,128)(2,1)S(1)} %collective-permute-done.3.far, ...), custom_call_target="tpu_custom_call" | custom-call | flops 268435456 | bytes 5000000 | tf_op jit(solution)/shard_map/warp_flux/pallas_call | solution.py:455
  21.9 49.1 %all_to_all.10.arriving = bf16[64,72,128]{2,1,0:T(8,128)(2,1)S(1)} all-to-all(bf16[64,72,128]{2,1,0:T(8,128)(2,1)S(1)} %warp_flux.1), channel_id=1, replica_groups=mesh['ccd'=64,'tile'=4] {'ccd'}, dimensions={0} | all-to-all | bytes 2359296 | tf_op jit(solution)/shard_map/all_to_all | solution.py:475
  71.0 2.2 %patch.1 = (f32[128,1024]{1,0:T(8,128)}, bf16[128,16,128]{2,1,0:T(8,128)(2,1)S(1)}) custom-call(bf16[64,72,128]{2,1,0:T(8,128)(2,1)S(1)} %all_to_all.10.arriving), custom_call_target="tpu_custom_call" | custom-call | flops 1000000 | bytes 2000000 | tf_op jit(solution)/shard_map/patch/pallas_call | solution.py:476
  73.2 24.1 %all_to_all.11.returned = bf16[128,16,128]{2,1,0:T(8,128)(2,1)S(1)} all-to-all(bf16[128,16,128]{2,1,0:T(8,128)(2,1)S(1)} %get-tuple-element.33), channel_id=1, replica_groups=mesh['ccd'=64,'tile'=4] {'ccd'}, dimensions={0} | all-to-all | bytes 1048576 | tf_op jit(solution)/shard_map/all_to_all | solution.py:494
  97.4 0.0 copy-done.1
  97.4 1.4 %difference.1 = f32[128,1024]{1,0:T(8,128)} custom-call(s32[64]{0:T(128)S(1)} %get-tuple-element.32.tmpl_slot, bf16[128,16,128]{2,1,0:T(8,128)(2,1)S(1)} %all_to_all.11.returned, f32[128,1024]{1,0:T(8,128)S(1)} %copy-done.1), custom_call_target="tpu_custom_call" | custom-call | flops 1000000 | bytes 2000000 | tf_op jit(solution)/shard_map/difference/pallas_call | solution.py:495
  (6 shorter events, 0.0 us)
Async XLA Ops:
  0.6 8.7 %copy-start.2 = (bf16[128,1024]{1,0:T(8,128)(2,1)S(1)}, bf16[128,1024]{1,0:T(8,128)(2,1)}, u32[]{:S(2)}) copy-start(bf16[128,1024]{1,0:T(8,128)(2,1)} %image.3) | copy-start | bytes 786436
  1.9 7.4 %collective-permute-start = (bf16[48,1024]{1,0:T(8,128)(2,1)S(1)}, bf16[48,1024]{1,0:T(8,128)(2,1)S(1)}, u32[]{:S(2)}, u32[]{:S(2)}) collective-permute-start(bf16[48,1024]{1,0:T(8,128)(2,1)S(1)} %get-tuple-element.19), channel_id=1, source_target_pairs={{0,1},{1,2},{2,3},{3,0},{4,5},{5,6},{6,7},{7,4},{8,9},{9,10},{10,1... | collective-permute-start | bytes 294920 | tf_op jit(solution)/shard_map/ppermute | solution.py:405
  4.1 5.2 %collective-permute-start.1 = (bf16[48,1024]{1,0:T(8,128)(2,1)S(1)}, bf16[48,1024]{1,0:T(8,128)(2,1)S(1)}, u32[]{:S(2)}, u32[]{:S(2)}) collective-permute-start(bf16[48,1024]{1,0:T(8,128)(2,1)S(1)} %get-tuple-element.20), channel_id=1, source_target_pairs={{0,3},{1,0},{2,1},{3,2},{4,7},{5,4},{6,5},{7,6},{8,11},{9,8},{10,9... | collective-permute-start | bytes 294920 | tf_op jit(solution)/shard_map/ppermute | solution.py:406
  5.7 12.3 %collective-permute-start.2 = (bf16[128,1024]{1,0:T(8,128)(2,1)S(1)}, bf16[128,1024]{1,0:T(8,128)(2,1)S(1)}, u32[]{:S(2)}, u32[]{:S(2)}) collective-permute-start(bf16[128,1024]{1,0:T(8,128)(2,1)S(1)} %get-tuple-element.24.good.own), channel_id=1, source_target_pairs={{0,2},{1,3},{2,0},{3,1},{4,6},{5,7},{6,4},{7,5},{8,10},{9,11},{10,... | collective-permute-start | bytes 786440 | tf_op jit(solution)/shard_map/ppermute | solution.py:407
  9.3 6.5 %copy-start.4 = (s32[64,1]{0,1:T(1,128)S(1)}, s32[64,1]{0,1:T(1,128)}, u32[]{:S(2)}) copy-start(s32[64,1]{0,1:T(1,128)} %param.21) | copy-start | bytes 772
  9.3 6.5 %copy-start.5 = (s32[64]{0:T(128)S(1)}, s32[64]{0:T(128)}, u32[]{:S(2)}) copy-start(s32[64]{0:T(128)} %dest_block.1) | copy-start | bytes 772
  9.3 6.5 %copy-start.6 = (s32[64,1]{0,1:T(1,128)S(1)}, s32[64,1]{0,1:T(1,128)}, u32[]{:S(2)}) copy-start(s32[64,1]{0,1:T(1,128)} %param.24) | copy-start | bytes 772
  9.3 6.5 %copy-start.7 = (s32[64]{0:T(128)S(1)}, s32[64]{0:T(128)}, u32[]{:S(2)}) copy-start(s32[64]{0:T(128)} %tmpl_block.1) | copy-start | bytes 772
  9.3 8.6 %copy-start = (bf16[1,1024,1024]{2,1,0:T(8,128)(2,1)S(1)}, bf16[1,1024,1024]{2,1,0:T(8,128)(2,1)}, u32[]{:S(2)}) copy-start(bf16[1,1024,1024]{2,1,0:T(8,128)(2,1)} %param.20) | copy-start | bytes 6291460
  9.3 8.6 %copy-start.3 = (bf16[128,512]{1,0:T(8,128)(2,1)S(1)}, bf16[128,512]{1,0:T(8,128)(2,1)}, u32[]{:S(2)}) copy-start(bf16[128,512]{1,0:T(8,128)(2,1)} %row_warp.1) | copy-start | bytes 393220
  12.9 7.5 %collective-permute-start.3 = (bf16[128,1024]{1,0:T(8,128)(2,1)S(1)}, bf16[128,1024]{1,0:T(8,128)(2,1)S(1)}, u32[]{:S(2)}, u32[]{:S(2)}) collective-permute-start(bf16[128,1024]{1,0:T(8,128)(2,1)S(1)} %get-tuple-element.25.flux), channel_id=1, source_target_pairs={{0,2},{1,3},{2,0},{3,1},{4,6},{5,7},{6,4},{7,5},{8,10},{9,11},{10,... | collective-permute-start | bytes 786440 | tf_op jit(solution)/shard_map/ppermute | solution.py:440
  14.3 4.6 %collective-permute-start.4 = (bf16[32,1024]{1,0:T(8,128)(2,1)}, bf16[32,1024]{1,0:T(8,128)(2,1)S(1)}, u32[]{:S(2)}, u32[]{:S(2)}) collective-permute-start(bf16[32,1024]{1,0:T(8,128)(2,1)} %get-tuple-element.28), channel_id=1, source_target_pairs={{0,3},{1,0},{2,1},{3,2},{4,7},{5,4},{6,5},{7,6},{8,11},{9,8},{10,9... | collective-permute-start | bytes 196616 | tf_op jit(solution)/shard_map/ppermute | solution.py:441
  15.7 4.7 %collective-permute-start.5 = (bf16[32,1024]{1,0:T(8,128)(2,1)}, bf16[32,1024]{1,0:T(8,128)(2,1)}, u32[]{:S(2)}, u32[]{:S(2)}) collective-permute-start(bf16[32,1024]{1,0:T(8,128)(2,1)} %get-tuple-element.28), channel_id=1, source_target_pairs={{0,1},{1,2},{2,3},{3,0},{4,5},{5,6},{6,7},{7,4},{8,9},{9,10},{10,1... | collective-permute-start | bytes 196616 | tf_op jit(solution)/shard_map/ppermute | solution.py:442
  71.0 26.3 %copy-start.1 = (f32[128,1024]{1,0:T(8,128)S(1)}, f32[128,1024]{1,0:T(8,128)}, u32[]{:S(2)}) copy-start(f32[128,1024]{1,0:T(8,128)} %new_science.1) | copy-start | bytes 1572868

commit v4 on v3

--- a/solution.py
+++ b/solution.py
@@ -143,7 +143,23 @@
 
 
 def edge_kernel(
-    image, mask, coef, cols, rows, to_next, to_previous, good, coef_near, cols_near, rows_near, held, sems
+    tile,
+    image,
+    mask,
+    row_warp,
+    coef,
+    cols,
+    rows,
+    to_next,
+    to_previous,
+    good,
+    coef_near,
+    cols_near,
+    rows_near,
+    level,
+    held,
+    own_part,
+    sems,
 ):
     last = ROWS - EDGE
     copies = []
@@ -160,24 +176,38 @@
     for first, count in parts[2:]:
         span = pl.ds(first, count)
         copies.append(pltpu.make_async_copy(mask.at[span], held.at[span], sems.at[len(copies)]))
-    for source, near in ((coef, coef_near), (cols, cols_near), (rows, rows_near)):
+    own_columns = pl.ds(pl.multiple_of(tile[0] * ROWS, ROWS), ROWS)
+    for source, near in (
+        (row_warp.at[:, own_columns], own_part),
+        (coef, coef_near),
+        (cols, cols_near),
+        (rows, rows_near),
+    ):
         copies.append(pltpu.make_async_copy(source, near, sems.at[len(copies)]))
     for copy in copies:
         copy.start()
     for (first, count), copy in zip(parts, copies[:2] + copies[4:7]):
         copy.wait()
         span = slice(first, first + count)
-        flags = jnp.where(jnp.bitwise_and(held[span, :], 3) == 3, 0.0, 1.0).astype(jnp.bfloat16)
-        good[span, :] = flags
-        if count == EDGE:
-            at = slice(EDGE, 2 * EDGE) if first == 0 else slice(2 * EDGE, 3 * EDGE)
-            to_next[at, :] = flags
-            to_previous[at, :] = flags
+        flags = jnp.where(jnp.bitwise_and(held[span, :], 3) == 3, 0.0, 1.0)
+        good[span, :] = flags.astype(jnp.bfloat16)
     for copy in copies[2:4] + copies[7:]:
         copy.wait()
-
-
-def conv_kernel(tile, visit_weight, before, image, after, table, good, flux, edges, stack):
+    is_level = jnp.max(jnp.abs(own_part[...].astype(jnp.float32))) > 0.0
+    for i in range(8):
+        level[i] = is_level.astype(jnp.int32)
+    send_ends(is_level, good, to_next.at[pl.ds(EDGE, EDGE)], to_previous.at[pl.ds(EDGE, EDGE)])
+
+
+def send_ends(is_level, plane, to_next, to_previous):
+    head, tail = plane[:EDGE, :].astype(jnp.float32), plane[ROWS - EDGE :, :].astype(jnp.float32)
+    to_next[...] = jnp.where(is_level, tail, head).astype(jnp.bfloat16)
+    to_previous[...] = jnp.where(is_level, head, tail).astype(jnp.bfloat16)
+
+
+def conv_kernel(
+    tile, level, visit_weight, before, image, after, table, good, flux, to_next, to_previous, stack
+):
     t = tile[0]
     for group in range(10):
         if group == 0:
@@ -210,24 +240,26 @@
             conv = parts[:BAND] + xn * (parts[BAND : 2 * BAND] + xn * parts[2 * BAND :])
             weight = scale * good[rows, columns].astype(jnp.float32)
             flux[rows, columns] = (weight * conv).astype(jnp.bfloat16)
-    edges[:EDGE, :] = flux[:EDGE, :]
-    edges[EDGE:, :] = flux[ROWS - EDGE :, :]
-
-
-def near_columns(t, row_warp):
+    send_ends(level[0] == 1, flux, to_next, to_previous)
+
+
+def near_columns(t, is_level, row_warp):
     def columns(block):
         return row_warp[:, pl.ds(pl.multiple_of(lax.rem(block, NTILE) * ROWS, ROWS), ROWS)]
 
-    after, before = columns(t + 1), columns(t + 3)
-    last = ROWS - EDGE
-    parts = [columns(t + 2), after[:, :EDGE], after[:, last:], before[:, :EDGE], before[:, last:]]
+    def end(block, first_if_level):
+        part = columns(block).astype(jnp.float32)
+        first, last = part[:, :EDGE], part[:, ROWS - EDGE :]
+        return jnp.where(is_level == first_if_level, first, last).astype(jnp.bfloat16)
+
+    parts = [columns(t + 2), end(t + 1, True), end(t + 3, False)]
     return columns(t), jnp.concatenate(parts, axis=1)
 
 
 def gather_rest(rest, far, after, before):
     rest[:ROWS, :] = far[...]
-    rest[ROWS : ROWS + 2 * EDGE, :] = after[...]
-    rest[ROWS + 2 * EDGE :, :] = before[...]
+    rest[ROWS : ROWS + EDGE, :] = after[...]
+    rest[ROWS + EDGE :, :] = before[...]
 
 
 def warp_columns(rowed, col_warp):
@@ -245,6 +277,7 @@
 
 def warp_weight_kernel(
     tile,
+    level,
     visit_weight,
     flux,
     own,
@@ -259,10 +292,10 @@
     rest,
     rowed,
 ):
-    near, turned = near_columns(tile[0], row_warp)
+    near, turned = near_columns(tile[0], level[0] == 1, row_warp)
     share[...] = jnp.dot(near, flux[...], preferred_element_type=jnp.float32)
     turn[...] = turned
-    gather_rest(rest, far, after.at[pl.ds(EDGE, 2 * EDGE)], before.at[pl.ds(EDGE, 2 * EDGE)])
+    gather_rest(rest, far, after.at[pl.ds(EDGE, EDGE)], before.at[pl.ds(EDGE, EDGE)])
     both = jnp.dot(near, own[...], preferred_element_type=jnp.float32) + jnp.dot(
         turned, rest[...], preferred_element_type=jnp.float32
     )
@@ -379,32 +412,40 @@
     down = [(i, (i + 3) % NTILE) for i in range(NTILE)]
     across = [(i, (i + 2) % NTILE) for i in range(NTILE)]
 
-    to_next, to_previous, good, coef, cols_t, rows_t = call(
+    to_next, to_previous, good, coef, cols_t, rows_t, level = call(
         edge_kernel,
         (
-            struct((3 * EDGE, WIDTH), bf16),
-            struct((3 * EDGE, WIDTH), bf16),
+            struct((2 * EDGE, WIDTH), bf16),
+            struct((2 * EDGE, WIDTH), bf16),
             struct((ROWS, WIDTH), bf16),
             struct((6, 1, NB), f32),
             struct((TAPS, NB), bf16),
             struct((TAPS, NB), bf16),
+            struct((8,), i32),
         ),
-        [HBM] * 5,
-        (VMEM,) * 6,
-        [pltpu.VMEM((ROWS, WIDTH), i32), pltpu.SemaphoreType.DMA((10,))],
+        [SMEM] + [HBM] * 6,
+        (VMEM,) * 6 + (SMEM,),
+        [
+            pltpu.VMEM((ROWS, WIDTH), i32),
+            pltpu.VMEM((ROWS, ROWS), bf16),
+            pltpu.SemaphoreType.DMA((11,)),
+        ],
         "edges",
         400_000,
         1_000_000,
     )(
+        tile,
         in_hbm(visit_image),
         in_hbm(mask_bits),
+        in_hbm(row_warp),
         in_hbm(kernel_coef.transpose(2, 0, 1)),
         in_hbm(basis_cols.T),
         in_hbm(basis_rows.T),
     )
     before = lax.ppermute(to_next, "tile", up)
     after = lax.ppermute(to_previous, "tile", down)
-    far_good = lax.ppermute(good, "tile", across)
+    later_good, before, after = lax.optimization_barrier((good, before, after))
+    far_good = lax.ppermute(later_good, "tile", across)
 
     dest_slot, tmpl_slot, notes = call(
         index_kernel,
@@ -427,31 +468,31 @@
         10_000_000,
         2_000_000,
     )(tile, coef, cols_t, rows_t)
-    flux, edges = call(
+    flux, flux_to_next, flux_to_previous = call(
         conv_kernel,
-        (struct((ROWS, WIDTH), bf16), struct((2 * EDGE, WIDTH), bf16)),
-        [SMEM, SMEM] + [VMEM] * 5,
-        (VMEM, VMEM),
+        (struct((ROWS, WIDTH), bf16),) + (struct((EDGE, WIDTH), bf16),) * 2,
+        [SMEM] * 3 + [VMEM] * 5,
+        (VMEM,) * 3,
         [pltpu.VMEM((2, DEPTH, WIDTH), bf16)],
         "matching",
         2 * 2 * 192 * DEPTH * WIDTH,
         3_000_000,
-    )(tile, visit_weight, before, visit_image, after, taps, good)
+    )(tile, level, visit_weight, before, visit_image, after, taps, good)
     far_flux = lax.ppermute(flux, "tile", across)
-    after_flux = lax.ppermute(edges, "tile", down)
-    before_flux = lax.ppermute(edges, "tile", up)
-    reach = ROWS + 4 * EDGE
+    after_flux = lax.ppermute(flux_to_previous, "tile", down)
+    before_flux = lax.ppermute(flux_to_next, "tile", up)
+    reach = ROWS + 2 * EDGE
     scratch = [pltpu.VMEM((reach, WIDTH), bf16), pltpu.VMEM((ROWS, WIDTH), bf16)]
     warped_weight, share, turn = call(
         warp_weight_kernel,
         (struct((ROWS, WIDTH), bf16), struct((ROWS, WIDTH), f32), struct((ROWS, reach), bf16)),
-        [SMEM, SMEM] + [VMEM] * 7,
+        [SMEM] * 3 + [VMEM] * 7,
         (VMEM,) * 3,
         scratch,
         "warp_weight",
         2 * 128 * WIDTH * WIDTH,
         4_000_000,
-    )(tile, visit_weight, flux, good, far_good, after, before, row_warp, col_warp[0])
+    )(tile, level, visit_weight, flux, good, far_good, after, before, row_warp, col_warp[0])
     outgoing = call(
         warp_flux_kernel,
         struct((64, MESSAGE, 128), bf16),

time: 99 us -> 96.4 us (0.974)
  blocking collectives: 73.2 us -> 67.7 us
  Pallas kernels: 14 us -> 15 us
    all_to_all x1, blocking collectives: 49.1 us -> 43.6 us  [per_device(): lax.all_to_all(outgoing, 'ccd', split_axis=0, concat_axis=0, tiled=True)]
    ppermute x3, starting transfers between devices: 3.02 us -> 4.58 us  [the longest x1 2.42 us: per_device(): far_good = lax.ppermute(later_good, 'tile', across)]
  transfers between devices with their start and end apart: 6 -> 6, of which waited for: 2 -> 1; matrix products, arithmetic and copies ran while one was open for 0% -> 0% of each run, Pallas kernels for 8% -> 9%
where the time goes in v4:
time: 96.4 us; the launch traced here: 96.2 us
  blocking collectives  67.7 us (70%)
  Pallas kernels  15 us (16%)
  starting transfers between devices  9.04 us (9%)
  waiting for transfers between devices  2.34 us (2%)
  between operations  1.44 us (1%)
    all_to_all x1, blocking collectives, per_device(): lax.all_to_all(outgoing, 'ccd', split_axis=0, concat_axis=0, tiled=True)  43.6 us
    all_to_all x1, blocking collectives, per_device(): lax.all_to_all(reply, 'ccd', split_axis=0, concat_axis=0, tiled=True)  24.1 us
    pallas_call x1, Pallas kernels, per_device(): call(conv_kernel, (struct((ROWS, WIDTH), bf16),) + (struct((EDGE, WIDTH),...  3.46 us
    ppermute x1, starting transfers between devices, per_device(): far_good = lax.ppermute(later_good, 'tile', across)  2.42 us
    ppermute x1, waiting for transfers between devices, per_device(): after_flux = lax.ppermute(flux_to_previous, 'tile', down)  2.33 us
    ppermute x1, starting transfers between devices, per_device(): before = lax.ppermute(to_next, 'tile', up)  2.2 us
    pallas_call x1, Pallas kernels, per_device(): call(patch_kernel, (struct((ROWS, WIDTH), f32), struct((SLOTS, 16, 128),...  2.18 us
    ppermute x1, starting transfers between devices, per_device(): after_flux = lax.ppermute(flux_to_previous, 'tile', down)  2.16 us
  transfers between devices with their start and end apart: 6, of which 1 were waited for; matrix products, arithmetic and copies ran while one was open for 0% of the time, Pallas kernels for 9%

profile of v4, /device:TPU:1, one launch (start us, length us, event | category | flops | bytes accessed | tf_op | source)
XLA Modules:
  0.0 96.2 jit_solution(5253509092404160791)
XLA Ops:
  0.6 0.0 copy-start.3
  0.6 2.0 %edges.1 = (bf16[32,1024]{1,0:T(8,128)(2,1)S(1)}, bf16[32,1024]{1,0:T(8,128)(2,1)S(1)}, bf16[128,1024]{1,0:T(8,128)(2,1)S(1)}, f32[6,1,31]{2,1,0:T(1,128)S(1)}, ...) custom-call(s32[1]{0:T(128)} %bitcast.3.tile, bf16[128,1024]{1,0:T(8,128)(2,1)} %image.3, ...), custom_call_target="tpu_custom_call" | custom-call | flops 400000 | bytes 1000000 | tf_op jit(solution)/shard_map/edges/pallas_call | solution.py:415
  2.7 2.2 %collective-permute-start = (bf16[32,1024]{1,0:T(8,128)(2,1)S(1)}, bf16[32,1024]{1,0:T(8,128)(2,1)S(1)}, u32[]{:S(2)}, u32[]{:S(2)}) collective-permute-start(bf16[32,1024]{1,0:T(8,128)(2,1)S(1)} %get-tuple-element.26), channel_id=1, source_target_pairs={{0,1},{1,2},{2,3},{3,0},{4,5},{5,6},{6,7},{7,4},{8,9},{9,10},{10,1... | collective-permute-start | bytes 196616 | tf_op jit(solution)/shard_map/ppermute | solution.py:445
  4.9 1.5 %collective-permute-start.1 = (bf16[32,1024]{1,0:T(8,128)(2,1)S(1)}, bf16[32,1024]{1,0:T(8,128)(2,1)S(1)}, u32[]{:S(2)}, u32[]{:S(2)}) collective-permute-start(bf16[32,1024]{1,0:T(8,128)(2,1)S(1)} %get-tuple-element.27), channel_id=1, source_target_pairs={{0,3},{1,0},{2,1},{3,2},{4,7},{5,4},{6,5},{7,6},{8,11},{9,8},{10,9... | collective-permute-start | bytes 196616 | tf_op jit(solution)/shard_map/ppermute | solution.py:446
  7.0 1.4 %taps.1.table = bf16[2,192,2048]{2,1,0:T(8,128)(2,1)S(1)} custom-call(s32[1]{0:T(128)} %bitcast.3.tile, f32[6,1,31]{2,1,0:T(1,128)S(1)} %get-tuple-element.30.coef, bf16[21,31]{1,0:T(8,128)(2,1)S(1)} %get-tuple-element.31.cols_t, bf16[21,31]{1,0:T(8,128)(2,1)S(1)} %get-tuple-element.32.rows_t), custom_call_target="tpu_custom_call" | custom-call | flops 10000000 | bytes 2000000 | tf_op jit(solution)/shard_map/taps/pallas_call | solution.py:461
  8.5 0.0 collective-permute-done.before
  8.5 0.0 collective-permute-done.1.after
  8.5 2.4 %collective-permute-start.2 = (bf16[128,1024]{1,0:T(8,128)(2,1)S(1)}, bf16[128,1024]{1,0:T(8,128)(2,1)S(1)}, u32[]{:S(2)}, u32[]{:S(2)}) collective-permute-start(bf16[128,1024]{1,0:T(8,128)(2,1)S(1)} %get-tuple-element.34.good.own), channel_id=1, source_target_pairs={{0,2},{1,3},{2,0},{3,1},{4,6},{5,7},{6,4},{7,5},{8,10},{9,11},{10,... | collective-permute-start | bytes 786440 | tf_op jit(solution)/shard_map/ppermute | solution.py:448
  10.9 0.0 copy-done.3
  10.9 0.0 copy-start
  10.9 0.0 copy-start.2
  10.9 3.5 %matching.1 = (bf16[128,1024]{1,0:T(8,128)(2,1)S(1)}, bf16[16,1024]{1,0:T(8,128)(2,1)S(1)}, bf16[16,1024]{1,0:T(8,128)(2,1)S(1)}) custom-call(s32[1]{0:T(128)} %bitcast.3.tile, s32[8]{0:T(128)S(1)} %get-tuple-element.24.level, f32[1]{0:T(128)S(6)} %copy.15.visit_weight, bf16[32,1024]{1,0:T(8,128)(2,1)S(1)} %collective-permute-done.before, ...), custom_call_target="tpu_custom_call" | custom-call | flops 1610612736 | bytes 3000000 | tf_op jit(solution)/shard_map/matching/pallas_call | solution.py:471
  14.4 0.7 collective-permute-start.3
  15.1 2.2 %collective-permute-start.4 = (bf16[16,1024]{1,0:T(8,128)(2,1)S(1)}, bf16[16,1024]{1,0:T(8,128)(2,1)S(1)}, u32[]{:S(2)}, u32[]{:S(2)}) collective-permute-start(bf16[16,1024]{1,0:T(8,128)(2,1)S(1)} %get-tuple-element.37), channel_id=1, source_target_pairs={{0,3},{1,0},{2,1},{3,2},{4,7},{5,4},{6,5},{7,6},{8,11},{9,8},{10,9... | collective-permute-start | bytes 98312 | tf_op jit(solution)/shard_map/ppermute | solution.py:482
  17.3 0.0 collective-permute-start.5
  17.3 0.0 copy-done.4
  17.3 0.0 copy-done.5
  17.3 0.0 copy-done.6
  17.3 0.0 copy-start.7
  17.3 0.6 copy-done.7
  18.0 2.2 %slots.1 = (s32[64]{0:T(128)S(1)}, s32[64]{0:T(128)S(1)}, bf16[64,8,128]{2,1,0:T(8,128)(2,1)S(1)}) custom-call(s32[1]{0:T(128)} %bitcast.home, s32[64]{0:T(128)S(1)} %bitcast.10, s32[64]{0:T(128)S(1)} %copy-done.5, s32[64]{0:T(128)S(1)} %bitcast.11, s32[64]{0:T(128)S(1)} %copy-done.7), custom_call_target="tpu_custom_call" | custom-call | flops 2000000 | bytes 1000000 | tf_op jit(solution)/shard_map/slots/pallas_call | solution.py:450
  20.1 0.0 collective-permute-done.2.far
  20.2 1.2 %warp_weight.1 = (bf16[128,1024]{1,0:T(8,128)(2,1)S(1)}, f32[128,1024]{1,0:T(8,128)S(1)}, bf16[128,160]{1,0:T(8,128)(2,1)S(1)}) custom-call(s32[1]{0:T(128)} %bitcast.3.tile, s32[8]{0:T(128)S(1)} %get-tuple-element.24.level, f32[1]{0:T(128)S(6)} %copy.15.visit_weight, bf16[128,1024]{1,0:T(8,128)(2,1)S(1)} %get-tuple-element.33.flux, ...), custom_call_target="tpu_custom_call" | custom-call | flops 268435456 | bytes 4000000 | tf_op jit(solution)/shard_map/warp_weight/pallas_call | solution.py:486
  21.4 2.3 %collective-permute-done.4.after = bf16[16,1024]{1,0:T(8,128)(2,1)S(1)} collective-permute-done((bf16[16,1024]{1,0:T(8,128)(2,1)S(1)}, bf16[16,1024]{1,0:T(8,128)(2,1)S(1)}, u32[]{:S(2)}, u32[]{:S(2)}) %collective-permute-start.4) | collective-permute-done | bytes 32800 | tf_op jit(solution)/shard_map/ppermute | solution.py:482
  23.7 0.0 collective-permute-done.5.before
  23.7 0.0 collective-permute-done.3.far
  23.7 1.2 %warp_flux.1 = bf16[64,72,128]{2,1,0:T(8,128)(2,1)S(1)} custom-call(s32[64]{0:T(128)S(1)} %get-tuple-element.23.dest_slot, f32[128,1024]{1,0:T(8,128)S(1)} %get-tuple-element.35.share, bf16[128,160]{1,0:T(8,128)(2,1)S(1)} %get-tuple-element.36.turn, bf16[128,1024]{1,0:T(8,128)(2,1)S(1)} %collective-permute-done.3.far, ...), custom_call_target="tpu_custom_call" | custom-call | flops 268435456 | bytes 5000000 | tf_op jit(solution)/shard_map/warp_flux/pallas_call | solution.py:496
  24.9 43.6 %all_to_all.10.arriving = bf16[64,72,128]{2,1,0:T(8,128)(2,1)S(1)} all-to-all(bf16[64,72,128]{2,1,0:T(8,128)(2,1)S(1)} %warp_flux.1), channel_id=1, replica_groups=mesh['ccd'=64,'tile'=4] {'ccd'}, dimensions={0} | all-to-all | bytes 2359296 | tf_op jit(solution)/shard_map/all_to_all | solution.py:516
  68.5 2.2 %patch.1 = (f32[128,1024]{1,0:T(8,128)}, bf16[128,16,128]{2,1,0:T(8,128)(2,1)S(1)}) custom-call(bf16[64,72,128]{2,1,0:T(8,128)(2,1)S(1)} %all_to_all.10.arriving), custom_call_target="tpu_custom_call" | custom-call | flops 1000000 | bytes 2000000 | tf_op jit(solution)/shard_map/patch/pallas_call | solution.py:517
  70.7 24.1 %all_to_all.11.returned = bf16[128,16,128]{2,1,0:T(8,128)(2,1)S(1)} all-to-all(bf16[128,16,128]{2,1,0:T(8,128)(2,1)S(1)} %get-tuple-element.43), channel_id=1, replica_groups=mesh['ccd'=64,'tile'=4] {'ccd'}, dimensions={0} | all-to-all | bytes 1048576 | tf_op jit(solution)/shard_map/all_to_all | solution.py:535
  94.8 0.0 copy-done.1
  94.8 1.4 %difference.1 = f32[128,1024]{1,0:T(8,128)} custom-call(s32[64]{0:T(128)S(1)} %get-tuple-element.42.tmpl_slot, bf16[128,16,128]{2,1,0:T(8,128)(2,1)S(1)} %all_to_all.11.returned, f32[128,1024]{1,0:T(8,128)S(1)} %copy-done.1), custom_call_target="tpu_custom_call" | custom-call | flops 1000000 | bytes 2000000 | tf_op jit(solution)/shard_map/difference/pallas_call | solution.py:536
  (6 shorter events, 0.0 us)
Async XLA Ops:
  0.6 10.3 %copy-start.3 = (bf16[128,1024]{1,0:T(8,128)(2,1)S(1)}, bf16[128,1024]{1,0:T(8,128)(2,1)}, u32[]{:S(2)}) copy-start(bf16[128,1024]{1,0:T(8,128)(2,1)} %image.3) | copy-start | bytes 786436
  2.7 5.8 %collective-permute-start = (bf16[32,1024]{1,0:T(8,128)(2,1)S(1)}, bf16[32,1024]{1,0:T(8,128)(2,1)S(1)}, u32[]{:S(2)}, u32[]{:S(2)}) collective-permute-start(bf16[32,1024]{1,0:T(8,128)(2,1)S(1)} %get-tuple-element.26), channel_id=1, source_target_pairs={{0,1},{1,2},{2,3},{3,0},{4,5},{5,6},{6,7},{7,4},{8,9},{9,10},{10,1... | collective-permute-start | bytes 196616 | tf_op jit(solution)/shard_map/ppermute | solution.py:445
  4.9 3.6 %collective-permute-start.1 = (bf16[32,1024]{1,0:T(8,128)(2,1)S(1)}, bf16[32,1024]{1,0:T(8,128)(2,1)S(1)}, u32[]{:S(2)}, u32[]{:S(2)}) collective-permute-start(bf16[32,1024]{1,0:T(8,128)(2,1)S(1)} %get-tuple-element.27), channel_id=1, source_target_pairs={{0,3},{1,0},{2,1},{3,2},{4,7},{5,4},{6,5},{7,6},{8,11},{9,8},{10,9... | collective-permute-start | bytes 196616 | tf_op jit(solution)/shard_map/ppermute | solution.py:446
  8.5 11.6 %collective-permute-start.2 = (bf16[128,1024]{1,0:T(8,128)(2,1)S(1)}, bf16[128,1024]{1,0:T(8,128)(2,1)S(1)}, u32[]{:S(2)}, u32[]{:S(2)}) collective-permute-start(bf16[128,1024]{1,0:T(8,128)(2,1)S(1)} %get-tuple-element.34.good.own), channel_id=1, source_target_pairs={{0,2},{1,3},{2,0},{3,1},{4,6},{5,7},{6,4},{7,5},{8,10},{9,11},{10,... | collective-permute-start | bytes 786440 | tf_op jit(solution)/shard_map/ppermute | solution.py:448
  10.9 6.4 %copy-start.4 = (s32[64,1]{0,1:T(1,128)S(1)}, s32[64,1]{0,1:T(1,128)}, u32[]{:S(2)}) copy-start(s32[64,1]{0,1:T(1,128)} %param.21) | copy-start | bytes 772
  10.9 6.4 %copy-start.5 = (s32[64]{0:T(128)S(1)}, s32[64]{0:T(128)}, u32[]{:S(2)}) copy-start(s32[64]{0:T(128)} %dest_block.1) | copy-start | bytes 772
  10.9 6.4 %copy-start.6 = (s32[64,1]{0,1:T(1,128)S(1)}, s32[64,1]{0,1:T(1,128)}, u32[]{:S(2)}) copy-start(s32[64,1]{0,1:T(1,128)} %param.24) | copy-start | bytes 772
  10.9 9.2 %copy-start = (bf16[1,1024,1024]{2,1,0:T(8,128)(2,1)S(1)}, bf16[1,1024,1024]{2,1,0:T(8,128)(2,1)}, u32[]{:S(2)}) copy-start(bf16[1,1024,1024]{2,1,0:T(8,128)(2,1)} %param.20) | copy-start | bytes 6291460
  10.9 9.2 %copy-start.2 = (bf16[128,512]{1,0:T(8,128)(2,1)S(1)}, bf16[128,512]{1,0:T(8,128)(2,1)}, u32[]{:S(2)}) copy-start(bf16[128,512]{1,0:T(8,128)(2,1)} %row_warp.3) | copy-start | bytes 393220
  14.4 9.3 %collective-permute-start.3 = (bf16[128,1024]{1,0:T(8,128)(2,1)S(1)}, bf16[128,1024]{1,0:T(8,128)(2,1)S(1)}, u32[]{:S(2)}, u32[]{:S(2)}) collective-permute-start(bf16[128,1024]{1,0:T(8,128)(2,1)S(1)} %get-tuple-element.33.flux), channel_id=1, source_target_pairs={{0,2},{1,3},{2,0},{3,1},{4,6},{5,7},{6,4},{7,5},{8,10},{9,11},{10,... | collective-permute-start | bytes 786440 | tf_op jit(solution)/shard_map/ppermute | solution.py:481
  15.1 8.6 %collective-permute-start.4 = (bf16[16,1024]{1,0:T(8,128)(2,1)S(1)}, bf16[16,1024]{1,0:T(8,128)(2,1)S(1)}, u32[]{:S(2)}, u32[]{:S(2)}) collective-permute-start(bf16[16,1024]{1,0:T(8,128)(2,1)S(1)} %get-tuple-element.37), channel_id=1, source_target_pairs={{0,3},{1,0},{2,1},{3,2},{4,7},{5,4},{6,5},{7,6},{8,11},{9,8},{10,9... | collective-permute-start | bytes 98312 | tf_op jit(solution)/shard_map/ppermute | solution.py:482
  17.3 6.4 %collective-permute-start.5 = (bf16[16,1024]{1,0:T(8,128)(2,1)S(1)}, bf16[16,1024]{1,0:T(8,128)(2,1)S(1)}, u32[]{:S(2)}, u32[]{:S(2)}) collective-permute-start(bf16[16,1024]{1,0:T(8,128)(2,1)S(1)} %get-tuple-element.38), channel_id=1, source_target_pairs={{0,1},{1,2},{2,3},{3,0},{4,5},{5,6},{6,7},{7,4},{8,9},{9,10},{10,1... | collective-permute-start | bytes 98312 | tf_op jit(solution)/shard_map/ppermute | solution.py:483
  17.3 0.7 copy-start.7
  68.5 26.3 %copy-start.1 = (f32[128,1024]{1,0:T(8,128)S(1)}, f32[128,1024]{1,0:T(8,128)}, u32[]{:S(2)}) copy-start(f32[128,1024]{1,0:T(8,128)} %new_science.1) | copy-start | bytes 1572868

commit v5 on v4

--- a/solution.py
+++ b/solution.py
@@ -178,14 +178,20 @@
         copies.append(pltpu.make_async_copy(mask.at[span], held.at[span], sems.at[len(copies)]))
     own_columns = pl.ds(pl.multiple_of(tile[0] * ROWS, ROWS), ROWS)
     for source, near in (
-        (row_warp.at[:, own_columns], own_part),
         (coef, coef_near),
         (cols, cols_near),
         (rows, rows_near),
     ):
         copies.append(pltpu.make_async_copy(source, near, sems.at[len(copies)]))
+    middle = pltpu.make_async_copy(
+        row_warp.at[pl.ds(ROWS // 2, EDGE), own_columns], own_part, sems.at[len(copies)]
+    )
+    middle.start()
     for copy in copies:
         copy.start()
+    middle.wait()
+    size = jnp.abs(own_part[...].astype(jnp.float32))
+    level[...] = jnp.broadcast_to(jnp.max(size, axis=(0, 1), keepdims=True), level.shape)
     for (first, count), copy in zip(parts, copies[:2] + copies[4:7]):
         copy.wait()
         span = slice(first, first + count)
@@ -193,20 +199,18 @@
         good[span, :] = flags.astype(jnp.bfloat16)
     for copy in copies[2:4] + copies[7:]:
         copy.wait()
-    is_level = jnp.max(jnp.abs(own_part[...].astype(jnp.float32))) > 0.0
-    for i in range(8):
-        level[i] = is_level.astype(jnp.int32)
-    send_ends(is_level, good, to_next.at[pl.ds(EDGE, EDGE)], to_previous.at[pl.ds(EDGE, EDGE)])
-
-
-def send_ends(is_level, plane, to_next, to_previous):
+    send_ends(level, good, to_next.at[pl.ds(EDGE, EDGE)], to_previous.at[pl.ds(EDGE, EDGE)])
+
+
+def send_ends(level, plane, to_next, to_previous):
+    is_level = jnp.broadcast_to(level[:1, :1] > 0.0, (EDGE, WIDTH))
     head, tail = plane[:EDGE, :].astype(jnp.float32), plane[ROWS - EDGE :, :].astype(jnp.float32)
     to_next[...] = jnp.where(is_level, tail, head).astype(jnp.bfloat16)
     to_previous[...] = jnp.where(is_level, head, tail).astype(jnp.bfloat16)
 
 
 def conv_kernel(
-    tile, level, visit_weight, before, image, after, table, good, flux, to_next, to_previous, stack
+    tile, visit_weight, level, before, image, after, table, good, flux, to_next, to_previous, stack
 ):
     t = tile[0]
     for group in range(10):
@@ -240,17 +244,20 @@
             conv = parts[:BAND] + xn * (parts[BAND : 2 * BAND] + xn * parts[2 * BAND :])
             weight = scale * good[rows, columns].astype(jnp.float32)
             flux[rows, columns] = (weight * conv).astype(jnp.bfloat16)
-    send_ends(level[0] == 1, flux, to_next, to_previous)
-
-
-def near_columns(t, is_level, row_warp):
+    send_ends(level, flux, to_next, to_previous)
+
+
+def near_columns(t, level, row_warp):
     def columns(block):
         return row_warp[:, pl.ds(pl.multiple_of(lax.rem(block, NTILE) * ROWS, ROWS), ROWS)]
+
+    is_level = jnp.broadcast_to(level[:1, :1] > 0.0, (ROWS, EDGE))
 
     def end(block, first_if_level):
         part = columns(block).astype(jnp.float32)
         first, last = part[:, :EDGE], part[:, ROWS - EDGE :]
-        return jnp.where(is_level == first_if_level, first, last).astype(jnp.bfloat16)
+        chosen = (first, last) if first_if_level else (last, first)
+        return jnp.where(is_level, chosen[0], chosen[1]).astype(jnp.bfloat16)
 
     parts = [columns(t + 2), end(t + 1, True), end(t + 3, False)]
     return columns(t), jnp.concatenate(parts, axis=1)
@@ -277,8 +284,8 @@
 
 def warp_weight_kernel(
     tile,
+    visit_weight,
     level,
-    visit_weight,
     flux,
     own,
     far,
@@ -292,7 +299,7 @@
     rest,
     rowed,
 ):
-    near, turned = near_columns(tile[0], level[0] == 1, row_warp)
+    near, turned = near_columns(tile[0], level, row_warp)
     share[...] = jnp.dot(near, flux[...], preferred_element_type=jnp.float32)
     turn[...] = turned
     gather_rest(rest, far, after.at[pl.ds(EDGE, EDGE)], before.at[pl.ds(EDGE, EDGE)])
@@ -306,7 +313,7 @@
 
 
 def warp_flux_kernel(
-    dest_slot,
+    dest_slot_in,
     share,
     turn,
     far,
@@ -318,12 +325,17 @@
     outgoing,
     rest,
     rowed,
+    dest_slot,
+    sem,
 ):
+    copy = pltpu.make_async_copy(dest_slot_in, dest_slot, sem)
+    copy.start()
     gather_rest(rest, far, after, before)
     rowed[...] = (
         share[...] + jnp.dot(turn[...], rest[...], preferred_element_type=jnp.float32)
     ).astype(jnp.bfloat16)
     outgoing[:, 64:, :] = notes[...]
+    copy.wait()
     for n, part in warp_columns(rowed, col_warp):
         for down in range(8):
             for c in range(2):
@@ -421,13 +433,13 @@
             struct((6, 1, NB), f32),
             struct((TAPS, NB), bf16),
             struct((TAPS, NB), bf16),
-            struct((8,), i32),
+            struct((8, 128), f32),
         ),
         [SMEM] + [HBM] * 6,
-        (VMEM,) * 6 + (SMEM,),
+        (VMEM,) * 7,
         [
             pltpu.VMEM((ROWS, WIDTH), i32),
-            pltpu.VMEM((ROWS, ROWS), bf16),
+            pltpu.VMEM((EDGE, ROWS), bf16),
             pltpu.SemaphoreType.DMA((11,)),
         ],
         "edges",
@@ -444,8 +456,6 @@
     )
     before = lax.ppermute(to_next, "tile", up)
     after = lax.ppermute(to_previous, "tile", down)
-    later_good, before, after = lax.optimization_barrier((good, before, after))
-    far_good = lax.ppermute(later_good, "tile", across)
 
     dest_slot, tmpl_slot, notes = call(
         index_kernel,
@@ -468,16 +478,18 @@
         10_000_000,
         2_000_000,
     )(tile, coef, cols_t, rows_t)
+    later_good, taps = lax.optimization_barrier((good, taps))
+    far_good = lax.ppermute(later_good, "tile", across)
     flux, flux_to_next, flux_to_previous = call(
         conv_kernel,
         (struct((ROWS, WIDTH), bf16),) + (struct((EDGE, WIDTH), bf16),) * 2,
-        [SMEM] * 3 + [VMEM] * 5,
+        [SMEM] * 2 + [VMEM] * 6,
         (VMEM,) * 3,
         [pltpu.VMEM((2, DEPTH, WIDTH), bf16)],
         "matching",
         2 * 2 * 192 * DEPTH * WIDTH,
         3_000_000,
-    )(tile, level, visit_weight, before, visit_image, after, taps, good)
+    )(tile, visit_weight, level, before, visit_image, after, taps, good)
     far_flux = lax.ppermute(flux, "tile", across)
     after_flux = lax.ppermute(flux_to_previous, "tile", down)
     before_flux = lax.ppermute(flux_to_next, "tile", up)
@@ -486,19 +498,19 @@
     warped_weight, share, turn = call(
         warp_weight_kernel,
         (struct((ROWS, WIDTH), bf16), struct((ROWS, WIDTH), f32), struct((ROWS, reach), bf16)),
-        [SMEM] * 3 + [VMEM] * 7,
+        [SMEM] * 2 + [VMEM] * 8,
         (VMEM,) * 3,
         scratch,
         "warp_weight",
         2 * 128 * WIDTH * WIDTH,
         4_000_000,
-    )(tile, level, visit_weight, flux, good, far_good, after, before, row_warp, col_warp[0])
+    )(tile, visit_weight, level, flux, good, far_good, after, before, row_warp, col_warp[0])
     outgoing = call(
         warp_flux_kernel,
         struct((64, MESSAGE, 128), bf16),
-        [SMEM] + [VMEM] * 8,
+        [VMEM] * 9,
         VMEM,
-        scratch,
+        scratch + [pltpu.SMEM((64,), i32), pltpu.SemaphoreType.DMA],
         "warp_flux",
         2 * 128 * WIDTH * WIDTH,
         5_000_000,

time: 96.4 us -> 94.8 us (0.983)
  Pallas kernels: 15 us -> 13.2 us
  blocking collectives: 67.7 us -> 69.4 us
    ppermute x1, waiting for transfers between devices: 2.33 us -> 0.01 us  [per_device(): after_flux = lax.ppermute(flux_to_previous, 'tile', down)]
    all_to_all x1, blocking collectives: 43.6 us -> 45.3 us  [per_device(): lax.all_to_all(outgoing, 'ccd', split_axis=0, concat_axis=0, tiled=True)]
    ppermute x1, waiting for transfers between devices: 0.01 us -> 1.4 us  [per_device(): before_flux = lax.ppermute(flux_to_next, 'tile', up)]
  transfers between devices with their start and end apart: 6 -> 6, of which waited for: 1 -> 1; matrix products, arithmetic and copies ran while one was open for 0% -> 0% of each run, Pallas kernels for 9% -> 8%
where the time goes in v5:
time: 94.8 us; the launch traced here: 94.6 us
  blocking collectives  69.4 us (73%)
  Pallas kernels  13.2 us (14%)
  starting transfers between devices  8.34 us (9%)
  between operations  1.46 us (2%)
  waiting for transfers between devices  1.42 us (1%)
    all_to_all x1, blocking collectives, per_device(): lax.all_to_all(outgoing, 'ccd', split_axis=0, concat_axis=0, tiled=True)  45.3 us
    all_to_all x1, blocking collectives, per_device(): lax.all_to_all(reply, 'ccd', split_axis=0, concat_axis=0, tiled=True)  24.2 us
    pallas_call x1, Pallas kernels, per_device(): call(conv_kernel, (struct((ROWS, WIDTH), bf16),) + (struct((EDGE, WIDTH),...  2.95 us
    ppermute x1, starting transfers between devices, per_device(): before = lax.ppermute(to_next, 'tile', up)  2.2 us
    pallas_call x1, Pallas kernels, per_device(): call(index_kernel, (struct((64,), i32), struct((64,), i32), struct((64, N...  2.15 us
    pallas_call x1, Pallas kernels, per_device(): call(patch_kernel, (struct((ROWS, WIDTH), f32), struct((SLOTS, 16, 128),...  2.15 us
  transfers between devices with their start and end apart: 6, of which 1 were waited for; matrix products, arithmetic and copies ran while one was open for 0% of the time, Pallas kernels for 8%

profile of v5, /device:TPU:1, one launch (start us, length us, event | category | flops | bytes accessed | tf_op | source)
XLA Modules:
  0.0 94.6 jit_solution(14618552934720761199)
XLA Ops:
  0.6 0.0 copy-start.3
  0.6 1.4 %edges.1 = (bf16[32,1024]{1,0:T(8,128)(2,1)S(1)}, bf16[32,1024]{1,0:T(8,128)(2,1)S(1)}, bf16[128,1024]{1,0:T(8,128)(2,1)S(1)}, f32[6,1,31]{2,1,0:T(1,128)S(1)}, ...) custom-call(s32[1]{0:T(128)} %bitcast.3.tile, bf16[128,1024]{1,0:T(8,128)(2,1)} %image.3, ...), custom_call_target="tpu_custom_call" | custom-call | flops 400000 | bytes 1000000 | tf_op jit(solution)/shard_map/edges/pallas_call | solution.py:427
  2.0 2.2 %collective-permute-start = (bf16[32,1024]{1,0:T(8,128)(2,1)S(1)}, bf16[32,1024]{1,0:T(8,128)(2,1)S(1)}, u32[]{:S(2)}, u32[]{:S(2)}) collective-permute-start(bf16[32,1024]{1,0:T(8,128)(2,1)S(1)} %get-tuple-element.24), channel_id=1, source_target_pairs={{0,1},{1,2},{2,3},{3,0},{4,5},{5,6},{6,7},{7,4},{8,9},{9,10},{10,1... | collective-permute-start | bytes 196616 | tf_op jit(solution)/shard_map/ppermute | solution.py:457
  4.2 1.5 %collective-permute-start.1 = (bf16[32,1024]{1,0:T(8,128)(2,1)S(1)}, bf16[32,1024]{1,0:T(8,128)(2,1)S(1)}, u32[]{:S(2)}, u32[]{:S(2)}) collective-permute-start(bf16[32,1024]{1,0:T(8,128)(2,1)S(1)} %get-tuple-element.25), channel_id=1, source_target_pairs={{0,3},{1,0},{2,1},{3,2},{4,7},{5,4},{6,5},{7,6},{8,11},{9,8},{10,9... | collective-permute-start | bytes 196616 | tf_op jit(solution)/shard_map/ppermute | solution.py:458
  5.7 1.4 %taps.1.table = bf16[2,192,2048]{2,1,0:T(8,128)(2,1)S(1)} custom-call(s32[1]{0:T(128)} %bitcast.3.tile, f32[6,1,31]{2,1,0:T(1,128)S(1)} %get-tuple-element.27.coef, bf16[21,31]{1,0:T(8,128)(2,1)S(1)} %get-tuple-element.28.cols_t, bf16[21,31]{1,0:T(8,128)(2,1)S(1)} %get-tuple-element.29.rows_t), custom_call_target="tpu_custom_call" | custom-call | flops 10000000 | bytes 2000000 | tf_op jit(solution)/shard_map/taps/pallas_call | solution.py:471
  7.1 1.6 %collective-permute-start.2 = (bf16[128,1024]{1,0:T(8,128)(2,1)S(1)}, bf16[128,1024]{1,0:T(8,128)(2,1)S(1)}, u32[]{:S(2)}, u32[]{:S(2)}) collective-permute-start(bf16[128,1024]{1,0:T(8,128)(2,1)S(1)} %get-tuple-element.32.good.own), channel_id=1, source_target_pairs={{0,2},{1,3},{2,0},{3,1},{4,6},{5,7},{6,4},{7,5},{8,10},{9,11},{10,... | collective-permute-start | bytes 786440 | tf_op jit(solution)/shard_map/ppermute | solution.py:482
  9.4 0.0 collective-permute-done.before
  9.4 0.0 collective-permute-done.1.after
  9.5 0.0 copy-done.3
  9.5 0.0 copy-start.4
  9.5 0.0 copy-start.5
  9.5 0.0 copy-start.6
  9.5 0.0 copy-start
  9.5 0.0 copy-start.2
  9.5 3.0 %matching.1 = (bf16[128,1024]{1,0:T(8,128)(2,1)S(1)}, bf16[16,1024]{1,0:T(8,128)(2,1)S(1)}, bf16[16,1024]{1,0:T(8,128)(2,1)S(1)}) custom-call(s32[1]{0:T(128)} %bitcast.3.tile, f32[1]{0:T(128)S(6)} %copy.15.visit_weight, f32[8,128]{1,0:T(8,128)S(1)} %get-tuple-element.23.level, bf16[32,1024]{1,0:T(8,128)(2,1)S(1)} %collective-permute-done.before, ...), custom_call_target="tpu_custom_call" | custom-call | flops 1610612736 | bytes 3000000 | tf_op jit(solution)/shard_map/matching/pallas_call | solution.py:483
  12.5 1.5 %collective-permute-start.3 = (bf16[128,1024]{1,0:T(8,128)(2,1)S(1)}, bf16[128,1024]{1,0:T(8,128)(2,1)S(1)}, u32[]{:S(2)}, u32[]{:S(2)}) collective-permute-start(bf16[128,1024]{1,0:T(8,128)(2,1)S(1)} %get-tuple-element.31.flux), channel_id=1, source_target_pairs={{0,2},{1,3},{2,0},{3,1},{4,6},{5,7},{6,4},{7,5},{8,10},{9,11},{10,... | collective-permute-start | bytes 786440 | tf_op jit(solution)/shard_map/ppermute | solution.py:493
  14.0 1.4 %collective-permute-start.4 = (bf16[16,1024]{1,0:T(8,128)(2,1)S(1)}, bf16[16,1024]{1,0:T(8,128)(2,1)S(1)}, u32[]{:S(2)}, u32[]{:S(2)}) collective-permute-start(bf16[16,1024]{1,0:T(8,128)(2,1)S(1)} %get-tuple-element.35), channel_id=1, source_target_pairs={{0,3},{1,0},{2,1},{3,2},{4,7},{5,4},{6,5},{7,6},{8,11},{9,8},{10,9... | collective-permute-start | bytes 98312 | tf_op jit(solution)/shard_map/ppermute | solution.py:494
  15.4 0.1 collective-permute-start.5
  15.4 0.0 copy-done.4
  15.5 0.0 copy-done.5
  15.5 0.6 copy-done.7
  16.1 2.2 %slots.1 = (s32[64]{0:T(128)S(1)}, s32[64]{0:T(128)S(1)}, bf16[64,8,128]{2,1,0:T(8,128)(2,1)S(1)}) custom-call(s32[1]{0:T(128)} %bitcast.home, s32[64]{0:T(128)S(1)} %bitcast.10, s32[64]{0:T(128)S(1)} %copy-done.5, s32[64]{0:T(128)S(1)} %bitcast.11, s32[64]{0:T(128)S(1)} %copy-done.7), custom_call_target="tpu_custom_call" | custom-call | flops 2000000 | bytes 1000000 | tf_op jit(solution)/shard_map/slots/pallas_call | solution.py:460
  18.3 0.0 collective-permute-done.2.far
  18.3 0.7 warp_weight.1
  19.0 0.0 collective-permute-done.4.after
  19.0 1.4 %collective-permute-done.5.before = bf16[16,1024]{1,0:T(8,128)(2,1)S(1)} collective-permute-done((bf16[16,1024]{1,0:T(8,128)(2,1)S(1)}, bf16[16,1024]{1,0:T(8,128)(2,1)S(1)}, u32[]{:S(2)}, u32[]{:S(2)}) %collective-permute-start.5) | collective-permute-done | bytes 32800 | tf_op jit(solution)/shard_map/ppermute | solution.py:495
  20.4 0.0 collective-permute-done.3.far
  20.4 1.2 %warp_flux.1 = bf16[64,72,128]{2,1,0:T(8,128)(2,1)S(1)} custom-call(s32[64]{0:T(128)S(1)} %get-tuple-element.22.dest_slot_in, f32[128,1024]{1,0:T(8,128)S(1)} %get-tuple-element.33.share, bf16[128,160]{1,0:T(8,128)(2,1)S(1)} %get-tuple-element.34.turn, bf16[128,1024]{1,0:T(8,128)(2,1)S(1)} %collective-permute-done.3.far, ...), custom_call_target="tpu_custom_call" | custom-call | flops 268435456 | bytes 5000000 | tf_op jit(solution)/shard_map/warp_flux/pallas_call | solution.py:508
  21.6 45.3 %all_to_all.10.arriving = bf16[64,72,128]{2,1,0:T(8,128)(2,1)S(1)} all-to-all(bf16[64,72,128]{2,1,0:T(8,128)(2,1)S(1)} %warp_flux.1), channel_id=1, replica_groups=mesh['ccd'=64,'tile'=4] {'ccd'}, dimensions={0} | all-to-all | bytes 2359296 | tf_op jit(solution)/shard_map/all_to_all | solution.py:528
  66.8 2.1 %patch.1 = (f32[128,1024]{1,0:T(8,128)}, bf16[128,16,128]{2,1,0:T(8,128)(2,1)S(1)}) custom-call(bf16[64,72,128]{2,1,0:T(8,128)(2,1)S(1)} %all_to_all.10.arriving), custom_call_target="tpu_custom_call" | custom-call | flops 1000000 | bytes 2000000 | tf_op jit(solution)/shard_map/patch/pallas_call | solution.py:529
  69.0 24.2 %all_to_all.11.returned = bf16[128,16,128]{2,1,0:T(8,128)(2,1)S(1)} all-to-all(bf16[128,16,128]{2,1,0:T(8,128)(2,1)S(1)} %get-tuple-element.41), channel_id=1, replica_groups=mesh['ccd'=64,'tile'=4] {'ccd'}, dimensions={0} | all-to-all | bytes 1048576 | tf_op jit(solution)/shard_map/all_to_all | solution.py:547
  93.2 1.4 %difference.1 = f32[128,1024]{1,0:T(8,128)} custom-call(s32[64]{0:T(128)S(1)} %get-tuple-element.40.tmpl_slot, bf16[128,16,128]{2,1,0:T(8,128)(2,1)S(1)} %all_to_all.11.returned, f32[128,1024]{1,0:T(8,128)S(1)} %copy-done.1), custom_call_target="tpu_custom_call" | custom-call | flops 1000000 | bytes 2000000 | tf_op jit(solution)/shard_map/difference/pallas_call | solution.py:548
  (6 shorter events, 0.0 us)
Async XLA Ops:
  0.6 8.8 %copy-start.3 = (bf16[128,1024]{1,0:T(8,128)(2,1)S(1)}, bf16[128,1024]{1,0:T(8,128)(2,1)}, u32[]{:S(2)}) copy-start(bf16[128,1024]{1,0:T(8,128)(2,1)} %image.3) | copy-start | bytes 786436
  2.0 7.4 %collective-permute-start = (bf16[32,1024]{1,0:T(8,128)(2,1)S(1)}, bf16[32,1024]{1,0:T(8,128)(2,1)S(1)}, u32[]{:S(2)}, u32[]{:S(2)}) collective-permute-start(bf16[32,1024]{1,0:T(8,128)(2,1)S(1)} %get-tuple-element.24), channel_id=1, source_target_pairs={{0,1},{1,2},{2,3},{3,0},{4,5},{5,6},{6,7},{7,4},{8,9},{9,10},{10,1... | collective-permute-start | bytes 196616 | tf_op jit(solution)/shard_map/ppermute | solution.py:457
  4.2 5.2 %collective-permute-start.1 = (bf16[32,1024]{1,0:T(8,128)(2,1)S(1)}, bf16[32,1024]{1,0:T(8,128)(2,1)S(1)}, u32[]{:S(2)}, u32[]{:S(2)}) collective-permute-start(bf16[32,1024]{1,0:T(8,128)(2,1)S(1)} %get-tuple-element.25), channel_id=1, source_target_pairs={{0,3},{1,0},{2,1},{3,2},{4,7},{5,4},{6,5},{7,6},{8,11},{9,8},{10,9... | collective-permute-start | bytes 196616 | tf_op jit(solution)/shard_map/ppermute | solution.py:458
  7.1 11.1 %collective-permute-start.2 = (bf16[128,1024]{1,0:T(8,128)(2,1)S(1)}, bf16[128,1024]{1,0:T(8,128)(2,1)S(1)}, u32[]{:S(2)}, u32[]{:S(2)}) collective-permute-start(bf16[128,1024]{1,0:T(8,128)(2,1)S(1)} %get-tuple-element.32.good.own), channel_id=1, source_target_pairs={{0,2},{1,3},{2,0},{3,1},{4,6},{5,7},{6,4},{7,5},{8,10},{9,11},{10,... | collective-permute-start | bytes 786440 | tf_op jit(solution)/shard_map/ppermute | solution.py:482
  9.5 6.0 %copy-start.4 = (s32[64,1]{0,1:T(1,128)S(1)}, s32[64,1]{0,1:T(1,128)}, u32[]{:S(2)}) copy-start(s32[64,1]{0,1:T(1,128)} %param.21) | copy-start | bytes 772
  9.5 6.0 %copy-start.5 = (s32[64]{0:T(128)S(1)}, s32[64]{0:T(128)}, u32[]{:S(2)}) copy-start(s32[64]{0:T(128)} %dest_block.1) | copy-start | bytes 772
  9.5 6.0 %copy-start.6 = (s32[64,1]{0,1:T(1,128)S(1)}, s32[64,1]{0,1:T(1,128)}, u32[]{:S(2)}) copy-start(s32[64,1]{0,1:T(1,128)} %param.24) | copy-start | bytes 772
  9.5 8.8 %copy-start = (bf16[1,1024,1024]{2,1,0:T(8,128)(2,1)S(1)}, bf16[1,1024,1024]{2,1,0:T(8,128)(2,1)}, u32[]{:S(2)}) copy-start(bf16[1,1024,1024]{2,1,0:T(8,128)(2,1)} %param.20) | copy-start | bytes 6291460
  9.5 8.8 %copy-start.2 = (bf16[128,512]{1,0:T(8,128)(2,1)S(1)}, bf16[128,512]{1,0:T(8,128)(2,1)}, u32[]{:S(2)}) copy-start(bf16[128,512]{1,0:T(8,128)(2,1)} %row_warp.3) | copy-start | bytes 393220
  12.5 7.9 %collective-permute-start.3 = (bf16[128,1024]{1,0:T(8,128)(2,1)S(1)}, bf16[128,1024]{1,0:T(8,128)(2,1)S(1)}, u32[]{:S(2)}, u32[]{:S(2)}) collective-permute-start(bf16[128,1024]{1,0:T(8,128)(2,1)S(1)} %get-tuple-element.31.flux), channel_id=1, source_target_pairs={{0,2},{1,3},{2,0},{3,1},{4,6},{5,7},{6,4},{7,5},{8,10},{9,11},{10,... | collective-permute-start | bytes 786440 | tf_op jit(solution)/shard_map/ppermute | solution.py:493
  14.0 5.0 %collective-permute-start.4 = (bf16[16,1024]{1,0:T(8,128)(2,1)S(1)}, bf16[16,1024]{1,0:T(8,128)(2,1)S(1)}, u32[]{:S(2)}, u32[]{:S(2)}) collective-permute-start(bf16[16,1024]{1,0:T(8,128)(2,1)S(1)} %get-tuple-element.35), channel_id=1, source_target_pairs={{0,3},{1,0},{2,1},{3,2},{4,7},{5,4},{6,5},{7,6},{8,11},{9,8},{10,9... | collective-permute-start | bytes 98312 | tf_op jit(solution)/shard_map/ppermute | solution.py:494
  15.4 5.0 %collective-permute-start.5 = (bf16[16,1024]{1,0:T(8,128)(2,1)S(1)}, bf16[16,1024]{1,0:T(8,128)(2,1)S(1)}, u32[]{:S(2)}, u32[]{:S(2)}) collective-permute-start(bf16[16,1024]{1,0:T(8,128)(2,1)S(1)} %get-tuple-element.36), channel_id=1, source_target_pairs={{0,1},{1,2},{2,3},{3,0},{4,5},{5,6},{6,7},{7,4},{8,9},{9,10},{10,1... | collective-permute-start | bytes 98312 | tf_op jit(solution)/shard_map/ppermute | solution.py:495
  15.5 0.7 copy-start.7
  66.8 26.3 %copy-start.1 = (f32[128,1024]{1,0:T(8,128)S(1)}, f32[128,1024]{1,0:T(8,128)}, u32[]{:S(2)}) copy-start(f32[128,1024]{1,0:T(8,128)} %new_science.1) | copy-start | bytes 1572868

commit v6 on v5

--- a/solution.py
+++ b/solution.py
@@ -99,20 +99,20 @@
         notes[patch] = note.astype(jnp.float32).astype(jnp.bfloat16)
 
 
-def table_kernel(tile, coef, cols_t, rows_t, table, wide):
+def table_kernel(tile, coef, cols_t, rows_t, table, wide, mixed_rows):
     wide[...] = jnp.zeros_like(wide)
+    mixed_rows[...] = jnp.zeros_like(mixed_rows)
     wide[6 : 6 + TAPS, :] = cols_t[...].astype(jnp.float32)
-    taps = []
     for p in range(6):
-        taps.append(
-            lax.dot_general(
-                rows_t[...].astype(jnp.float32) * coef[p],
-                wide[...],
-                (((1,), (1,)), ((), ())),
-                preferred_element_type=jnp.float32,
-                precision=lax.Precision.HIGHEST,
-            )
-        )
+        mixed_rows[24 * p : 24 * p + TAPS, :] = rows_t[...].astype(jnp.float32) * coef[p]
+    every = lax.dot_general(
+        mixed_rows[...],
+        wide[...],
+        (((1,), (1,)), ((), ())),
+        preferred_element_type=jnp.float32,
+        precision=lax.Precision.HIGHEST,
+    )
+    taps = [every[24 * p : 24 * p + TAPS] for p in range(6)]
     lane = lax.broadcasted_iota(jnp.int32, (BAND, 128), 1)
     row = lax.broadcasted_iota(jnp.int32, (BAND, 128), 0)
     for band in range(2):
@@ -349,7 +349,7 @@
                 ]
 
 
-def patch_kernel(arriving, coadd, reply, sums, values, served, note, table, sem, out_sem):
+def patch_kernel(arriving, values, reply, sums, served, note, table, sem):
     notes = arriving[0, 64:, :].astype(jnp.float32)
     for sender in range(1, 64):
         notes = notes + arriving[sender, 64:, :].astype(jnp.float32)
@@ -371,8 +371,6 @@
         value = sums[block, :16, :] / jnp.maximum(sums[block, 16:, :], FLOOR)
         values[down * 16 : down * 16 + 16, c * 128 : c * 128 + 128] = value
         served[block] = value.astype(jnp.bfloat16)
-    out = pltpu.make_async_copy(values, coadd, out_sem)
-    out.start()
 
     def serve(sender, _):
         for rank in range(2):
@@ -380,11 +378,11 @@
         return 0
 
     lax.fori_loop(0, 64, serve, 0, unroll=4)
-    out.wait()
-
-
-def difference_kernel(tmpl_slot, returned, new_science, difference, held, sems):
-    copies = []
+
+
+def difference_kernel(tmpl_slot, returned, new_science, values, coadd, difference, held, sems):
+    copies = [pltpu.make_async_copy(values, coadd, sems.at[4])]
+    copies[0].start()
     for down in range(8):
         rows = slice(down * 16, down * 16 + 16)
         for c in range(8):
@@ -473,7 +471,7 @@
         struct((2, 3 * BAND, DEPTH), bf16),
         [SMEM, VMEM, VMEM, VMEM],
         VMEM,
-        [pltpu.VMEM((128, NB), f32)],
+        [pltpu.VMEM((128, NB), f32), pltpu.VMEM((144, NB), f32)],
         "taps",
         10_000_000,
         2_000_000,
@@ -526,18 +524,16 @@
         notes,
     )
     arriving = lax.all_to_all(outgoing, "ccd", split_axis=0, concat_axis=0, tiled=True)
-    coadd, reply = call(
+    values, reply = call(
         patch_kernel,
         (struct((ROWS, WIDTH), f32), struct((SLOTS, 16, 128), bf16)),
         [VMEM],
-        (HBM, VMEM),
+        (VMEM, VMEM),
         [
             pltpu.VMEM((NBLK + 8, 32, 128), f32),
-            pltpu.VMEM((ROWS, WIDTH), f32),
             pltpu.VMEM((NBLK, 16, 128), bf16),
             pltpu.VMEM((NOTE, 128), i32),
             pltpu.SMEM((NOTE, 128), i32),
-            pltpu.SemaphoreType.DMA,
             pltpu.SemaphoreType.DMA,
         ],
         "patch",
@@ -545,17 +541,16 @@
         2_000_000,
     )(arriving)
     returned = lax.all_to_all(reply, "ccd", split_axis=0, concat_axis=0, tiled=True)
-    difference = call(
+    return call(
         difference_kernel,
-        struct((ROWS, WIDTH), f32),
-        [SMEM, VMEM, VMEM],
-        HBM,
-        [pltpu.VMEM((ROWS, WIDTH), f32), pltpu.SemaphoreType.DMA((4,))],
+        (struct((ROWS, WIDTH), f32),) * 2,
+        [SMEM, VMEM, VMEM, VMEM],
+        (HBM, HBM),
+        [pltpu.VMEM((ROWS, WIDTH), f32), pltpu.SemaphoreType.DMA((5,))],
         "difference",
         1_000_000,
-        2_000_000,
-    )(tmpl_slot, returned, new_science)
-    return coadd, difference
+        3_000_000,
+    )(tmpl_slot, returned, new_science, values)
 
 
 def solution(mesh):

time: 94.8 us -> 94.2 us (level)
  transfers between devices with their start and end apart: 6 -> 6, of which waited for: 1 -> 1; matrix products, arithmetic and copies ran while one was open for 0% -> 0% of each run, Pallas kernels for 8% -> 7%
where the time goes in v6:
time: 94.2 us; the launch traced here: 94 us
  blocking collectives  69.4 us (74%)
  Pallas kernels  12.6 us (13%)
  starting transfers between devices  8.35 us (9%)
  between operations  1.46 us (2%)
  waiting for transfers between devices  1.4 us (1%)
    all_to_all x1, blocking collectives, per_device(): lax.all_to_all(outgoing, 'ccd', split_axis=0, concat_axis=0, tiled=True)  45.3 us
    all_to_all x1, blocking collectives, per_device(): lax.all_to_all(reply, 'ccd', split_axis=0, concat_axis=0, tiled=True)  24.2 us
    pallas_call x1, Pallas kernels, per_device(): call(conv_kernel, (struct((ROWS, WIDTH), bf16),) + (struct((EDGE, WIDTH),...  2.95 us
    ppermute x1, starting transfers between devices, per_device(): before = lax.ppermute(to_next, 'tile', up)  2.2 us
    pallas_call x1, Pallas kernels, per_device(): call(index_kernel, (struct((64,), i32), struct((64,), i32), struct((64, N...  2.15 us
  transfers between devices with their start and end apart: 6, of which 1 were waited for; matrix products, arithmetic and copies ran while one was open for 0% of the time, Pallas kernels for 7%

profile of v6, /device:TPU:1, one launch (start us, length us, event | category | flops | bytes accessed | tf_op | source)
XLA Modules:
  0.0 94.0 jit_solution(2038276437959257455)
XLA Ops:
  0.6 0.0 copy-start.3
  0.6 1.4 %edges.1 = (bf16[32,1024]{1,0:T(8,128)(2,1)S(1)}, bf16[32,1024]{1,0:T(8,128)(2,1)S(1)}, bf16[128,1024]{1,0:T(8,128)(2,1)S(1)}, f32[6,1,31]{2,1,0:T(1,128)S(1)}, ...) custom-call(s32[1]{0:T(128)} %bitcast.3.tile, bf16[128,1024]{1,0:T(8,128)(2,1)} %image.3, ...), custom_call_target="tpu_custom_call" | custom-call | flops 400000 | bytes 1000000 | tf_op jit(solution)/shard_map/edges/pallas_call | solution.py:425
  2.0 2.2 %collective-permute-start = (bf16[32,1024]{1,0:T(8,128)(2,1)S(1)}, bf16[32,1024]{1,0:T(8,128)(2,1)S(1)}, u32[]{:S(2)}, u32[]{:S(2)}) collective-permute-start(bf16[32,1024]{1,0:T(8,128)(2,1)S(1)} %get-tuple-element.25), channel_id=1, source_target_pairs={{0,1},{1,2},{2,3},{3,0},{4,5},{5,6},{6,7},{7,4},{8,9},{9,10},{10,1... | collective-permute-start | bytes 196616 | tf_op jit(solution)/shard_map/ppermute | solution.py:455
  4.2 1.5 %collective-permute-start.1 = (bf16[32,1024]{1,0:T(8,128)(2,1)S(1)}, bf16[32,1024]{1,0:T(8,128)(2,1)S(1)}, u32[]{:S(2)}, u32[]{:S(2)}) collective-permute-start(bf16[32,1024]{1,0:T(8,128)(2,1)S(1)} %get-tuple-element.26), channel_id=1, source_target_pairs={{0,3},{1,0},{2,1},{3,2},{4,7},{5,4},{6,5},{7,6},{8,11},{9,8},{10,9... | collective-permute-start | bytes 196616 | tf_op jit(solution)/shard_map/ppermute | solution.py:456
  5.7 1.1 %taps.1.table = bf16[2,192,2048]{2,1,0:T(8,128)(2,1)S(1)} custom-call(s32[1]{0:T(128)} %bitcast.3.tile, f32[6,1,31]{2,1,0:T(1,128)S(1)} %get-tuple-element.28.coef, bf16[21,31]{1,0:T(8,128)(2,1)S(1)} %get-tuple-element.29.cols_t, bf16[21,31]{1,0:T(8,128)(2,1)S(1)} %get-tuple-element.30.rows_t), custom_call_target="tpu_custom_call" | custom-call | flops 10000000 | bytes 2000000 | tf_op jit(solution)/shard_map/taps/pallas_call | solution.py:469
  6.8 1.6 %collective-permute-start.2 = (bf16[128,1024]{1,0:T(8,128)(2,1)S(1)}, bf16[128,1024]{1,0:T(8,128)(2,1)S(1)}, u32[]{:S(2)}, u32[]{:S(2)}) collective-permute-start(bf16[128,1024]{1,0:T(8,128)(2,1)S(1)} %get-tuple-element.33.good.own), channel_id=1, source_target_pairs={{0,2},{1,3},{2,0},{3,1},{4,6},{5,7},{6,4},{7,5},{8,10},{9,11},{10,... | collective-permute-start | bytes 786440 | tf_op jit(solution)/shard_map/ppermute | solution.py:480
  9.1 0.0 collective-permute-done.before
  9.1 0.0 collective-permute-done.1.after
  9.1 0.0 copy-done.3
  9.2 0.0 copy-start.4
  9.2 0.0 copy-start.5
  9.2 0.0 copy-start.6
  9.2 0.0 copy-start
  9.2 0.0 copy-start.2
  9.2 2.9 %matching.1 = (bf16[128,1024]{1,0:T(8,128)(2,1)S(1)}, bf16[16,1024]{1,0:T(8,128)(2,1)S(1)}, bf16[16,1024]{1,0:T(8,128)(2,1)S(1)}) custom-call(s32[1]{0:T(128)} %bitcast.3.tile, f32[1]{0:T(128)S(6)} %copy.15.visit_weight, f32[8,128]{1,0:T(8,128)S(1)} %get-tuple-element.24.level, bf16[32,1024]{1,0:T(8,128)(2,1)S(1)} %collective-permute-done.before, ...), custom_call_target="tpu_custom_call" | custom-call | flops 1610612736 | bytes 3000000 | tf_op jit(solution)/shard_map/matching/pallas_call | solution.py:481
  12.2 1.5 %collective-permute-start.3 = (bf16[128,1024]{1,0:T(8,128)(2,1)S(1)}, bf16[128,1024]{1,0:T(8,128)(2,1)S(1)}, u32[]{:S(2)}, u32[]{:S(2)}) collective-permute-start(bf16[128,1024]{1,0:T(8,128)(2,1)S(1)} %get-tuple-element.32.flux), channel_id=1, source_target_pairs={{0,2},{1,3},{2,0},{3,1},{4,6},{5,7},{6,4},{7,5},{8,10},{9,11},{10,... | collective-permute-start | bytes 786440 | tf_op jit(solution)/shard_map/ppermute | solution.py:491
  13.7 1.4 %collective-permute-start.4 = (bf16[16,1024]{1,0:T(8,128)(2,1)S(1)}, bf16[16,1024]{1,0:T(8,128)(2,1)S(1)}, u32[]{:S(2)}, u32[]{:S(2)}) collective-permute-start(bf16[16,1024]{1,0:T(8,128)(2,1)S(1)} %get-tuple-element.36), channel_id=1, source_target_pairs={{0,3},{1,0},{2,1},{3,2},{4,7},{5,4},{6,5},{7,6},{8,11},{9,8},{10,9... | collective-permute-start | bytes 98312 | tf_op jit(solution)/shard_map/ppermute | solution.py:492
  15.0 0.1 collective-permute-start.5
  15.1 0.0 copy-done.4
  15.2 0.6 copy-done.7
  15.8 2.2 %slots.1 = (s32[64]{0:T(128)S(1)}, s32[64]{0:T(128)S(1)}, bf16[64,8,128]{2,1,0:T(8,128)(2,1)S(1)}) custom-call(s32[1]{0:T(128)} %bitcast.home, s32[64]{0:T(128)S(1)} %bitcast.10, s32[64]{0:T(128)S(1)} %copy-done.5, s32[64]{0:T(128)S(1)} %bitcast.11, s32[64]{0:T(128)S(1)} %copy-done.7), custom_call_target="tpu_custom_call" | custom-call | flops 2000000 | bytes 1000000 | tf_op jit(solution)/shard_map/slots/pallas_call | solution.py:458
  18.0 0.0 collective-permute-done.2.far
  18.0 0.7 warp_weight.1
  18.7 0.0 collective-permute-done.4.after
  18.7 1.4 %collective-permute-done.5.before = bf16[16,1024]{1,0:T(8,128)(2,1)S(1)} collective-permute-done((bf16[16,1024]{1,0:T(8,128)(2,1)S(1)}, bf16[16,1024]{1,0:T(8,128)(2,1)S(1)}, u32[]{:S(2)}, u32[]{:S(2)}) %collective-permute-start.5) | collective-permute-done | bytes 32800 | tf_op jit(solution)/shard_map/ppermute | solution.py:493
  20.1 0.0 collective-permute-done.3.far
  20.1 1.2 %warp_flux.1 = bf16[64,72,128]{2,1,0:T(8,128)(2,1)S(1)} custom-call(s32[64]{0:T(128)S(1)} %get-tuple-element.23.dest_slot_in, f32[128,1024]{1,0:T(8,128)S(1)} %get-tuple-element.34.share, bf16[128,160]{1,0:T(8,128)(2,1)S(1)} %get-tuple-element.35.turn, bf16[128,1024]{1,0:T(8,128)(2,1)S(1)} %collective-permute-done.3.far, ...), custom_call_target="tpu_custom_call" | custom-call | flops 268435456 | bytes 5000000 | tf_op jit(solution)/shard_map/warp_flux/pallas_call | solution.py:506
  21.3 45.3 %all_to_all.10.arriving = bf16[64,72,128]{2,1,0:T(8,128)(2,1)S(1)} all-to-all(bf16[64,72,128]{2,1,0:T(8,128)(2,1)S(1)} %warp_flux.1), channel_id=1, replica_groups=mesh['ccd'=64,'tile'=4] {'ccd'}, dimensions={0} | all-to-all | bytes 2359296 | tf_op jit(solution)/shard_map/all_to_all | solution.py:526
  66.5 1.7 %patch.1 = (f32[128,1024]{1,0:T(8,128)S(1)}, bf16[128,16,128]{2,1,0:T(8,128)(2,1)S(1)}) custom-call(bf16[64,72,128]{2,1,0:T(8,128)(2,1)S(1)} %all_to_all.10.arriving), custom_call_target="tpu_custom_call" | custom-call | flops 1000000 | bytes 2000000 | tf_op jit(solution)/shard_map/patch/pallas_call | solution.py:527
  68.3 24.2 %all_to_all.11.returned = bf16[128,16,128]{2,1,0:T(8,128)(2,1)S(1)} all-to-all(bf16[128,16,128]{2,1,0:T(8,128)(2,1)S(1)} %get-tuple-element.40), channel_id=1, replica_groups=mesh['ccd'=64,'tile'=4] {'ccd'}, dimensions={0} | all-to-all | bytes 1048576 | tf_op jit(solution)/shard_map/all_to_all | solution.py:543
  92.4 0.0 copy-done.1
  92.4 1.5 %difference.1 = (f32[128,1024]{1,0:T(8,128)}, f32[128,1024]{1,0:T(8,128)}) custom-call(s32[64]{0:T(128)S(1)} %get-tuple-element.22.tmpl_slot, bf16[128,16,128]{2,1,0:T(8,128)(2,1)S(1)} %all_to_all.11.returned, f32[128,1024]{1,0:T(8,128)S(1)} %copy-done.1, f32[128,1024]{1,0:T(8,128)S(1)} %get-tuple-element.41.values), custom_call_target="tpu_custom_call" | custom-call | flops 1000000 | bytes 3000000 | tf_op jit(solution)/shard_map/difference/pallas_call | solution.py:544
  (6 shorter events, 0.0 us)
Async XLA Ops:
  0.6 8.5 %copy-start.3 = (bf16[128,1024]{1,0:T(8,128)(2,1)S(1)}, bf16[128,1024]{1,0:T(8,128)(2,1)}, u32[]{:S(2)}) copy-start(bf16[128,1024]{1,0:T(8,128)(2,1)} %image.3) | copy-start | bytes 786436
  2.0 7.1 %collective-permute-start = (bf16[32,1024]{1,0:T(8,128)(2,1)S(1)}, bf16[32,1024]{1,0:T(8,128)(2,1)S(1)}, u32[]{:S(2)}, u32[]{:S(2)}) collective-permute-start(bf16[32,1024]{1,0:T(8,128)(2,1)S(1)} %get-tuple-element.25), channel_id=1, source_target_pairs={{0,1},{1,2},{2,3},{3,0},{4,5},{5,6},{6,7},{7,4},{8,9},{9,10},{10,1... | collective-permute-start | bytes 196616 | tf_op jit(solution)/shard_map/ppermute | solution.py:455
  4.2 4.9 %collective-permute-start.1 = (bf16[32,1024]{1,0:T(8,128)(2,1)S(1)}, bf16[32,1024]{1,0:T(8,128)(2,1)S(1)}, u32[]{:S(2)}, u32[]{:S(2)}) collective-permute-start(bf16[32,1024]{1,0:T(8,128)(2,1)S(1)} %get-tuple-element.26), channel_id=1, source_target_pairs={{0,3},{1,0},{2,1},{3,2},{4,7},{5,4},{6,5},{7,6},{8,11},{9,8},{10,9... | collective-permute-start | bytes 196616 | tf_op jit(solution)/shard_map/ppermute | solution.py:456
  6.8 11.1 %collective-permute-start.2 = (bf16[128,1024]{1,0:T(8,128)(2,1)S(1)}, bf16[128,1024]{1,0:T(8,128)(2,1)S(1)}, u32[]{:S(2)}, u32[]{:S(2)}) collective-permute-start(bf16[128,1024]{1,0:T(8,128)(2,1)S(1)} %get-tuple-element.33.good.own), channel_id=1, source_target_pairs={{0,2},{1,3},{2,0},{3,1},{4,6},{5,7},{6,4},{7,5},{8,10},{9,11},{10,... | collective-permute-start | bytes 786440 | tf_op jit(solution)/shard_map/ppermute | solution.py:480
  9.2 6.0 %copy-start.4 = (s32[64,1]{0,1:T(1,128)S(1)}, s32[64,1]{0,1:T(1,128)}, u32[]{:S(2)}) copy-start(s32[64,1]{0,1:T(1,128)} %param.21) | copy-start | bytes 772
  9.2 6.0 %copy-start.5 = (s32[64]{0:T(128)S(1)}, s32[64]{0:T(128)}, u32[]{:S(2)}) copy-start(s32[64]{0:T(128)} %dest_block.1) | copy-start | bytes 772
  9.2 6.0 %copy-start.6 = (s32[64,1]{0,1:T(1,128)S(1)}, s32[64,1]{0,1:T(1,128)}, u32[]{:S(2)}) copy-start(s32[64,1]{0,1:T(1,128)} %param.24) | copy-start | bytes 772
  9.2 8.8 %copy-start = (bf16[1,1024,1024]{2,1,0:T(8,128)(2,1)S(1)}, bf16[1,1024,1024]{2,1,0:T(8,128)(2,1)}, u32[]{:S(2)}) copy-start(bf16[1,1024,1024]{2,1,0:T(8,128)(2,1)} %param.20) | copy-start | bytes 6291460
  9.2 8.8 %copy-start.2 = (bf16[128,512]{1,0:T(8,128)(2,1)S(1)}, bf16[128,512]{1,0:T(8,128)(2,1)}, u32[]{:S(2)}) copy-start(bf16[128,512]{1,0:T(8,128)(2,1)} %row_warp.3) | copy-start | bytes 393220
  12.2 7.9 %collective-permute-start.3 = (bf16[128,1024]{1,0:T(8,128)(2,1)S(1)}, bf16[128,1024]{1,0:T(8,128)(2,1)S(1)}, u32[]{:S(2)}, u32[]{:S(2)}) collective-permute-start(bf16[128,1024]{1,0:T(8,128)(2,1)S(1)} %get-tuple-element.32.flux), channel_id=1, source_target_pairs={{0,2},{1,3},{2,0},{3,1},{4,6},{5,7},{6,4},{7,5},{8,10},{9,11},{10,... | collective-permute-start | bytes 786440 | tf_op jit(solution)/shard_map/ppermute | solution.py:491
  13.7 5.0 %collective-permute-start.4 = (bf16[16,1024]{1,0:T(8,128)(2,1)S(1)}, bf16[16,1024]{1,0:T(8,128)(2,1)S(1)}, u32[]{:S(2)}, u32[]{:S(2)}) collective-permute-start(bf16[16,1024]{1,0:T(8,128)(2,1)S(1)} %get-tuple-element.36), channel_id=1, source_target_pairs={{0,3},{1,0},{2,1},{3,2},{4,7},{5,4},{6,5},{7,6},{8,11},{9,8},{10,9... | collective-permute-start | bytes 98312 | tf_op jit(solution)/shard_map/ppermute | solution.py:492
  15.0 5.0 %collective-permute-start.5 = (bf16[16,1024]{1,0:T(8,128)(2,1)S(1)}, bf16[16,1024]{1,0:T(8,128)(2,1)S(1)}, u32[]{:S(2)}, u32[]{:S(2)}) collective-permute-start(bf16[16,1024]{1,0:T(8,128)(2,1)S(1)} %get-tuple-element.37), channel_id=1, source_target_pairs={{0,1},{1,2},{2,3},{3,0},{4,5},{5,6},{6,7},{7,4},{8,9},{9,10},{10,1... | collective-permute-start | bytes 98312 | tf_op jit(solution)/shard_map/ppermute | solution.py:493
  15.1 0.7 copy-start.7
  66.5 25.9 %copy-start.1 = (f32[128,1024]{1,0:T(8,128)S(1)}, f32[128,1024]{1,0:T(8,128)}, u32[]{:S(2)}) copy-start(f32[128,1024]{1,0:T(8,128)} %new_science.1) | copy-start | bytes 1572868

commit v7 on v6

--- a/solution.py
+++ b/solution.py
@@ -349,7 +349,7 @@
                 ]
 
 
-def patch_kernel(arriving, values, reply, sums, served, note, table, sem):
+def patch_kernel(arriving, values, reply, sums, more, served, note, table, sem):
     notes = arriving[0, 64:, :].astype(jnp.float32)
     for sender in range(1, 64):
         notes = notes + arriving[sender, 64:, :].astype(jnp.float32)
@@ -357,27 +357,31 @@
     copy = pltpu.make_async_copy(note, table, sem)
     copy.start()
     sums[...] = jnp.zeros_like(sums)
+    more[...] = jnp.zeros_like(more)
     copy.wait()
 
     def add(sender, _):
         for rank in range(2):
             at = table[0, 2 * sender + rank]
-            sums[at] = sums[at] + arriving[sender, rank * 32 : rank * 32 + 32, :].astype(jnp.float32)
+            total = (sums, more)[rank]
+            total[at] = total[at] + arriving[sender, rank * 32 : rank * 32 + 32, :].astype(jnp.float32)
         return 0
 
     lax.fori_loop(0, 64, add, 0, unroll=4)
     for block in range(NBLK):
         down, c = block // 8, block % 8
-        value = sums[block, :16, :] / jnp.maximum(sums[block, 16:, :], FLOOR)
+        total = sums[block] + more[block]
+        value = total[:16, :] / jnp.maximum(total[16:, :], FLOOR)
         values[down * 16 : down * 16 + 16, c * 128 : c * 128 + 128] = value
         served[block] = value.astype(jnp.bfloat16)
 
-    def serve(sender, _):
-        for rank in range(2):
-            reply[2 * sender + rank] = served[table[1, 2 * sender + rank]]
+    def serve(group, _):
+        asked = [served[table[1, 8 * group + i]] for i in range(8)]
+        for i in range(8):
+            reply[8 * group + i] = asked[i]
         return 0
 
-    lax.fori_loop(0, 64, serve, 0, unroll=4)
+    lax.fori_loop(0, 16, serve, 0)
 
 
 def difference_kernel(tmpl_slot, returned, new_science, values, coadd, difference, held, sems):
@@ -531,6 +535,7 @@
         (VMEM, VMEM),
         [
             pltpu.VMEM((NBLK + 8, 32, 128), f32),
+            pltpu.VMEM((NBLK + 8, 32, 128), f32),
             pltpu.VMEM((NBLK, 16, 128), bf16),
             pltpu.VMEM((NOTE, 128), i32),
             pltpu.SMEM((NOTE, 128), i32),

time: 94.2 us -> 94.2 us (level)
  no operation moved by 1% of the time
where the time goes in v7:
time: 94.2 us; the launch traced here: 94 us
  blocking collectives  69.4 us (74%)
  Pallas kernels  12.7 us (13%)
  starting transfers between devices  8.35 us (9%)
  between operations  1.46 us (2%)
  waiting for transfers between devices  1.4 us (1%)
    all_to_all x1, blocking collectives, per_device(): lax.all_to_all(outgoing, 'ccd', split_axis=0, concat_axis=0, tiled=True)  45.3 us
    all_to_all x1, blocking collectives, per_device(): lax.all_to_all(reply, 'ccd', split_axis=0, concat_axis=0, tiled=True)  24.1 us
    pallas_call x1, Pallas kernels, per_device(): call(conv_kernel, (struct((ROWS, WIDTH), bf16),) + (struct((EDGE, WIDTH),...  2.95 us
    ppermute x1, starting transfers between devices, per_device(): before = lax.ppermute(to_next, 'tile', up)  2.2 us
    pallas_call x1, Pallas kernels, per_device(): call(index_kernel, (struct((64,), i32), struct((64,), i32), struct((64, N...  2.15 us
  transfers between devices with their start and end apart: 6, of which 1 were waited for; matrix products, arithmetic and copies ran while one was open for 0% of the time, Pallas kernels for 7%

profile of v7, /device:TPU:1, one launch (start us, length us, event | category | flops | bytes accessed | tf_op | source)
XLA Modules:
  0.0 94.0 jit_solution(158265135299348041)
XLA Ops:
  0.6 0.0 copy-start.3
  0.6 1.4 %edges.1 = (bf16[32,1024]{1,0:T(8,128)(2,1)S(1)}, bf16[32,1024]{1,0:T(8,128)(2,1)S(1)}, bf16[128,1024]{1,0:T(8,128)(2,1)S(1)}, f32[6,1,31]{2,1,0:T(1,128)S(1)}, ...) custom-call(s32[1]{0:T(128)} %bitcast.3.tile, bf16[128,1024]{1,0:T(8,128)(2,1)} %image.3, ...), custom_call_target="tpu_custom_call" | custom-call | flops 400000 | bytes 1000000 | tf_op jit(solution)/shard_map/edges/pallas_call | solution.py:429
  2.0 2.2 %collective-permute-start = (bf16[32,1024]{1,0:T(8,128)(2,1)S(1)}, bf16[32,1024]{1,0:T(8,128)(2,1)S(1)}, u32[]{:S(2)}, u32[]{:S(2)}) collective-permute-start(bf16[32,1024]{1,0:T(8,128)(2,1)S(1)} %get-tuple-element.25), channel_id=1, source_target_pairs={{0,1},{1,2},{2,3},{3,0},{4,5},{5,6},{6,7},{7,4},{8,9},{9,10},{10,1... | collective-permute-start | bytes 196616 | tf_op jit(solution)/shard_map/ppermute | solution.py:459
  4.2 1.5 %collective-permute-start.1 = (bf16[32,1024]{1,0:T(8,128)(2,1)S(1)}, bf16[32,1024]{1,0:T(8,128)(2,1)S(1)}, u32[]{:S(2)}, u32[]{:S(2)}) collective-permute-start(bf16[32,1024]{1,0:T(8,128)(2,1)S(1)} %get-tuple-element.26), channel_id=1, source_target_pairs={{0,3},{1,0},{2,1},{3,2},{4,7},{5,4},{6,5},{7,6},{8,11},{9,8},{10,9... | collective-permute-start | bytes 196616 | tf_op jit(solution)/shard_map/ppermute | solution.py:460
  5.7 1.1 %taps.1.table = bf16[2,192,2048]{2,1,0:T(8,128)(2,1)S(1)} custom-call(s32[1]{0:T(128)} %bitcast.3.tile, f32[6,1,31]{2,1,0:T(1,128)S(1)} %get-tuple-element.28.coef, bf16[21,31]{1,0:T(8,128)(2,1)S(1)} %get-tuple-element.29.cols_t, bf16[21,31]{1,0:T(8,128)(2,1)S(1)} %get-tuple-element.30.rows_t), custom_call_target="tpu_custom_call" | custom-call | flops 10000000 | bytes 2000000 | tf_op jit(solution)/shard_map/taps/pallas_call | solution.py:473
  6.8 1.6 %collective-permute-start.2 = (bf16[128,1024]{1,0:T(8,128)(2,1)S(1)}, bf16[128,1024]{1,0:T(8,128)(2,1)S(1)}, u32[]{:S(2)}, u32[]{:S(2)}) collective-permute-start(bf16[128,1024]{1,0:T(8,128)(2,1)S(1)} %get-tuple-element.33.good.own), channel_id=1, source_target_pairs={{0,2},{1,3},{2,0},{3,1},{4,6},{5,7},{6,4},{7,5},{8,10},{9,11},{10,... | collective-permute-start | bytes 786440 | tf_op jit(solution)/shard_map/ppermute | solution.py:484
  9.1 0.0 collective-permute-done.before
  9.1 0.0 collective-permute-done.1.after
  9.2 0.0 copy-start.4
  9.2 0.0 copy-start.5
  9.2 0.0 copy-start.6
  9.2 0.0 copy-start
  9.2 0.0 copy-start.2
  9.2 2.9 %matching.1 = (bf16[128,1024]{1,0:T(8,128)(2,1)S(1)}, bf16[16,1024]{1,0:T(8,128)(2,1)S(1)}, bf16[16,1024]{1,0:T(8,128)(2,1)S(1)}) custom-call(s32[1]{0:T(128)} %bitcast.3.tile, f32[1]{0:T(128)S(6)} %copy.15.visit_weight, f32[8,128]{1,0:T(8,128)S(1)} %get-tuple-element.24.level, bf16[32,1024]{1,0:T(8,128)(2,1)S(1)} %collective-permute-done.before, ...), custom_call_target="tpu_custom_call" | custom-call | flops 1610612736 | bytes 3000000 | tf_op jit(solution)/shard_map/matching/pallas_call | solution.py:485
  12.2 1.5 %collective-permute-start.3 = (bf16[128,1024]{1,0:T(8,128)(2,1)S(1)}, bf16[128,1024]{1,0:T(8,128)(2,1)S(1)}, u32[]{:S(2)}, u32[]{:S(2)}) collective-permute-start(bf16[128,1024]{1,0:T(8,128)(2,1)S(1)} %get-tuple-element.32.flux), channel_id=1, source_target_pairs={{0,2},{1,3},{2,0},{3,1},{4,6},{5,7},{6,4},{7,5},{8,10},{9,11},{10,... | collective-permute-start | bytes 786440 | tf_op jit(solution)/shard_map/ppermute | solution.py:495
  13.7 1.4 %collective-permute-start.4 = (bf16[16,1024]{1,0:T(8,128)(2,1)S(1)}, bf16[16,1024]{1,0:T(8,128)(2,1)S(1)}, u32[]{:S(2)}, u32[]{:S(2)}) collective-permute-start(bf16[16,1024]{1,0:T(8,128)(2,1)S(1)} %get-tuple-element.36), channel_id=1, source_target_pairs={{0,3},{1,0},{2,1},{3,2},{4,7},{5,4},{6,5},{7,6},{8,11},{9,8},{10,9... | collective-permute-start | bytes 98312 | tf_op jit(solution)/shard_map/ppermute | solution.py:496
  15.0 0.1 collective-permute-start.5
  15.1 0.0 copy-done.5
  15.2 0.6 copy-done.7
  15.8 2.2 %slots.1 = (s32[64]{0:T(128)S(1)}, s32[64]{0:T(128)S(1)}, bf16[64,8,128]{2,1,0:T(8,128)(2,1)S(1)}) custom-call(s32[1]{0:T(128)} %bitcast.home, s32[64]{0:T(128)S(1)} %bitcast.10, s32[64]{0:T(128)S(1)} %copy-done.5, s32[64]{0:T(128)S(1)} %bitcast.11, s32[64]{0:T(128)S(1)} %copy-done.7), custom_call_target="tpu_custom_call" | custom-call | flops 2000000 | bytes 1000000 | tf_op jit(solution)/shard_map/slots/pallas_call | solution.py:462
  18.0 0.0 collective-permute-done.2.far
  18.0 0.0 copy-done
  18.0 0.0 copy-done.2
  18.0 0.7 warp_weight.1
  18.7 0.0 collective-permute-done.4.after
  18.7 1.4 %collective-permute-done.5.before = bf16[16,1024]{1,0:T(8,128)(2,1)S(1)} collective-permute-done((bf16[16,1024]{1,0:T(8,128)(2,1)S(1)}, bf16[16,1024]{1,0:T(8,128)(2,1)S(1)}, u32[]{:S(2)}, u32[]{:S(2)}) %collective-permute-start.5) | collective-permute-done | bytes 32800 | tf_op jit(solution)/shard_map/ppermute | solution.py:497
  20.1 0.0 collective-permute-done.3.far
  20.1 1.2 %warp_flux.1 = bf16[64,72,128]{2,1,0:T(8,128)(2,1)S(1)} custom-call(s32[64]{0:T(128)S(1)} %get-tuple-element.23.dest_slot_in, f32[128,1024]{1,0:T(8,128)S(1)} %get-tuple-element.34.share, bf16[128,160]{1,0:T(8,128)(2,1)S(1)} %get-tuple-element.35.turn, bf16[128,1024]{1,0:T(8,128)(2,1)S(1)} %collective-permute-done.3.far, ...), custom_call_target="tpu_custom_call" | custom-call | flops 268435456 | bytes 5000000 | tf_op jit(solution)/shard_map/warp_flux/pallas_call | solution.py:510
  21.3 45.3 %all_to_all.10.arriving = bf16[64,72,128]{2,1,0:T(8,128)(2,1)S(1)} all-to-all(bf16[64,72,128]{2,1,0:T(8,128)(2,1)S(1)} %warp_flux.1), channel_id=1, replica_groups=mesh['ccd'=64,'tile'=4] {'ccd'}, dimensions={0} | all-to-all | bytes 2359296 | tf_op jit(solution)/shard_map/all_to_all | solution.py:530
  66.5 1.8 %patch.1 = (f32[128,1024]{1,0:T(8,128)S(1)}, bf16[128,16,128]{2,1,0:T(8,128)(2,1)S(1)}) custom-call(bf16[64,72,128]{2,1,0:T(8,128)(2,1)S(1)} %all_to_all.10.arriving), custom_call_target="tpu_custom_call" | custom-call | flops 1000000 | bytes 2000000 | tf_op jit(solution)/shard_map/patch/pallas_call | solution.py:531
  68.3 24.1 %all_to_all.11.returned = bf16[128,16,128]{2,1,0:T(8,128)(2,1)S(1)} all-to-all(bf16[128,16,128]{2,1,0:T(8,128)(2,1)S(1)} %get-tuple-element.40), channel_id=1, replica_groups=mesh['ccd'=64,'tile'=4] {'ccd'}, dimensions={0} | all-to-all | bytes 1048576 | tf_op jit(solution)/shard_map/all_to_all | solution.py:548
  92.4 1.5 %difference.1 = (f32[128,1024]{1,0:T(8,128)}, f32[128,1024]{1,0:T(8,128)}) custom-call(s32[64]{0:T(128)S(1)} %get-tuple-element.22.tmpl_slot, bf16[128,16,128]{2,1,0:T(8,128)(2,1)S(1)} %all_to_all.11.returned, f32[128,1024]{1,0:T(8,128)S(1)} %copy-done.1, f32[128,1024]{1,0:T(8,128)S(1)} %get-tuple-element.41.values), custom_call_target="tpu_custom_call" | custom-call | flops 1000000 | bytes 3000000 | tf_op jit(solution)/shard_map/difference/pallas_call | solution.py:549
  (6 shorter events, 0.0 us)
Async XLA Ops:
  0.6 8.5 %copy-start.3 = (bf16[128,1024]{1,0:T(8,128)(2,1)S(1)}, bf16[128,1024]{1,0:T(8,128)(2,1)}, u32[]{:S(2)}) copy-start(bf16[128,1024]{1,0:T(8,128)(2,1)} %image.3) | copy-start | bytes 786436
  2.0 7.1 %collective-permute-start = (bf16[32,1024]{1,0:T(8,128)(2,1)S(1)}, bf16[32,1024]{1,0:T(8,128)(2,1)S(1)}, u32[]{:S(2)}, u32[]{:S(2)}) collective-permute-start(bf16[32,1024]{1,0:T(8,128)(2,1)S(1)} %get-tuple-element.25), channel_id=1, source_target_pairs={{0,1},{1,2},{2,3},{3,0},{4,5},{5,6},{6,7},{7,4},{8,9},{9,10},{10,1... | collective-permute-start | bytes 196616 | tf_op jit(solution)/shard_map/ppermute | solution.py:459
  4.2 4.9 %collective-permute-start.1 = (bf16[32,1024]{1,0:T(8,128)(2,1)S(1)}, bf16[32,1024]{1,0:T(8,128)(2,1)S(1)}, u32[]{:S(2)}, u32[]{:S(2)}) collective-permute-start(bf16[32,1024]{1,0:T(8,128)(2,1)S(1)} %get-tuple-element.26), channel_id=1, source_target_pairs={{0,3},{1,0},{2,1},{3,2},{4,7},{5,4},{6,5},{7,6},{8,11},{9,8},{10,9... | collective-permute-start | bytes 196616 | tf_op jit(solution)/shard_map/ppermute | solution.py:460
  6.8 11.1 %collective-permute-start.2 = (bf16[128,1024]{1,0:T(8,128)(2,1)S(1)}, bf16[128,1024]{1,0:T(8,128)(2,1)S(1)}, u32[]{:S(2)}, u32[]{:S(2)}) collective-permute-start(bf16[128,1024]{1,0:T(8,128)(2,1)S(1)} %get-tuple-element.33.good.own), channel_id=1, source_target_pairs={{0,2},{1,3},{2,0},{3,1},{4,6},{5,7},{6,4},{7,5},{8,10},{9,11},{10,... | collective-permute-start | bytes 786440 | tf_op jit(solution)/shard_map/ppermute | solution.py:484
  9.2 6.0 %copy-start.4 = (s32[64,1]{0,1:T(1,128)S(1)}, s32[64,1]{0,1:T(1,128)}, u32[]{:S(2)}) copy-start(s32[64,1]{0,1:T(1,128)} %param.21) | copy-start | bytes 772
  9.2 6.0 %copy-start.5 = (s32[64]{0:T(128)S(1)}, s32[64]{0:T(128)}, u32[]{:S(2)}) copy-start(s32[64]{0:T(128)} %dest_block.1) | copy-start | bytes 772
  9.2 6.0 %copy-start.6 = (s32[64,1]{0,1:T(1,128)S(1)}, s32[64,1]{0,1:T(1,128)}, u32[]{:S(2)}) copy-start(s32[64,1]{0,1:T(1,128)} %param.24) | copy-start | bytes 772
  9.2 8.8 %copy-start = (bf16[1,1024,1024]{2,1,0:T(8,128)(2,1)S(1)}, bf16[1,1024,1024]{2,1,0:T(8,128)(2,1)}, u32[]{:S(2)}) copy-start(bf16[1,1024,1024]{2,1,0:T(8,128)(2,1)} %param.20) | copy-start | bytes 6291460
  9.2 8.8 %copy-start.2 = (bf16[128,512]{1,0:T(8,128)(2,1)S(1)}, bf16[128,512]{1,0:T(8,128)(2,1)}, u32[]{:S(2)}) copy-start(bf16[128,512]{1,0:T(8,128)(2,1)} %row_warp.3) | copy-start | bytes 393220
  12.2 7.9 %collective-permute-start.3 = (bf16[128,1024]{1,0:T(8,128)(2,1)S(1)}, bf16[128,1024]{1,0:T(8,128)(2,1)S(1)}, u32[]{:S(2)}, u32[]{:S(2)}) collective-permute-start(bf16[128,1024]{1,0:T(8,128)(2,1)S(1)} %get-tuple-element.32.flux), channel_id=1, source_target_pairs={{0,2},{1,3},{2,0},{3,1},{4,6},{5,7},{6,4},{7,5},{8,10},{9,11},{10,... | collective-permute-start | bytes 786440 | tf_op jit(solution)/shard_map/ppermute | solution.py:495
  13.7 5.0 %collective-permute-start.4 = (bf16[16,1024]{1,0:T(8,128)(2,1)S(1)}, bf16[16,1024]{1,0:T(8,128)(2,1)S(1)}, u32[]{:S(2)}, u32[]{:S(2)}) collective-permute-start(bf16[16,1024]{1,0:T(8,128)(2,1)S(1)} %get-tuple-element.36), channel_id=1, source_target_pairs={{0,3},{1,0},{2,1},{3,2},{4,7},{5,4},{6,5},{7,6},{8,11},{9,8},{10,9... | collective-permute-start | bytes 98312 | tf_op jit(solution)/shard_map/ppermute | solution.py:496
  15.0 5.0 %collective-permute-start.5 = (bf16[16,1024]{1,0:T(8,128)(2,1)S(1)}, bf16[16,1024]{1,0:T(8,128)(2,1)S(1)}, u32[]{:S(2)}, u32[]{:S(2)}) collective-permute-start(bf16[16,1024]{1,0:T(8,128)(2,1)S(1)} %get-tuple-element.37), channel_id=1, source_target_pairs={{0,1},{1,2},{2,3},{3,0},{4,5},{5,6},{6,7},{7,4},{8,9},{9,10},{10,1... | collective-permute-start | bytes 98312 | tf_op jit(solution)/shard_map/ppermute | solution.py:497
  15.1 0.7 copy-start.7
  66.5 25.9 %copy-start.1 = (f32[128,1024]{1,0:T(8,128)S(1)}, f32[128,1024]{1,0:T(8,128)}, u32[]{:S(2)}) copy-start(f32[128,1024]{1,0:T(8,128)} %new_science.1) | copy-start | bytes 1572868

commit v8 on v7

--- a/solution.py
+++ b/solution.py
@@ -37,7 +37,7 @@
     return pltpu.with_memory_space_constraint(array, pltpu.HBM)
 
 
-def call(body, out_shape, in_specs, out_specs, scratch, name, flops, nbytes):
+def call(body, out_shape, in_specs, out_specs, scratch, name, flops, nbytes, aliases={}):
     return pl.pallas_call(
         body,
         out_shape=out_shape,
@@ -45,6 +45,7 @@
         out_specs=out_specs,
         scratch_shapes=scratch,
         name=name,
+        input_output_aliases=aliases,
         compiler_params=pltpu.CompilerParams(vmem_limit_bytes=20 * 1024 * 1024),
         cost_estimate=pl.CostEstimate(flops=flops, bytes_accessed=nbytes, transcendentals=0),
     )
@@ -282,9 +283,19 @@
         )
 
 
+def place_blocks(n, part, dest_slot, plane, outgoing):
+    for down in range(8):
+        for c in range(2):
+            slot = dest_slot[down * 8 + 2 * n + c]
+            owner, at = slot // 2, pl.multiple_of(lax.rem(slot, 2) * 32 + plane * 16, 16)
+            block = part[down * 16 : down * 16 + 16, c * 128 : c * 128 + 128]
+            outgoing[owner, pl.ds(at, 16), :] = block
+
+
 def warp_weight_kernel(
     tile,
     visit_weight,
+    dest_slot,
     level,
     flux,
     own,
@@ -293,7 +304,8 @@
     before,
     row_warp,
     col_warp,
-    warped,
+    notes,
+    outgoing,
     share,
     turn,
     rest,
@@ -309,7 +321,8 @@
     scale = visit_weight[0].astype(jnp.bfloat16).astype(jnp.float32)
     rowed[...] = (scale * both).astype(jnp.bfloat16)
     for n, part in warp_columns(rowed, col_warp):
-        warped[:, 256 * n : 256 * n + 256] = part
+        place_blocks(n, part, dest_slot, 1, outgoing)
+    outgoing[:, 64:, :] = notes[...]
 
 
 def warp_flux_kernel(
@@ -320,8 +333,7 @@
     after,
     before,
     col_warp,
-    warped_weight,
-    notes,
+    begun,
     outgoing,
     rest,
     rowed,
@@ -334,19 +346,9 @@
     rowed[...] = (
         share[...] + jnp.dot(turn[...], rest[...], preferred_element_type=jnp.float32)
     ).astype(jnp.bfloat16)
-    outgoing[:, 64:, :] = notes[...]
     copy.wait()
     for n, part in warp_columns(rowed, col_warp):
-        for down in range(8):
-            for c in range(2):
-                column = 2 * n + c
-                slot = dest_slot[down * 8 + column]
-                owner, at = slot // 2, pl.multiple_of(lax.rem(slot, 2) * 32, 32)
-                rows = slice(down * 16, down * 16 + 16)
-                outgoing[owner, pl.ds(at, 16), :] = part[rows, c * 128 : c * 128 + 128]
-                outgoing[owner, pl.ds(at + 16, 16), :] = warped_weight[
-                    rows, column * 128 : column * 128 + 128
-                ]
+        place_blocks(n, part, dest_slot, 0, outgoing)
 
 
 def patch_kernel(arriving, values, reply, sums, more, served, note, table, sem):
@@ -497,25 +499,39 @@
     before_flux = lax.ppermute(flux_to_next, "tile", up)
     reach = ROWS + 2 * EDGE
     scratch = [pltpu.VMEM((reach, WIDTH), bf16), pltpu.VMEM((ROWS, WIDTH), bf16)]
-    warped_weight, share, turn = call(
+    begun, share, turn = call(
         warp_weight_kernel,
-        (struct((ROWS, WIDTH), bf16), struct((ROWS, WIDTH), f32), struct((ROWS, reach), bf16)),
-        [SMEM] * 2 + [VMEM] * 8,
+        (struct((64, MESSAGE, 128), bf16), struct((ROWS, WIDTH), f32), struct((ROWS, reach), bf16)),
+        [SMEM] * 3 + [VMEM] * 9,
         (VMEM,) * 3,
         scratch,
         "warp_weight",
         2 * 128 * WIDTH * WIDTH,
         4_000_000,
-    )(tile, visit_weight, level, flux, good, far_good, after, before, row_warp, col_warp[0])
+    )(
+        tile,
+        visit_weight,
+        dest_slot,
+        level,
+        flux,
+        good,
+        far_good,
+        after,
+        before,
+        row_warp,
+        col_warp[0],
+        notes,
+    )
     outgoing = call(
         warp_flux_kernel,
         struct((64, MESSAGE, 128), bf16),
-        [VMEM] * 9,
+        [VMEM] * 8,
         VMEM,
         scratch + [pltpu.SMEM((64,), i32), pltpu.SemaphoreType.DMA],
         "warp_flux",
         2 * 128 * WIDTH * WIDTH,
         5_000_000,
+        {7: 0},
     )(
         dest_slot,
         share,
@@ -524,8 +540,7 @@
         after_flux,
         before_flux,
         col_warp[0],
-        warped_weight,
-        notes,
+        begun,
     )
     arriving = lax.all_to_all(outgoing, "ccd", split_axis=0, concat_axis=0, tiled=True)
     values, reply = call(

time: 94.2 us -> 94 us (level)
  transfers between devices with their start and end apart: 6 -> 6, of which waited for: 1 -> 1; matrix products, arithmetic and copies ran while one was open for 0% -> 0% of each run, Pallas kernels for 7% -> 8%
where the time goes in v8:
time: 94 us; the launch traced here: 93.8 us
  blocking collectives  69.4 us (74%)
  Pallas kernels  13.2 us (14%)
  starting transfers between devices  8.34 us (9%)
  between operations  1.46 us (2%)
    all_to_all x1, blocking collectives, per_device(): lax.all_to_all(outgoing, 'ccd', split_axis=0, concat_axis=0, tiled=True)  45.3 us
    all_to_all x1, blocking collectives, per_device(): lax.all_to_all(reply, 'ccd', split_axis=0, concat_axis=0, tiled=True)  24.1 us
    pallas_call x1, Pallas kernels, per_device(): call(conv_kernel, (struct((ROWS, WIDTH), bf16),) + (struct((EDGE, WIDTH),...  2.95 us
    ppermute x1, starting transfers between devices, per_device(): before = lax.ppermute(to_next, 'tile', up)  2.2 us
    pallas_call x1, Pallas kernels, per_device(): call(index_kernel, (struct((64,), i32), struct((64,), i32), struct((64, N...  2.15 us
  transfers between devices with their start and end apart: 6, of which 1 were waited for; matrix products, arithmetic and copies ran while one was open for 0% of the time, Pallas kernels for 8%

profile of v8, /device:TPU:1, one launch (start us, length us, event | category | flops | bytes accessed | tf_op | source)
XLA Modules:
  0.0 93.8 jit_solution(6665358164159275995)
XLA Ops:
  0.6 0.0 copy-start.3
  0.6 1.4 %edges.1 = (bf16[32,1024]{1,0:T(8,128)(2,1)S(1)}, bf16[32,1024]{1,0:T(8,128)(2,1)S(1)}, bf16[128,1024]{1,0:T(8,128)(2,1)S(1)}, f32[6,1,31]{2,1,0:T(1,128)S(1)}, ...) custom-call(s32[1]{0:T(128)} %bitcast.3.tile, bf16[128,1024]{1,0:T(8,128)(2,1)} %image.3, ...), custom_call_target="tpu_custom_call" | custom-call | flops 400000 | bytes 1000000 | tf_op jit(solution)/shard_map/edges/pallas_call | solution.py:431
  2.0 2.2 %collective-permute-start = (bf16[32,1024]{1,0:T(8,128)(2,1)S(1)}, bf16[32,1024]{1,0:T(8,128)(2,1)S(1)}, u32[]{:S(2)}, u32[]{:S(2)}) collective-permute-start(bf16[32,1024]{1,0:T(8,128)(2,1)S(1)} %get-tuple-element.25), channel_id=1, source_target_pairs={{0,1},{1,2},{2,3},{3,0},{4,5},{5,6},{6,7},{7,4},{8,9},{9,10},{10,1... | collective-permute-start | bytes 196616 | tf_op jit(solution)/shard_map/ppermute | solution.py:461
  4.2 1.5 %collective-permute-start.1 = (bf16[32,1024]{1,0:T(8,128)(2,1)S(1)}, bf16[32,1024]{1,0:T(8,128)(2,1)S(1)}, u32[]{:S(2)}, u32[]{:S(2)}) collective-permute-start(bf16[32,1024]{1,0:T(8,128)(2,1)S(1)} %get-tuple-element.26), channel_id=1, source_target_pairs={{0,3},{1,0},{2,1},{3,2},{4,7},{5,4},{6,5},{7,6},{8,11},{9,8},{10,9... | collective-permute-start | bytes 196616 | tf_op jit(solution)/shard_map/ppermute | solution.py:462
  5.7 1.1 %taps.1.table = bf16[2,192,2048]{2,1,0:T(8,128)(2,1)S(1)} custom-call(s32[1]{0:T(128)} %bitcast.3.tile, f32[6,1,31]{2,1,0:T(1,128)S(1)} %get-tuple-element.28.coef, bf16[21,31]{1,0:T(8,128)(2,1)S(1)} %get-tuple-element.29.cols_t, bf16[21,31]{1,0:T(8,128)(2,1)S(1)} %get-tuple-element.30.rows_t), custom_call_target="tpu_custom_call" | custom-call | flops 10000000 | bytes 2000000 | tf_op jit(solution)/shard_map/taps/pallas_call | solution.py:475
  6.8 1.6 %collective-permute-start.2 = (bf16[128,1024]{1,0:T(8,128)(2,1)S(1)}, bf16[128,1024]{1,0:T(8,128)(2,1)S(1)}, u32[]{:S(2)}, u32[]{:S(2)}) collective-permute-start(bf16[128,1024]{1,0:T(8,128)(2,1)S(1)} %get-tuple-element.33.good.own), channel_id=1, source_target_pairs={{0,2},{1,3},{2,0},{3,1},{4,6},{5,7},{6,4},{7,5},{8,10},{9,11},{10,... | collective-permute-start | bytes 786440 | tf_op jit(solution)/shard_map/ppermute | solution.py:486
  9.1 0.0 collective-permute-done.before
  9.1 0.0 collective-permute-done.1.after
  9.1 0.0 copy-done.3
  9.2 0.0 copy-start.4
  9.2 0.0 copy-start.5
  9.2 0.0 copy-start.6
  9.2 0.0 copy-start
  9.2 0.0 copy-start.2
  9.2 3.0 %matching.1 = (bf16[128,1024]{1,0:T(8,128)(2,1)S(1)}, bf16[16,1024]{1,0:T(8,128)(2,1)S(1)}, bf16[16,1024]{1,0:T(8,128)(2,1)S(1)}) custom-call(s32[1]{0:T(128)} %bitcast.3.tile, f32[1]{0:T(128)S(6)} %copy.17.visit_weight, f32[8,128]{1,0:T(8,128)S(1)} %get-tuple-element.24.level, bf16[32,1024]{1,0:T(8,128)(2,1)S(1)} %collective-permute-done.before, ...), custom_call_target="tpu_custom_call" | custom-call | flops 1610612736 | bytes 3000000 | tf_op jit(solution)/shard_map/matching/pallas_call | solution.py:487
  12.2 1.5 %collective-permute-start.3 = (bf16[128,1024]{1,0:T(8,128)(2,1)S(1)}, bf16[128,1024]{1,0:T(8,128)(2,1)S(1)}, u32[]{:S(2)}, u32[]{:S(2)}) collective-permute-start(bf16[128,1024]{1,0:T(8,128)(2,1)S(1)} %get-tuple-element.32.flux), channel_id=1, source_target_pairs={{0,2},{1,3},{2,0},{3,1},{4,6},{5,7},{6,4},{7,5},{8,10},{9,11},{10,... | collective-permute-start | bytes 786440 | tf_op jit(solution)/shard_map/ppermute | solution.py:497
  13.7 1.4 %collective-permute-start.4 = (bf16[16,1024]{1,0:T(8,128)(2,1)S(1)}, bf16[16,1024]{1,0:T(8,128)(2,1)S(1)}, u32[]{:S(2)}, u32[]{:S(2)}) collective-permute-start(bf16[16,1024]{1,0:T(8,128)(2,1)S(1)} %get-tuple-element.37), channel_id=1, source_target_pairs={{0,3},{1,0},{2,1},{3,2},{4,7},{5,4},{6,5},{7,6},{8,11},{9,8},{10,9... | collective-permute-start | bytes 98312 | tf_op jit(solution)/shard_map/ppermute | solution.py:498
  15.1 0.1 collective-permute-start.5
  15.1 0.0 copy-done.4
  15.2 0.6 copy-done.7
  15.8 2.2 %slots.1 = (s32[64]{0:T(128)S(1)}, s32[64]{0:T(128)S(1)}, bf16[64,8,128]{2,1,0:T(8,128)(2,1)S(1)}) custom-call(s32[1]{0:T(128)} %bitcast.home, s32[64]{0:T(128)S(1)} %bitcast.10, s32[64]{0:T(128)S(1)} %copy-done.5, s32[64]{0:T(128)S(1)} %bitcast.11, s32[64]{0:T(128)S(1)} %copy-done.7), custom_call_target="tpu_custom_call" | custom-call | flops 2000000 | bytes 1000000 | tf_op jit(solution)/shard_map/slots/pallas_call | solution.py:464
  18.0 0.0 collective-permute-done.2.far
  18.0 1.4 %warp_weight.1 = (bf16[64,72,128]{2,1,0:T(8,128)(2,1)S(1)}, f32[128,1024]{1,0:T(8,128)S(1)}, bf16[128,160]{1,0:T(8,128)(2,1)S(1)}) custom-call(s32[1]{0:T(128)} %bitcast.3.tile, f32[1]{0:T(128)S(6)} %copy.17.visit_weight, s32[64]{0:T(128)S(1)} %get-tuple-element.23.dest_slot.dest_slot_in, f32[8,128]{1,0:T(8,128)S(1)} %get-tuple-element.24.level, ...), custom_call_target="tpu_custom_call" | custom-call | flops 268435456 | bytes 4000000 | tf_op jit(solution)/shard_map/warp_weight/pallas_call | solution.py:502
  19.4 0.0 collective-permute-done.4.after
  19.4 0.7 collective-permute-done.5.before
  20.1 0.0 collective-permute-done.3.far
  20.1 1.0 %warp_flux.1 = bf16[64,72,128]{2,1,0:T(8,128)(2,1)S(1)} custom-call(s32[64]{0:T(128)S(1)} %get-tuple-element.23.dest_slot.dest_slot_in, f32[128,1024]{1,0:T(8,128)S(1)} %get-tuple-element.35.share, bf16[128,160]{1,0:T(8,128)(2,1)S(1)} %get-tuple-element.36.turn, bf16[128,1024]{1,0:T(8,128)(2,1)S(1)} %collective-permute-done.3.far, ...), custom_call_target="tpu_custom_call", output_to_operand_aliasing={{}: (7, {})} | custom-call | flops 268435456 | bytes 5000000 | tf_op jit(solution)/shard_map/warp_flux/pallas_call | solution.py:525
  21.1 45.3 %all_to_all.10.arriving = bf16[64,72,128]{2,1,0:T(8,128)(2,1)S(1)} all-to-all(bf16[64,72,128]{2,1,0:T(8,128)(2,1)S(1)} %warp_flux.1), channel_id=1, replica_groups=mesh['ccd'=64,'tile'=4] {'ccd'}, dimensions={0} | all-to-all | bytes 2359296 | tf_op jit(solution)/shard_map/all_to_all | solution.py:545
  66.4 1.8 %patch.1 = (f32[128,1024]{1,0:T(8,128)S(1)}, bf16[128,16,128]{2,1,0:T(8,128)(2,1)S(1)}) custom-call(bf16[64,72,128]{2,1,0:T(8,128)(2,1)S(1)} %all_to_all.10.arriving), custom_call_target="tpu_custom_call" | custom-call | flops 1000000 | bytes 2000000 | tf_op jit(solution)/shard_map/patch/pallas_call | solution.py:546
  68.1 24.1 %all_to_all.11.returned = bf16[128,16,128]{2,1,0:T(8,128)(2,1)S(1)} all-to-all(bf16[128,16,128]{2,1,0:T(8,128)(2,1)S(1)} %get-tuple-element.40), channel_id=1, replica_groups=mesh['ccd'=64,'tile'=4] {'ccd'}, dimensions={0} | all-to-all | bytes 1048576 | tf_op jit(solution)/shard_map/all_to_all | solution.py:563
  92.3 0.0 copy-done.1
  92.3 1.5 %difference.1 = (f32[128,1024]{1,0:T(8,128)}, f32[128,1024]{1,0:T(8,128)}) custom-call(s32[64]{0:T(128)S(1)} %get-tuple-element.22.tmpl_slot, bf16[128,16,128]{2,1,0:T(8,128)(2,1)S(1)} %all_to_all.11.returned, f32[128,1024]{1,0:T(8,128)S(1)} %copy-done.1, f32[128,1024]{1,0:T(8,128)S(1)} %get-tuple-element.41.values), custom_call_target="tpu_custom_call" | custom-call | flops 1000000 | bytes 3000000 | tf_op jit(solution)/shard_map/difference/pallas_call | solution.py:564
  (6 shorter events, 0.0 us)
Async XLA Ops:
  0.6 8.5 %copy-start.3 = (bf16[128,1024]{1,0:T(8,128)(2,1)S(1)}, bf16[128,1024]{1,0:T(8,128)(2,1)}, u32[]{:S(2)}) copy-start(bf16[128,1024]{1,0:T(8,128)(2,1)} %image.3) | copy-start | bytes 786436
  2.0 7.1 %collective-permute-start = (bf16[32,1024]{1,0:T(8,128)(2,1)S(1)}, bf16[32,1024]{1,0:T(8,128)(2,1)S(1)}, u32[]{:S(2)}, u32[]{:S(2)}) collective-permute-start(bf16[32,1024]{1,0:T(8,128)(2,1)S(1)} %get-tuple-element.25), channel_id=1, source_target_pairs={{0,1},{1,2},{2,3},{3,0},{4,5},{5,6},{6,7},{7,4},{8,9},{9,10},{10,1... | collective-permute-start | bytes 196616 | tf_op jit(solution)/shard_map/ppermute | solution.py:461
  4.2 4.9 %collective-permute-start.1 = (bf16[32,1024]{1,0:T(8,128)(2,1)S(1)}, bf16[32,1024]{1,0:T(8,128)(2,1)S(1)}, u32[]{:S(2)}, u32[]{:S(2)}) collective-permute-start(bf16[32,1024]{1,0:T(8,128)(2,1)S(1)} %get-tuple-element.26), channel_id=1, source_target_pairs={{0,3},{1,0},{2,1},{3,2},{4,7},{5,4},{6,5},{7,6},{8,11},{9,8},{10,9... | collective-permute-start | bytes 196616 | tf_op jit(solution)/shard_map/ppermute | solution.py:462
  6.8 11.1 %collective-permute-start.2 = (bf16[128,1024]{1,0:T(8,128)(2,1)S(1)}, bf16[128,1024]{1,0:T(8,128)(2,1)S(1)}, u32[]{:S(2)}, u32[]{:S(2)}) collective-permute-start(bf16[128,1024]{1,0:T(8,128)(2,1)S(1)} %get-tuple-element.33.good.own), channel_id=1, source_target_pairs={{0,2},{1,3},{2,0},{3,1},{4,6},{5,7},{6,4},{7,5},{8,10},{9,11},{10,... | collective-permute-start | bytes 786440 | tf_op jit(solution)/shard_map/ppermute | solution.py:486
  9.2 6.0 %copy-start.4 = (s32[64,1]{0,1:T(1,128)S(1)}, s32[64,1]{0,1:T(1,128)}, u32[]{:S(2)}) copy-start(s32[64,1]{0,1:T(1,128)} %param.21) | copy-start | bytes 772
  9.2 6.0 %copy-start.5 = (s32[64]{0:T(128)S(1)}, s32[64]{0:T(128)}, u32[]{:S(2)}) copy-start(s32[64]{0:T(128)} %dest_block.1) | copy-start | bytes 772
  9.2 6.0 %copy-start.6 = (s32[64,1]{0,1:T(1,128)S(1)}, s32[64,1]{0,1:T(1,128)}, u32[]{:S(2)}) copy-start(s32[64,1]{0,1:T(1,128)} %param.24) | copy-start | bytes 772
  9.2 8.8 %copy-start = (bf16[1,1024,1024]{2,1,0:T(8,128)(2,1)S(1)}, bf16[1,1024,1024]{2,1,0:T(8,128)(2,1)}, u32[]{:S(2)}) copy-start(bf16[1,1024,1024]{2,1,0:T(8,128)(2,1)} %param.20) | copy-start | bytes 6291460
  9.2 8.8 %copy-start.2 = (bf16[128,512]{1,0:T(8,128)(2,1)S(1)}, bf16[128,512]{1,0:T(8,128)(2,1)}, u32[]{:S(2)}) copy-start(bf16[128,512]{1,0:T(8,128)(2,1)} %row_warp.3) | copy-start | bytes 393220
  12.2 7.9 %collective-permute-start.3 = (bf16[128,1024]{1,0:T(8,128)(2,1)S(1)}, bf16[128,1024]{1,0:T(8,128)(2,1)S(1)}, u32[]{:S(2)}, u32[]{:S(2)}) collective-permute-start(bf16[128,1024]{1,0:T(8,128)(2,1)S(1)} %get-tuple-element.32.flux), channel_id=1, source_target_pairs={{0,2},{1,3},{2,0},{3,1},{4,6},{5,7},{6,4},{7,5},{8,10},{9,11},{10,... | collective-permute-start | bytes 786440 | tf_op jit(solution)/shard_map/ppermute | solution.py:497
  13.7 5.7 %collective-permute-start.4 = (bf16[16,1024]{1,0:T(8,128)(2,1)S(1)}, bf16[16,1024]{1,0:T(8,128)(2,1)S(1)}, u32[]{:S(2)}, u32[]{:S(2)}) collective-permute-start(bf16[16,1024]{1,0:T(8,128)(2,1)S(1)} %get-tuple-element.37), channel_id=1, source_target_pairs={{0,3},{1,0},{2,1},{3,2},{4,7},{5,4},{6,5},{7,6},{8,11},{9,8},{10,9... | collective-permute-start | bytes 98312 | tf_op jit(solution)/shard_map/ppermute | solution.py:498
  15.1 5.0 %collective-permute-start.5 = (bf16[16,1024]{1,0:T(8,128)(2,1)S(1)}, bf16[16,1024]{1,0:T(8,128)(2,1)S(1)}, u32[]{:S(2)}, u32[]{:S(2)}) collective-permute-start(bf16[16,1024]{1,0:T(8,128)(2,1)S(1)} %get-tuple-element.38), channel_id=1, source_target_pairs={{0,1},{1,2},{2,3},{3,0},{4,5},{5,6},{6,7},{7,4},{8,9},{9,10},{10,1... | collective-permute-start | bytes 98312 | tf_op jit(solution)/shard_map/ppermute | solution.py:499
  15.2 0.7 copy-start.7
  66.4 25.9 %copy-start.1 = (f32[128,1024]{1,0:T(8,128)S(1)}, f32[128,1024]{1,0:T(8,128)}, u32[]{:S(2)}) copy-start(f32[128,1024]{1,0:T(8,128)} %new_science.1) | copy-start | bytes 1572868
